TPU v7x, 32 devices: a whole 2x2x4 slice. The times are simulated.
32 devices in a mesh: groups: 2 (over x), dp: 8 (over z, y), owner: 2 (over core).
Axes of the slice: x: 2, y: 2, z: 4, core: 2. Of those that a mesh axis runs over, the one named last changes fastest.
Arguments:
- embeddings: float32 [32768, 1024], P(('groups', 'dp', 'owner')), parts along dimension 0, may hold values from -14 to 14
- cluster_ids: int32 [32768], P(('groups', 'dp', 'owner')), parts along dimension 0, may hold values from 0 to 63, as said below
Outputs:
- nearest: float32 [32768], P(('groups', 'dp', 'owner')), parts along dimension 0
There are 2 independent parts, one for each index of `groups`. A program takes and returns all parts, laid end to end along the dimension named above; each array names one. Nothing has to cross between parts.
Inputs may be any that keep to these rules, and one draw needn't show every extreme that they name: `cluster_ids`: cluster c belongs to index c // 8 of dp. The examples of one device include at most 256 of the clusters of any one index of dp; in every draw one index of dp has exactly 256 from every device. Some clusters may have a single member.
All inputs are finite; a program needn't handle non-finite values.
Results may differ from a plain program's by a relative error of at most 0.00032.
Values may be sent and summed in bfloat16 or wider, within the bound.
No kernel may reach another device: no remote copies, remote signals or barrier semaphores. Data moves between devices by JAX's collectives and lax.ppermute only.
A program may use at most 64 MiB of HBM per device.

v0:
```python
import math

import jax
import jax.numpy as jnp
from jax import lax
from jax.sharding import PartitionSpec as P

CL_DEV = 8


def local(embeddings, cluster_ids):
    count = embeddings.shape[0]
    width = embeddings.shape[1]
    peers = lax.axis_size("dp")
    paired = lax.axis_size("owner")
    slots = 2 * count // peers
    squares = jnp.sum(embeddings * embeddings, axis=1, keepdims=True)
    unit = (embeddings * lax.rsqrt(squares + 1e-06)).astype(jnp.bfloat16)
    target = cluster_ids // CL_DEV
    onehot = (target[:, None] == jnp.arange(peers, dtype=jnp.int32)[None, :]).astype(jnp.int32)
    ranking = jnp.cumsum(onehot, axis=0) - 1
    position = jnp.sum(ranking * onehot, axis=1)
    where_to = target * slots + position
    send_rows = jnp.zeros((peers * slots, width), jnp.bfloat16).at[where_to].set(unit)
    send_ids = jnp.full((peers * slots,), -1, jnp.int32).at[where_to].set(cluster_ids)
    both_rows = jnp.broadcast_to(
        send_rows.reshape(peers, 1, slots, width), (peers, paired, slots, width)
    )
    both_ids = jnp.broadcast_to(send_ids.reshape(peers, 1, slots), (peers, paired, slots))
    got_rows, got_ids = (
        lax.all_to_all(
            both_rows.reshape(peers * paired * slots, width),
            ("dp", "owner"),
            split_axis=0,
            concat_axis=0,
            tiled=True,
        ),
        lax.all_to_all(
            both_ids.reshape(peers * paired * slots),
            ("dp", "owner"),
            split_axis=0,
            concat_axis=0,
            tiled=True,
        ),
    )
    mine = lax.axis_index("owner")
    rolled_rows = jnp.roll(got_rows.reshape(peers, paired, slots, width), -mine, axis=1)
    rolled_ids = jnp.roll(got_ids.reshape(peers, paired, slots), -mine, axis=1)
    own_rows = rolled_rows[:, 0].reshape(peers * slots, width)
    own_ids = rolled_ids[:, 0].reshape(peers * slots)
    rest_rows = jnp.transpose(rolled_rows[:, 1:], (1, 0, 2, 3)).reshape(-1, width)
    rest_ids = jnp.transpose(rolled_ids[:, 1:], (1, 0, 2)).reshape(-1)
    columns = jnp.concatenate([own_rows, rest_rows], axis=0)
    column_ids = jnp.concatenate([own_ids, rest_ids], axis=0)
    total = peers * slots
    block = math.gcd(total, 512)
    column_pos = jnp.arange(columns.shape[0], dtype=jnp.int32)

    def block_best(start):
        queries = lax.dynamic_slice_in_dim(own_rows, start, block, 0)
        query_ids = lax.dynamic_slice_in_dim(own_ids, start, block, 0)
        scores = lax.dot_general(
            queries, columns, (((1,), (1,)), ((), ())), preferred_element_type=jnp.float32
        )
        row_pos = start + jnp.arange(block, dtype=jnp.int32)
        same = (query_ids[:, None] == column_ids[None, :]) & (column_ids[None, :] >= 0)
        same = same & (row_pos[:, None] != column_pos[None, :])
        return jnp.max(jnp.where(same, scores, jnp.float32(-1.0)), axis=1)

    starts = jnp.arange(total // block, dtype=jnp.int32) * block
    best = lax.map(block_best, starts).reshape(peers, slots)
    returned = lax.all_to_all(best, "dp", split_axis=0, concat_axis=0, tiled=True)
    return returned.reshape(-1)[where_to]


def solution(mesh):
    return jax.shard_map(
        local,
        mesh=mesh,
        in_specs=(P(("groups", "dp", "owner"), None), P(("groups", "dp", "owner"))),
        out_specs=P(("groups", "dp", "owner")),
        check_vma=False,
    )
```

profile of v0, /device:TPU:0, one launch (start us, length us, event | category | flops | bytes accessed | tf_op | source)
XLA Modules:
  0.0 313.1 jit_solution(15476565237646127374)
XLA Ops:
  0.0 0.7 add_select_fusion
  0.7 2.3 reduce-window.6
  3.0 0.3 slice_reduce_fusion
  3.3 0.2 reduce-window.9
  3.5 0.7 broadcast_clamp_fusion
  4.2 4.5 %scatter_custom_fusion = s32[2048]{0:T(1024)S(1)} fusion(s32[1024]{0:T(1024)S(1)} %get-tuple-element.79, s32[1024]{0:T(1024)} %param.5, s32[]{:T(128)} %constant.80.clone.1), kind=kCustom, calls=%fused_computation.40 | custom fusion | bytes 8704 | tf_op jit(solution)/shard_map/scatter | solution.py:25
  8.7 0.6 all_to_all.18
  9.4 7.4 %all-to-all-start = ((s32[16,256,1]{1,2,0:T(1,128)}), s32[16,256,1]{1,2,0:T(1,128)S(1)}, u32[]{:S(2)}, u32[]{:S(2)}) async-start(s32[16,256,1]{1,2,0:T(1,128)} %all_to_all.18), calls=%async_computation | async-start | bytes 32768 | tf_op jit(solution)/shard_map/all_to_all | solution.py:38
  16.8 2.5 multiply_reduce_fusion
  19.3 9.3 %scatter_custom_fusion.1 = bf16[2048,1024]{1,0:T(8,128)(2,1)} fusion(s32[1024]{0:T(1024)S(1)} %get-tuple-element.79, f32[1024,1024]{1,0:T(8,128)} %param.4, f32[1024]{0:T(1024)S(1)} %add_rsqrt_fusion, bf16[]{:T(256)} %constant.76.clone.1), kind=kCustom, calls=%fused_computation.17 | custom fusion | flops 2097152 | bytes 8392706 | tf_op jit(solution)/shard_map/scatter | solution.py:24
  28.6 6.7 %broadcast_in_dim.51 = bf16[8,2,256,1024]{3,2,1,0:T(8,128)(2,1)} broadcast(bf16[8,256,1024]{2,1,0:T(8,128)(2,1)} %bitcast.36), dimensions={0,2,3} | broadcast | bytes 12582912 | tf_op jit(solution)/shard_map/broadcast_in_dim | solution.py:26
  35.2 6.1 %all-to-all-start.1 = ((bf16[16,256,1024]{2,1,0:T(8,128)(2,1)}), bf16[16,256,1024]{2,1,0:T(8,128)(2,1)}, u32[]{:S(2)}, u32[]{:S(2)}) async-start(bf16[16,256,1024]{2,1,0:T(8,128)(2,1)} %bitcast.35), calls=%async_computation.1 | async-start | bytes 16777216 | tf_op jit(solution)/shard_map/all_to_all | solution.py:31
  41.5 150.5 %all-to-all-done.1 = bf16[16,256,1024]{2,1,0:T(8,128)(2,1)} async-done(((bf16[16,256,1024]{2,1,0:T(8,128)(2,1)}), bf16[16,256,1024]{2,1,0:T(8,128)(2,1)}, u32[]{:S(2)}, u32[]{:S(2)}) %all-to-all-start.1) | async-done | bytes 8388640 | tf_op jit(solution)/shard_map/all_to_all | solution.py:31
  192.0 5.6 %fusion.5 = bf16[8,2,256,1024]{3,2,1,0:T(8,128)(2,1)S(1)} fusion(s32[]{:T(128)S(6)} %select_n.40, bf16[8,2,256,1024]{3,2,1,0:T(8,128)(2,1)} %bitcast.6), kind=kLoop, calls=%fused_computation.13 | loop fusion | flops 4194304 | bytes 16777220 | tf_op jit(solution)/shard_map/jit(_roll_dynamic)/concatenate | solution.py:47
  197.7 3.7 %fusion.18 = (bf16[8,1,256,1024]{3,2,1,0:T(8,128)(2,1)}, bf16[8,1,256,1024]{3,2,1,0:T(8,128)(2,1)}) fusion(bf16[8,2,256,1024]{3,2,1,0:T(8,128)(2,1)S(1)} %fusion.5), kind=kLoop, calls=%fused_computation.46 | loop fusion | bytes 16777216 | tf_op jit(solution)/shard_map/slice | solution.py:51
  201.4 7.7 %pad_maximum_fusion = bf16[4096,1024]{1,0:T(8,128)(2,1)} fusion(bf16[2048,1024]{1,0:T(8,128)(2,1)} %bitcast.39, bf16[2048,1024]{1,0:T(8,128)(2,1)} %bitcast.37), kind=kLoop, calls=%fused_computation.14 | loop fusion | flops 16777216 | bytes 16777216 | tf_op jit(solution)/shard_map/concatenate | solution.py:53
  209.0 50.8 %while.11 = (s32[]{:T(128)}, f32[4,512]{1,0:T(4,128)S(1)}, s32[4]{0:T(128)S(1)}, s32[2048]{0:T(1024)S(1)}, s32[4096]{0:T(1024)S(1)}, /*index=5*/bf16[2048,1024]{...) while((s32[]{:T(128)}, f32[4,512]{1,0:T(4,128)S(1)}, ...), condition=%wide.region_8.9_spmd.clone, body=%wide.region_6.8_spmd.clone.sunk | while | flops 4307554304 | bytes 9494691 | solution.py:71
  209.0 0.6 dynamic_slice.45
  211.5 0.6 iota_add_fusion.2
  212.2 9.5 %select_reduce_fusion.2 = f32[512]{0:T(512)S(1)} fusion(bf16[4096,1024]{1,0:T(8,128)(2,1)} %get-tuple-element.155, s32[512]{0:T(512)S(1)} %iota_add_fusion.2, s32[4096]{0:T(1024)S(1)} %get-tuple-element.153, s32[512]{0:T(512)S(1)} %dynamic_slice.46, pred[4096]{0:T(1024)(128)(4,1)S(1)} %broadcast_compare_fusion.2, ...), kind=kOutput, calls=%fused_computation.5.clone.1 | convolution fusion | flops 4307549696 | bytes 9463812 | tf_op jit(solution)/shard_map/while/body/eval_jaxpr/dot_general | solution.py:62
  221.7 0.6 dynamic_slice.45
  224.1 0.1 dynamic_slice.46
  224.2 0.6 iota_add_fusion.2
  224.9 9.5 %select_reduce_fusion.2 = f32[512]{0:T(512)S(1)} fusion(bf16[4096,1024]{1,0:T(8,128)(2,1)} %get-tuple-element.155, s32[512]{0:T(512)S(1)} %iota_add_fusion.2, s32[4096]{0:T(1024)S(1)} %get-tuple-element.153, s32[512]{0:T(512)S(1)} %dynamic_slice.46, pred[4096]{0:T(1024)(128)(4,1)S(1)} %broadcast_compare_fusion.2, ...), kind=kOutput, calls=%fused_computation.5.clone.1 | convolution fusion | flops 4307549696 | bytes 9463812 | tf_op jit(solution)/shard_map/while/body/eval_jaxpr/dot_general | solution.py:62
  234.4 0.6 dynamic_slice.45
  236.9 0.6 iota_add_fusion.2
  237.6 9.5 %select_reduce_fusion.2 = f32[512]{0:T(512)S(1)} fusion(bf16[4096,1024]{1,0:T(8,128)(2,1)} %get-tuple-element.155, s32[512]{0:T(512)S(1)} %iota_add_fusion.2, s32[4096]{0:T(1024)S(1)} %get-tuple-element.153, s32[512]{0:T(512)S(1)} %dynamic_slice.46, pred[4096]{0:T(1024)(128)(4,1)S(1)} %broadcast_compare_fusion.2, ...), kind=kOutput, calls=%fused_computation.5.clone.1 | convolution fusion | flops 4307549696 | bytes 9463812 | tf_op jit(solution)/shard_map/while/body/eval_jaxpr/dot_general | solution.py:62
  247.1 0.6 dynamic_slice.45
  249.6 0.6 iota_add_fusion.2
  250.3 9.5 %select_reduce_fusion.2 = f32[512]{0:T(512)S(1)} fusion(bf16[4096,1024]{1,0:T(8,128)(2,1)} %get-tuple-element.155, s32[512]{0:T(512)S(1)} %iota_add_fusion.2, s32[4096]{0:T(1024)S(1)} %get-tuple-element.153, s32[512]{0:T(512)S(1)} %dynamic_slice.46, pred[4096]{0:T(1024)(128)(4,1)S(1)} %broadcast_compare_fusion.2, ...), kind=kOutput, calls=%fused_computation.5.clone.1 | convolution fusion | flops 4307549696 | bytes 9463812 | tf_op jit(solution)/shard_map/while/body/eval_jaxpr/dot_general | solution.py:62
  259.8 42.7 %all_to_all.27 = f32[8,1,256]{2,1,0:T(1,128)S(1)} all-to-all(f32[8,1,256]{2,1,0:T(1,128)S(1)} %all_to_all.22), channel_id=1, replica_groups=mesh['groups'=2,'dp'=8,'owner'=2] {'dp'}, dimensions={0} | all-to-all | bytes 16384 | tf_op jit(solution)/shard_map/all_to_all | solution.py:72
  302.5 10.5 %gather_fusion = f32[1024]{0:T(1024)} fusion(f32[2048]{0:T(1024)S(1)} %bitcast.34, s32[1024]{0:T(1024)S(1)} %get-tuple-element.78), kind=kCustom, calls=%fused_computation | custom fusion | bytes 12288 | tf_op jit(solution)/shard_map/gather | solution.py:73
  (26 shorter events, 0.7 us)
Async XLA Ops:
  9.4 19.2 %all-to-all-start = ((s32[16,256,1]{1,2,0:T(1,128)}), s32[16,256,1]{1,2,0:T(1,128)S(1)}, u32[]{:S(2)}, u32[]{:S(2)}) async-start(s32[16,256,1]{1,2,0:T(1,128)} %all_to_all.18), calls=%async_computation | async-start | bytes 32768 | tf_op jit(solution)/shard_map/all_to_all | solution.py:38
  35.2 156.8 %all-to-all-start.1 = ((bf16[16,256,1024]{2,1,0:T(8,128)(2,1)}), bf16[16,256,1024]{2,1,0:T(8,128)(2,1)}, u32[]{:S(2)}, u32[]{:S(2)}) async-start(bf16[16,256,1024]{2,1,0:T(8,128)(2,1)} %bitcast.35), calls=%async_computation.1 | async-start | bytes 16777216 | tf_op jit(solution)/shard_map/all_to_all | solution.py:31
where the time goes:
time: 314 us; the launch traced here: 313 us
  waiting for transfers between devices  150 us (48%)
  blocking collectives  42.7 us (14%)
  matrix products  37.9 us (12%)
  other arithmetic  31.6 us (10%)
  local copies, waits for them, and re-layouts  29.3 us (9%)
  starting transfers between devices  13.5 us (4%)
  loops' own time  7.4 us (2%)
    all_to_all x1, waiting for transfers between devices, local(): lax.all_to_all(both_rows.reshape(peers * paired * slots, width), ('dp', '...  150 us
    all_to_all x1, blocking collectives, local(): lax.all_to_all(best, 'dp', split_axis=0, concat_axis=0, tiled=True)  42.7 us
    dot_general x4, matrix products, block_best(): lax.dot_general(queries, columns, (((1,), (1,)), ((), ())), preferred_ele...  37.9 us
    gather x1, local copies, waits for them, and re-layouts, local(): return returned.reshape(-1)[where_to]  10.5 us
    scatter x1, other arithmetic, local(): jnp.zeros((peers * slots, width), jnp.bfloat16).at[where_to].set(unit)  9.27 us
    concatenate x1, other arithmetic, local(): columns = jnp.concatenate([own_rows, rest_rows], axis=0)  7.67 us
    another operation x1, loops' own time, local(): best = lax.map(block_best, starts).reshape(peers, slots)  7.4 us
    all_to_all x1, starting transfers between devices, local(): lax.all_to_all(both_ids.reshape(peers * paired * slots), ('dp', 'owner'),...  7.39 us
  transfers between devices with their start and end apart: 2, of which 1 were waited for; matrix products, arithmetic and copies ran while one was open for 4% of the time, Pallas kernels for 0%

commit v1 on v0

v1 whole, which is shorter than its diff:
```python
import functools
import math

import jax
import jax.numpy as jnp
from jax import lax
from jax.experimental import pallas as pl
from jax.experimental.pallas import tpu as pltpu
from jax.sharding import PartitionSpec as P

CL_DEV = 8
LANES = 128
SUB = 16
VMEM_LIMIT = 48 * 1024 * 1024
ANY = pl.BlockSpec(memory_space=pl.ANY)
VMEM = pl.BlockSpec(memory_space=pltpu.VMEM)
SMEM = pl.BlockSpec(memory_space=pltpu.SMEM)
NT = (((1,), (1,)), ((), ()))


def pad_lanes(row, width):
    extra = width - row.shape[1]
    if extra == 0:
        return row
    return jnp.concatenate([row, jnp.zeros((row.shape[0], extra), row.dtype)], axis=1)


def as_column(row):
    return jnp.transpose(jnp.broadcast_to(row, (8, row.shape[1])))[:, 0:1]


def code_of(leader, bad):
    return 16 + 2 * leader + bad


def lead_kernel(peers, cap, block, me_ref, ids_ref, emb_ref, unit_ref, info_ref, hdr_ref, lead_ref):
    count, width = emb_ref.shape
    ids = ids_ref[...]
    target = jnp.right_shift(ids, int(math.log2(CL_DEV)))
    local_id = jnp.bitwise_and(ids, CL_DEV - 1)
    tio = lax.broadcasted_iota(jnp.int32, (peers, 1), 0)
    onehot = (lax.broadcasted_iota(jnp.int32, (peers, count), 0) == target).astype(jnp.int32)
    lane = lax.broadcasted_iota(jnp.int32, (peers, count), 1)
    cum = onehot
    step = 1
    while step < count:
        cum = cum + jnp.where(lane >= step, pltpu.roll(cum, step, 1), 0)
        step *= 2
    rank = jnp.sum(cum * onehot, axis=0, keepdims=True) - 1
    counts = cum[:, count - 1 : count]
    leader = jnp.min(jnp.where(counts == cap, tio, peers - 1), axis=0, keepdims=True)
    others = jnp.max(jnp.where(tio == leader, cap - counts, counts), axis=0, keepdims=True)
    lead_short = jnp.max(jnp.where(tio == leader, cap - counts, 0), axis=0, keepdims=True)
    bad = ((others > block - 1) | (lead_short != 0)).astype(jnp.int32)
    is_lead = target == leader
    rel = target - me_ref[0]
    rel = jnp.where(rel < 0, rel + peers, rel)
    slots = peers * block
    fits = rank < block - 1
    dest = jnp.where(is_lead, slots + rank, jnp.where(fits, rel * block + rank, -1))
    pitch = -(-block // LANES) * LANES
    final = jnp.where(is_lead, peers * pitch + rank, target * pitch + rank)
    row8 = lax.broadcasted_iota(jnp.int32, (8, count), 0)
    info_ref[...] = jnp.where(row8 == 0, dest, final)

    both = jnp.where(row8 == 0, dest, local_id + 1).astype(jnp.float32)
    both = jnp.transpose(both)
    dest_col, id_col = both[:, 0:1], both[:, 1:2]
    pieces = []
    for start in range(0, slots + cap, LANES):
        at = (lax.broadcasted_iota(jnp.int32, (count, LANES), 1) + start).astype(jnp.float32)
        pieces.append(jnp.sum(jnp.where(dest_col == at, id_col, 0.0), axis=0, keepdims=True))
    ids_at = jnp.concatenate(pieces, axis=1)
    block_ids = ids_at[:, :slots]
    slot_lane = lax.broadcasted_iota(jnp.int32, (1, slots), 1)
    last = functools.reduce(jnp.logical_or, [slot_lane == k * block + block - 1 for k in range(peers)])
    code = code_of(leader, bad).astype(jnp.float32)
    block_ids = jnp.where(last, code, block_ids)
    hdr_ref[...] = jnp.broadcast_to(pad_lanes(block_ids, width), (8, width))

    emb = emb_ref[...]
    squares = jnp.sum(emb * emb, axis=1, keepdims=True)
    unit = (emb * lax.rsqrt(squares + 1e-06)).astype(jnp.bfloat16)
    unit_ref[...] = unit
    at = lax.broadcasted_iota(jnp.int32, (cap, count), 0) + slots
    pick = jnp.where(at == dest, 1.0, 0.0).astype(jnp.bfloat16)
    lead_ref[:cap, :] = jnp.dot(pick, unit, preferred_element_type=jnp.float32).astype(jnp.bfloat16)
    lead_hdr = pad_lanes(ids_at[:, slots:], width)
    lead_ref[cap:, :] = jnp.broadcast_to(lead_hdr, (SUB, width)).astype(jnp.bfloat16)


def pack_kernel(peers, block, unit_ref, info_ref, hdr_ref, *rest):
    outs, pick = rest[:peers], rest[peers]
    count, width = unit_ref.shape
    dest = info_ref[0:1, :]
    at = lax.broadcasted_iota(jnp.int32, (peers * block, count), 0)
    pick[...] = jnp.where(at == dest, 1.0, 0.0).astype(jnp.bfloat16)
    is_hdr = lax.broadcasted_iota(jnp.int32, (block, 1), 0) == block - 1
    tile = 256
    for start in range(0, width, tile):
        cols = slice(start, start + tile)
        acc = jnp.dot(pick[...], unit_ref[:, cols], preferred_element_type=jnp.float32)
        for k in range(peers):
            rows = acc[k * block : (k + 1) * block]
            rows = jnp.where(is_hdr, hdr_ref[0:1, cols], rows)
            outs[k][:, cols] = rows.astype(jnp.bfloat16)


def leader_best_kernel(reach, cap, pos_ref, *rest):
    queries, rest = rest[:4], rest[4:]
    ups, rest = rest[: reach - 1], rest[reach - 1 :]
    downs, rest = rest[: reach - 1], rest[reach - 1 :]
    outs, (q, c, q_hdr, c_hdr, sem) = rest[:4], rest[4:]
    pos = pos_ref[0]

    def copies(src, index, rows, hdrs, which):
        return [
            pltpu.make_async_copy(src.at[pl.ds(0, cap), :], rows.at[pl.ds(index * cap, cap), :], sem.at[which]),
            pltpu.make_async_copy(src.at[pl.ds(cap, SUB), :], hdrs.at[pl.ds(index * SUB, SUB), :], sem.at[which + 1]),
        ]

    started = []
    for j in range(4):
        started += copies(queries[j], j, q, q_hdr, 2 * j)
    started += copies(queries[0], 0, c, c_hdr, 8)
    for copy in started:
        copy.start()
    for k in range(1, reach):
        up = copies(ups[k - 1], k, c, c_hdr, 8 + 2 * k)
        down = copies(downs[reach - k - 1], k, c, c_hdr, 8 + 2 * k)

        @pl.when(pos >= k)
        def _():
            for copy in up:
                copy.start()

        @pl.when(pos < k)
        def _():
            for copy in down:
                copy.start()

        started += up
    for copy in started:
        copy.wait()
    c_ids = [c_hdr[k * SUB : (k + 1) * SUB, :cap].astype(jnp.float32)[0:1] for k in range(reach)]
    c_col = as_column(jnp.concatenate(c_ids, axis=1))
    for j in range(4):
        q_id = q_hdr[j * SUB : (j + 1) * SUB, :cap].astype(jnp.float32)[0:1]
        scores = lax.dot_general(c[...], q[j * cap : (j + 1) * cap, :], NT, preferred_element_type=jnp.float32)
        same = c_col == q_id
        if j == 0:
            r = lax.broadcasted_iota(jnp.int32, (reach * cap, cap), 0)
            l = lax.broadcasted_iota(jnp.int32, (reach * cap, cap), 1)
            same = same & (r != l)
        outs[j][...] = jnp.max(jnp.where(same, scores, -1.0), axis=0, keepdims=True)


def block_best_kernel(peers, block, me_ref, *rest):
    mine, rest = rest[:peers], rest[peers:]
    other, rest = rest[:peers], rest[peers:]
    out, flag, (own, far, sem) = rest[0], rest[1], rest[2:]
    width = own.shape[1]
    slots = peers * block
    started = []
    for k in range(peers):
        started.append(pltpu.make_async_copy(mine[k], own.at[pl.ds(k * block, block), :], sem.at[k]))
        started.append(pltpu.make_async_copy(other[k], far.at[pl.ds(k * block, block), :], sem.at[peers + k]))
    for copy in started:
        copy.start()
    for copy in started:
        copy.wait()
    lane = lax.broadcasted_iota(jnp.int32, (1, width), 1)

    def ids_of(rows):
        total = jnp.zeros((1, width), jnp.float32)
        for k in range(peers):
            tail = rows[(k + 1) * block - SUB : (k + 1) * block, :].astype(jnp.float32)[SUB - 1 : SUB]
            inside = (lane >= k * block) & (lane < (k + 1) * block)
            total = jnp.where(inside, tail, total)
        return total

    own_ids, far_ids = ids_of(own), ids_of(far)
    is_code = functools.reduce(jnp.logical_or, [lane == k * block + block - 1 for k in range(peers)])
    my_code = own_ids[:, block - 1 : block]
    odd = jnp.where(is_code & ((own_ids != my_code) | (far_ids != my_code)), 1.0, 0.0)
    half = jnp.floor(my_code * 0.5)
    odd = jnp.maximum(jnp.max(odd, axis=1, keepdims=True), my_code - 2.0 * half)
    flag[...] = jnp.broadcast_to(odd, flag.shape)

    q_id = own_ids[:, :slots]
    best = None
    for rows, ids in ((own, own_ids), (far, far_ids)):
        scores = lax.dot_general(rows[...], own[...], NT, preferred_element_type=jnp.float32)
        same = as_column(ids)[:slots] == q_id
        if rows is own:
            r = lax.broadcasted_iota(jnp.int32, (slots, slots), 0)
            l = lax.broadcasted_iota(jnp.int32, (slots, slots), 1)
            same = same & (r != l)
        top = jnp.max(jnp.where(same, scores, -1.0), axis=0, keepdims=True)
        best = top if best is None else jnp.maximum(best, top)
    best = jnp.broadcast_to(pad_lanes(best, width), (8, width))
    pitch = out.shape[1]
    for k in range(peers):
        piece = best if k == 0 else pltpu.roll(best, width - k * block, 1)
        to = me_ref[0] - k
        to = jnp.where(to < 0, to + peers, to)
        out[pl.ds(to, 1), :] = piece[0:1, :pitch]


def final_kernel(peers, cap, info_ref, back_ref, *rest):
    leads, out = rest[:-1], rest[-1]
    count = info_ref.shape[1]
    pitch = back_ref.shape[1]
    where = info_ref[1:2, :]
    lead = functools.reduce(jnp.maximum, [ref[...] for ref in leads])
    total = jnp.zeros((1, count), jnp.float32)
    at = lax.broadcasted_iota(jnp.int32, (pitch, count), 0)
    cols = jnp.transpose(jnp.concatenate([back_ref[...]] * (8 // math.gcd(peers, 8)), axis=0))
    for h in range(peers):
        hit = at + h * pitch == where
        total += jnp.sum(jnp.where(hit, cols[:, h : h + 1], 0.0), axis=0, keepdims=True)
    at = lax.broadcasted_iota(jnp.int32, (cap, count), 0) + peers * pitch
    total += jnp.sum(jnp.where(at == where, as_column(lead), 0.0), axis=0, keepdims=True)
    out[...] = total


def call(kernel, name, outs, in_specs, out_specs, scratch=(), flops=0, nbytes=0):
    return pl.pallas_call(
        kernel,
        name=name,
        out_shape=outs,
        in_specs=in_specs,
        out_specs=out_specs,
        scratch_shapes=list(scratch),
        compiler_params=pltpu.CompilerParams(vmem_limit_bytes=VMEM_LIMIT),
        cost_estimate=pl.CostEstimate(flops=flops, bytes_accessed=nbytes, transcendentals=0),
    )


def whole_exchange(embeddings, cluster_ids):
    count, width = embeddings.shape
    peers = lax.axis_size("dp")
    slots = 2 * count // peers
    squares = jnp.sum(embeddings * embeddings, axis=1, keepdims=True)
    unit = (embeddings * lax.rsqrt(squares + 1e-06)).astype(jnp.bfloat16)
    target = cluster_ids // CL_DEV
    onehot = (target[:, None] == jnp.arange(peers, dtype=jnp.int32)[None, :]).astype(jnp.int32)
    ranking = jnp.cumsum(onehot, axis=0) - 1
    position = jnp.sum(ranking * onehot, axis=1)
    where_to = target * slots + position
    total = peers * slots
    send_rows = jnp.zeros((total, width), jnp.bfloat16).at[where_to].set(unit)
    send_ids = jnp.full((total,), -1, jnp.int32).at[where_to].set(cluster_ids)
    own_rows = lax.all_to_all(send_rows, "dp", split_axis=0, concat_axis=0, tiled=True)
    own_ids = lax.all_to_all(send_ids, "dp", split_axis=0, concat_axis=0, tiled=True)
    swap = [(0, 1), (1, 0)]
    far_rows = lax.ppermute(own_rows, "owner", swap)
    far_ids = lax.ppermute(own_ids, "owner", swap)
    block = math.gcd(total, 512)
    column_pos = jnp.arange(total, dtype=jnp.int32)

    def block_best(start):
        queries = lax.dynamic_slice_in_dim(own_rows, start, block, 0)
        query_ids = lax.dynamic_slice_in_dim(own_ids, start, block, 0)
        row_pos = start + jnp.arange(block, dtype=jnp.int32)
        tops = []
        for rows, ids, own in ((own_rows, own_ids, True), (far_rows, far_ids, False)):
            scores = lax.dot_general(queries, rows, NT, preferred_element_type=jnp.float32)
            same = (query_ids[:, None] == ids[None, :]) & (ids[None, :] >= 0)
            if own:
                same = same & (row_pos[:, None] != column_pos[None, :])
            tops.append(jnp.max(jnp.where(same, scores, jnp.float32(-1.0)), axis=1))
        return jnp.maximum(tops[0], tops[1])

    starts = jnp.arange(total // block, dtype=jnp.int32) * block
    best = lax.map(block_best, starts).reshape(peers, slots)
    returned = lax.all_to_all(best, "dp", split_axis=0, concat_axis=0, tiled=True)
    return returned.reshape(-1)[where_to]


def local(embeddings, cluster_ids):
    count, width = embeddings.shape
    peers = lax.axis_size("dp")
    groups = lax.axis_size("groups")
    cap = 2 * count // peers
    mean = -(-(count - cap) // (peers - 1))
    block = -(-(mean + 1) // SUB) * SUB
    slots = peers * block
    pitch = -(-block // LANES) * LANES
    reach = peers // 2
    bf16, f32 = jnp.bfloat16, jnp.float32
    shape = jax.ShapeDtypeStruct
    me = lax.axis_index("dp")
    me1 = me.reshape(1)

    unit, info, hdr, lead = call(
        functools.partial(lead_kernel, peers, cap, block),
        "lead",
        [shape((count, width), bf16), shape((8, count), jnp.int32), shape((8, width), f32), shape((cap + SUB, width), bf16)],
        [SMEM, VMEM, VMEM],
        [VMEM] * 4,
        flops=2 * cap * count * width,
        nbytes=6 * count * width,
    )(me1, cluster_ids.reshape(1, count), embeddings)

    def dp_pairs(step):
        pairs = []
        for z in range(reach):
            for y in range(2):
                to = step(z, y)
                if to is not None:
                    pairs.append((2 * z + y, 2 * to[0] + to[1]))
        return pairs

    other_y = dp_pairs(lambda z, y: (z, 1 - y))
    up_pairs = dp_pairs(lambda z, y: (z + 1, y) if z + 1 < reach else None)
    down_pairs = dp_pairs(lambda z, y: (z - 1, y) if z > 0 else None)
    swap = [(0, 1), (1, 0)]

    ups, downs = [], []
    up, down = lead, lead
    for _ in range(reach - 1):
        up = lax.ppermute(up, "dp", up_pairs)
        down = lax.ppermute(down, "dp", down_pairs)
        ups.append(up)
        downs.append(down)
    blocks = call(
        functools.partial(pack_kernel, peers, block),
        "pack",
        [shape((block, width), bf16)] * peers,
        [VMEM] * 3,
        [VMEM] * peers,
        [pltpu.VMEM((slots, count), bf16)],
        flops=2 * slots * count * width,
        nbytes=4 * count * width,
    )(unit, info, hdr)
    got = [blocks[0]]
    for k in range(1, peers):
        got.append(lax.ppermute(blocks[k], "dp", [(d, (d + k) % peers) for d in range(peers)]))
    far = [lax.ppermute(rows, "owner", swap) for rows in got]

    lead_y = lax.ppermute(lead, "dp", other_y)
    lead_o = lax.ppermute(lead, "owner", swap)
    lead_yo = lax.ppermute(lead_y, "owner", swap)
    tops = call(
        functools.partial(leader_best_kernel, reach, cap),
        "leader_best",
        [shape((1, cap), f32)] * 4,
        [SMEM] + [ANY] * (4 + 2 * (reach - 1)),
        [VMEM] * 4,
        [
            pltpu.VMEM((4 * cap, width), bf16),
            pltpu.VMEM((reach * cap, width), bf16),
            pltpu.VMEM((4 * SUB, width), bf16),
            pltpu.VMEM((reach * SUB, width), bf16),
            pltpu.SemaphoreType.DMA((8 + 2 * reach,)),
        ],
        flops=8 * cap * cap * reach * width,
        nbytes=2 * (4 + reach) * cap * width,
    )((me // 2).reshape(1), lead, lead_y, lead_o, lead_yo, *ups, *downs)
    tops = [
        tops[0],
        lax.ppermute(tops[1], "dp", other_y),
        lax.ppermute(tops[2], "owner", swap),
        lax.ppermute(lax.ppermute(tops[3], "owner", swap), "dp", other_y),
    ]

    best, flag = call(
        functools.partial(block_best_kernel, peers, block),
        "block_best",
        [shape((peers, pitch), f32), shape((8, LANES), f32)],
        [SMEM] + [ANY] * (2 * peers),
        [VMEM] * 2,
        [pltpu.VMEM((slots, width), bf16), pltpu.VMEM((slots, width), bf16), pltpu.SemaphoreType.DMA((2 * peers,))],
        flops=4 * slots * slots * width,
        nbytes=4 * slots * width,
    )(me1, *got, *far)
    back = lax.all_to_all(best, "dp", split_axis=0, concat_axis=0, tiled=True)
    flags = [flag]
    for k in range(1, groups):
        flags.append(lax.ppermute(flag, "groups", [(g, (g + k) % groups) for g in range(groups)]))
    odd = functools.reduce(jnp.maximum, flags)[0, 0]
    nearest = call(
        functools.partial(final_kernel, peers, cap),
        "final",
        shape((1, count), f32),
        [VMEM] * 6,
        VMEM,
        flops=0,
        nbytes=4 * count,
    )(info, back, *tops).reshape(count)
    return lax.cond(odd > 0, whole_exchange, lambda e, c: nearest, embeddings, cluster_ids)


def solution(mesh):
    return jax.shard_map(
        local,
        mesh=mesh,
        in_specs=(P(("groups", "dp", "owner"), None), P(("groups", "dp", "owner"))),
        out_specs=P(("groups", "dp", "owner")),
        check_vma=False,
    )
```

time: 314 us -> 135 us (0.43)
  waiting for transfers between devices: 150 us -> 16.9 us
  starting transfers between devices: 13.5 us -> 71.5 us
  blocking collectives: 42.7 us -> 0 us
  matrix products: 37.9 us -> 0 us
  other arithmetic: 31.6 us -> 0.01 us
  Pallas kernels: 0 us -> 21.2 us
  loops' own time: 7.4 us -> 0.23 us
  local copies, waits for them, and re-layouts: 29.3 us -> 24 us
    all_to_all x2 -> x1, waiting for transfers between devices: 150 us -> 0.01 us  [local(): back = lax.all_to_all(best, 'dp', split_axis=0, concat_axis=0, tiled=True)]
    ppermute x0 -> x29, starting transfers between devices: none -> 64.7 us  [the longest x7 30.5 us: local(): lax.ppermute(blocks[k], 'dp', [(d, (d + k) % peers) for d in range(peers)])]
    all_to_all x1 -> x0, blocking collectives: 42.7 us -> none  [local(): lax.all_to_all(best, 'dp', split_axis=0, concat_axis=0, tiled=True)]
    dot_general x4 -> x0, matrix products: 37.9 us -> none  [block_best(): lax.dot_general(queries, columns, (((1,), (1,)), ((), ())), preferred_ele...]
    unnamed x0 -> x60, local copies, waits for them, and re-layouts: none -> 23.5 us
    pallas_call x0 -> x5, Pallas kernels: none -> 21.2 us  [the longest x1 10.1 us: local(): call(functools.partial(block_best_kernel, peers, block), 'block_best', [s...]
    ppermute x0 -> x29, waiting for transfers between devices: none -> 16.9 us  [the longest x7 10.3 us: local(): lax.ppermute(blocks[k], 'dp', [(d, (d + k) % peers) for d in range(peers)])]
    concatenate x4 -> x0, other arithmetic: 13.3 us -> none  [the longest x1 7.67 us: local(): columns = jnp.concatenate([own_rows, rest_rows], axis=0)]
  transfers between devices with their start and end apart: 2 -> 30, of which waited for: 1 -> 7; matrix products, arithmetic and copies ran while one was open for 4% -> 0% of each run, Pallas kernels for 0% -> 11%
where the time goes in v1:
time: 135 us
  starting transfers between devices  71.5 us (53%)
  local copies, waits for them, and re-layouts  24 us (18%)
  Pallas kernels  21.2 us (16%)
  waiting for transfers between devices  16.9 us (13%)
    ppermute x7, starting transfers between devices, local(): lax.ppermute(blocks[k], 'dp', [(d, (d + k) % peers) for d in range(peers)])  30.5 us
    unnamed x60, local copies, waits for them, and re-layouts  23.5 us
    ppermute x3, starting transfers between devices, local(): up = lax.ppermute(up, 'dp', up_pairs)  19.1 us
    ppermute x7, waiting for transfers between devices, local(): lax.ppermute(blocks[k], 'dp', [(d, (d + k) % peers) for d in range(peers)])  10.3 us
    pallas_call x1, Pallas kernels, local(): call(functools.partial(block_best_kernel, peers, block), 'block_best', [s...  10.1 us
    all_to_all x1, starting transfers between devices, local(): back = lax.all_to_all(best, 'dp', split_axis=0, concat_axis=0, tiled=True)  6.76 us
    ppermute x1, starting transfers between devices, local(): lead_y = lax.ppermute(lead, 'dp', other_y)  4.48 us
    pallas_call x1, Pallas kernels, local(): call(functools.partial(leader_best_kernel, reach, cap), 'leader_best', [s...  4.11 us
  transfers between devices with their start and end apart: 30, of which 7 were waited for; matrix products, arithmetic and copies ran while one was open for 0% of the time, Pallas kernels for 11%

profile of v1, /device:TPU:0, one launch (start us, length us, event | category | flops | bytes accessed | tf_op | source)
XLA Modules:
  0.0 134.6 jit_solution(1468301800878611602)
XLA Ops:
  0.0 4.1 %lead.1 = (bf16[1024,1024]{1,0:T(8,128)(2,1)S(1)}, s32[8,1024]{1,0:T(8,128)S(1)}, f32[8,1024]{1,0:T(8,128)S(1)}, bf16[272,1024]{1,0:T(8,128)(2,1)S(1)}) custom-call(s32[1]{0:T(128)} %bitcast.8.me_ref, s32[1,1024]{1,0:T(1,128)} %bitcast.49, f32[1024,1024]{1,0:T(8,128)} %emb_ref.1), custom_call_target="tpu_custom_call" | custom-call | flops 536870912 | bytes 6291456 | tf_op jit(solution)/shard_map/lead/pallas_call | solution.py:296
  4.1 2.1 %pack.1 = (bf16[112,1024]{1,0:T(8,128)(2,1)S(1)}, bf16[112,1024]{1,0:T(8,128)(2,1)S(1)}, bf16[112,1024]{1,0:T(8,128)(2,1)S(1)}, bf16[112,1024]{1,0:T(8,128)(2,1)...) custom-call(bf16[1024,1024]{1,0:T(8,128)(2,1)S(1)} %get-tuple-elemen, ...), custom_call_target="tpu_custom_call" | custom-call | flops 1879048192 | bytes 4194304 | tf_op jit(solution)/shard_map/pack/pallas_call | solution.py:327
  6.1 3.0 %collective-permute-start.2 = (bf16[112,1024]{1,0:T(8,128)(2,1)S(1)}, bf16[112,1024]{1,0:T(8,128)(2,1)S(1)}, u32[]{:S(2)}, u32[]{:S(2)}) collective-permute-start(bf16[112,1024]{1,0:T(8,128)(2,1)S(1)} %get-tuple-element.81), channel_id=1, source_target_pairs={{0,2},{2,4},{4,6},{6,8},{8,10},{10,12},{12,14},{14,0},{1,3},{3,5},... | collective-permute-start | bytes 688136 | tf_op jit(solution)/shard_map/ppermute | solution.py:339
  9.2 1.6 %collective-permute-start.3 = (bf16[112,1024]{1,0:T(8,128)(2,1)S(1)}, bf16[112,1024]{1,0:T(8,128)(2,1)S(1)}, u32[]{:S(2)}, u32[]{:S(2)}) collective-permute-start(bf16[112,1024]{1,0:T(8,128)(2,1)S(1)} %get-tuple-element.82), channel_id=1, source_target_pairs={{0,4},{2,6},{4,8},{6,10},{8,12},{10,14},{12,0},{14,2},{1,5},{3,7},... | collective-permute-start | bytes 688136 | tf_op jit(solution)/shard_map/ppermute | solution.py:339
  10.7 2.5 %collective-permute-start.4 = (bf16[112,1024]{1,0:T(8,128)(2,1)S(1)}, bf16[112,1024]{1,0:T(8,128)(2,1)S(1)}, u32[]{:S(2)}, u32[]{:S(2)}) collective-permute-start(bf16[112,1024]{1,0:T(8,128)(2,1)S(1)} %get-tuple-element.83), channel_id=1, source_target_pairs={{0,6},{2,8},{4,10},{6,12},{8,14},{10,0},{12,2},{14,4},{1,7},{3,9},... | collective-permute-start | bytes 688136 | tf_op jit(solution)/shard_map/ppermute | solution.py:339
  13.3 1.2 collective-permute-start.5
  14.5 3.5 %collective-permute-start.21 = (bf16[272,1024]{1,0:T(8,128)(2,1)S(1)}, bf16[272,1024]{1,0:T(8,128)(2,1)S(1)}, u32[]{:S(2)}, u32[]{:S(2)}) collective-permute-start(bf16[272,1024]{1,0:T(8,128)(2,1)S(1)} %get-tuple-element.90.rest_0_), channel_id=1, source_target_pairs={{0,4},{2,6},{4,8},{6,10},{8,12},{10,14},{1,5},{3,7},{5,9},{7,11},{... | collective-permute-start | bytes 1671176 | tf_op jit(solution)/shard_map/ppermute | solution.py:323
  18.7 1.3 collective-permute-start.24
  20.0 14.3 %collective-permute-start.6 = (bf16[112,1024]{1,0:T(8,128)(2,1)S(1)}, bf16[112,1024]{1,0:T(8,128)(2,1)S(1)}, u32[]{:S(2)}, u32[]{:S(2)}) collective-permute-start(bf16[112,1024]{1,0:T(8,128)(2,1)S(1)} %get-tuple-element.85), channel_id=1, source_target_pairs={{0,10},{2,12},{4,14},{6,0},{8,2},{10,4},{12,6},{14,8},{1,11},{3,13... | collective-permute-start | bytes 688136 | tf_op jit(solution)/shard_map/ppermute | solution.py:339
  34.4 3.3 %collective-permute-done.4.rest_3_ = bf16[112,1024]{1,0:T(8,128)(2,1)S(1)} collective-permute-done((bf16[112,1024]{1,0:T(8,128)(2,1)S(1)}, bf16[112,1024]{1,0:T(8,128)(2,1)S(1)}, u32[]{:S(2)}, u32[]{:S(2)}) %collective-permute-start.4) | collective-permute-done | bytes 229408 | tf_op jit(solution)/shard_map/ppermute | solution.py:339
  37.7 2.6 %collective-permute-start.7 = (bf16[112,1024]{1,0:T(8,128)(2,1)S(1)}, bf16[112,1024]{1,0:T(8,128)(2,1)S(1)}, u32[]{:S(2)}, u32[]{:S(2)}) collective-permute-start(bf16[112,1024]{1,0:T(8,128)(2,1)S(1)} %get-tuple-element.86), channel_id=1, source_target_pairs={{0,12},{2,14},{4,0},{6,2},{8,4},{10,6},{12,8},{14,10},{1,13},{3,15... | collective-permute-start | bytes 688136 | tf_op jit(solution)/shard_map/ppermute | solution.py:339
  40.3 5.2 %collective-permute-start.8 = (bf16[112,1024]{1,0:T(8,128)(2,1)S(1)}, bf16[112,1024]{1,0:T(8,128)(2,1)}, u32[]{:S(2)}, u32[]{:S(2)}) collective-permute-start(bf16[112,1024]{1,0:T(8,128)(2,1)S(1)} %get-tuple-element.87), channel_id=1, source_target_pairs={{0,14},{2,0},{4,2},{6,4},{8,6},{10,8},{12,10},{14,12},{1,15},{3,1}... | collective-permute-start | bytes 688136 | tf_op jit(solution)/shard_map/ppermute | solution.py:339
  45.5 4.8 %collective-permute-done.6.rest_5_ = bf16[112,1024]{1,0:T(8,128)(2,1)S(1)} collective-permute-done((bf16[112,1024]{1,0:T(8,128)(2,1)S(1)}, bf16[112,1024]{1,0:T(8,128)(2,1)S(1)}, u32[]{:S(2)}, u32[]{:S(2)}) %collective-permute-start.6) | collective-permute-done | bytes 229408 | tf_op jit(solution)/shard_map/ppermute | solution.py:339
  52.2 1.5 %collective-permute-done.8.rest_7_ = bf16[112,1024]{1,0:T(8,128)(2,1)} collective-permute-done((bf16[112,1024]{1,0:T(8,128)(2,1)S(1)}, bf16[112,1024]{1,0:T(8,128)(2,1)}, u32[]{:S(2)}, u32[]{:S(2)}) %collective-permute-start.8) | collective-permute-done | bytes 229408 | tf_op jit(solution)/shard_map/ppermute | solution.py:339
  55.1 4.5 %collective-permute-start.18 = (bf16[272,1024]{1,0:T(8,128)(2,1)S(1)}, bf16[272,1024]{1,0:T(8,128)(2,1)S(1)}, u32[]{:S(2)}, u32[]{:S(2)}) collective-permute-start(bf16[272,1024]{1,0:T(8,128)(2,1)S(1)} %get-tuple-element.90.rest_0_), channel_id=1, source_target_pairs={{0,2},{2,0},{4,6},{6,4},{8,10},{10,8},{12,14},{14,12},{1,3},{3,1},... | collective-permute-start | bytes 1671176 | tf_op jit(solution)/shard_map/ppermute | solution.py:342
  59.6 10.4 %collective-permute-start.22 = (bf16[272,1024]{1,0:T(8,128)(2,1)S(1)}, bf16[272,1024]{1,0:T(8,128)(2,1)S(1)}, u32[]{:S(2)}, u32[]{:S(2)}) collective-permute-start(bf16[272,1024]{1,0:T(8,128)(2,1)S(1)} %collective-permute-done.21.rest_4_), channel_id=1, source_target_pairs={{0,4},{2,6},{4,8},{6,10},{8,12},{10,14},{1,5},{3,7},{5,9},{7,11},{... | collective-permute-start | bytes 1671176 | tf_op jit(solution)/shard_map/ppermute | solution.py:323
  70.0 1.3 collective-permute-start.25
  79.2 3.1 %collective-permute-done.22.rest_5_ = bf16[272,1024]{1,0:T(8,128)(2,1)S(1)} collective-permute-done((bf16[272,1024]{1,0:T(8,128)(2,1)S(1)}, bf16[272,1024]{1,0:T(8,128)(2,1)S(1)}, u32[]{:S(2)}, u32[]{:S(2)}) %collective-permute-start.22) | collective-permute-done | bytes 557088 | tf_op jit(solution)/shard_map/ppermute | solution.py:323
  82.2 5.2 %collective-permute-start.23 = (bf16[272,1024]{1,0:T(8,128)(2,1)S(1)}, bf16[272,1024]{1,0:T(8,128)(2,1)}, u32[]{:S(2)}, u32[]{:S(2)}) collective-permute-start(bf16[272,1024]{1,0:T(8,128)(2,1)S(1)} %collective-permute-done.22.rest_5_), channel_id=1, source_target_pairs={{0,4},{2,6},{4,8},{6,10},{8,12},{10,14},{1,5},{3,7},{5,9},{7,11},{... | collective-permute-start | bytes 1671176 | tf_op jit(solution)/shard_map/ppermute | solution.py:323
  87.5 1.3 collective-permute-start.26
  89.4 1.8 %collective-permute-done.16.rest_15_ = bf16[112,1024]{1,0:T(8,128)(2,1)} collective-permute-done((bf16[112,1024]{1,0:T(8,128)(2,1)}, bf16[112,1024]{1,0:T(8,128)(2,1)}, u32[]{:S(2)}, u32[]{:S(2)}) %collective-permute-start.16) | collective-permute-done | bytes 229408 | tf_op jit(solution)/shard_map/ppermute | solution.py:340
  91.3 0.9 copy-done.1
  92.2 0.9 copy-done.3
  93.2 0.9 copy-done.5
  94.1 0.9 copy-done.7
  95.0 0.9 copy-done.9
  104.4 10.1 %block_best.1 = (f32[8,128]{1,0:T(8,128)}, f32[8,128]{1,0:T(8,128)S(1)}) custom-call(s32[1]{0:T(128)} %bitcast.8.me_ref, bf16[112,1024]{1,0:T(8,128)(2,1)S(1)} %copy-done.1, bf16[112,1024]{1,0:T(8,128)(2,1)S(1)} %copy-done.3, bf16[112,1024]{1,0:T(8,128)(2,1)S(1)} %copy-done.5, bf16[112,1024]{1,0:T(8,128)(2,1)S(1)} %copy-done.7, ...), custom_call_target="tpu_custom_call" | custom-call | flops 3288334336 | bytes 3670016 | tf_op jit(solution)/shard_map/block_best/pallas_call | solution.py:368
  114.6 6.8 %all-to-all-start.3 = ((f32[8,1,128]{2,1,0:T(1,128)}), f32[8,1,128]{2,1,0:T(1,128)S(1)}, u32[]{:S(2)}, u32[]{:S(2)}) async-start(f32[8,1,128]{2,1,0:T(1,128)} %bitcast.12), calls=%async_computation.3 | async-start | bytes 8192 | tf_op jit(solution)/shard_map/all_to_all | solution.py:378
  121.3 1.5 %collective-permute-start.17 = (f32[8,128]{1,0:T(8,128)S(1)}, f32[8,128]{1,0:T(8,128)S(1)}, u32[]{:S(2)}, u32[]{:S(2)}) collective-permute-start(f32[8,128]{1,0:T(8,128)S(1)} %get-tuple-element.88), channel_id=1, source_target_pairs={{0,16},{16,0},{1,17},{17,1},{2,18},{18,2},{3,19},{19,3},{4,20},{20... | collective-permute-start | bytes 12296 | tf_op jit(solution)/shard_map/ppermute | solution.py:381
  122.9 4.1 %leader_best.1 = (f32[1,256]{1,0:T(1,128)S(1)}, f32[1,256]{1,0:T(1,128)S(1)}, f32[1,256]{1,0:T(1,128)S(1)}, f32[1,256]{1,0:T(1,128)S(1)}) custom-call(s32[1]{0:T(128)} %bitcast.14.pos_ref, bf16[272,1024]{1,0:T(8,128)(2,1)S(1)} %get-tuple-element.90.rest_0_, bf16[272,1024]{1,0:T(8,128)(2,1)S(1)} %collective-permute-done.18.rest_1_, ...), custom_call_target="tpu_custom_call" | custom-call | flops 2147483648 | bytes 4194304 | tf_op jit(solution)/shard_map/leader_best/pallas_call | solution.py:345
  127.0 2.1 %collective-permute-start.27 = (f32[1,256]{1,0:T(1,128)S(1)}, f32[1,256]{1,0:T(1,128)S(1)}, u32[]{:S(2)}, u32[]{:S(2)}) collective-permute-start(f32[1,256]{1,0:T(1,128)S(1)} %get-tuple-element.92), channel_id=1, source_target_pairs={{0,2},{2,0},{4,6},{6,4},{8,10},{10,8},{12,14},{14,12},{1,3},{3,1},... | collective-permute-start | bytes 3080 | tf_op jit(solution)/shard_map/ppermute | solution.py:363
  131.3 1.6 %collective-permute-done.30.rest_3_ = f32[1,256]{1,0:T(1,128)S(1)} collective-permute-done((f32[1,256]{1,0:T(1,128)S(1)}, f32[1,256]{1,0:T(1,128)S(1)}, u32[]{:S(2)}, u32[]{:S(2)}) %collective-permute-start.30) | collective-permute-done | bytes 1056 | tf_op jit(solution)/shard_map/ppermute | solution.py:365
  (96 shorter events, 24.3 us)
Async XLA Ops:
  6.1 12.6 %collective-permute-start.2 = (bf16[112,1024]{1,0:T(8,128)(2,1)S(1)}, bf16[112,1024]{1,0:T(8,128)(2,1)S(1)}, u32[]{:S(2)}, u32[]{:S(2)}) collective-permute-start(bf16[112,1024]{1,0:T(8,128)(2,1)S(1)} %get-tuple-element.81), channel_id=1, source_target_pairs={{0,2},{2,4},{4,6},{6,8},{8,10},{10,12},{12,14},{14,0},{1,3},{3,5},... | collective-permute-start | bytes 688136 | tf_op jit(solution)/shard_map/ppermute | solution.py:339
  9.2 10.9 %collective-permute-start.3 = (bf16[112,1024]{1,0:T(8,128)(2,1)S(1)}, bf16[112,1024]{1,0:T(8,128)(2,1)S(1)}, u32[]{:S(2)}, u32[]{:S(2)}) collective-permute-start(bf16[112,1024]{1,0:T(8,128)(2,1)S(1)} %get-tuple-element.82), channel_id=1, source_target_pairs={{0,4},{2,6},{4,8},{6,10},{8,12},{10,14},{12,0},{14,2},{1,5},{3,7},... | collective-permute-start | bytes 688136 | tf_op jit(solution)/shard_map/ppermute | solution.py:339
  10.7 26.9 %collective-permute-start.4 = (bf16[112,1024]{1,0:T(8,128)(2,1)S(1)}, bf16[112,1024]{1,0:T(8,128)(2,1)S(1)}, u32[]{:S(2)}, u32[]{:S(2)}) collective-permute-start(bf16[112,1024]{1,0:T(8,128)(2,1)S(1)} %get-tuple-element.83), channel_id=1, source_target_pairs={{0,6},{2,8},{4,10},{6,12},{8,14},{10,0},{12,2},{14,4},{1,7},{3,9},... | collective-permute-start | bytes 688136 | tf_op jit(solution)/shard_map/ppermute | solution.py:339
  13.3 27.0 %collective-permute-start.5 = (bf16[112,1024]{1,0:T(8,128)(2,1)S(1)}, bf16[112,1024]{1,0:T(8,128)(2,1)S(1)}, u32[]{:S(2)}, u32[]{:S(2)}) collective-permute-start(bf16[112,1024]{1,0:T(8,128)(2,1)S(1)} %get-tuple-element.84), channel_id=1, source_target_pairs={{0,8},{2,10},{4,12},{6,14},{8,0},{10,2},{12,4},{14,6},{1,9},{3,11}... | collective-permute-start | bytes 688136 | tf_op jit(solution)/shard_map/ppermute | solution.py:339
  14.5 45.1 %collective-permute-start.21 = (bf16[272,1024]{1,0:T(8,128)(2,1)S(1)}, bf16[272,1024]{1,0:T(8,128)(2,1)S(1)}, u32[]{:S(2)}, u32[]{:S(2)}) collective-permute-start(bf16[272,1024]{1,0:T(8,128)(2,1)S(1)} %get-tuple-element.90.rest_0_), channel_id=1, source_target_pairs={{0,4},{2,6},{4,8},{6,10},{8,12},{10,14},{1,5},{3,7},{5,9},{7,11},{... | collective-permute-start | bytes 1671176 | tf_op jit(solution)/shard_map/ppermute | solution.py:323
  18.7 51.3 %collective-permute-start.24 = (bf16[272,1024]{1,0:T(8,128)(2,1)S(1)}, bf16[272,1024]{1,0:T(8,128)(2,1)S(1)}, u32[]{:S(2)}, u32[]{:S(2)}) collective-permute-start(bf16[272,1024]{1,0:T(8,128)(2,1)S(1)} %get-tuple-element.90.rest_0_), channel_id=1, source_target_pairs={{4,0},{6,2},{8,4},{10,6},{12,8},{14,10},{5,1},{7,3},{9,5},{11,7},{... | collective-permute-start | bytes 1671176 | tf_op jit(solution)/shard_map/ppermute | solution.py:324
  20.0 30.3 %collective-permute-start.6 = (bf16[112,1024]{1,0:T(8,128)(2,1)S(1)}, bf16[112,1024]{1,0:T(8,128)(2,1)S(1)}, u32[]{:S(2)}, u32[]{:S(2)}) collective-permute-start(bf16[112,1024]{1,0:T(8,128)(2,1)S(1)} %get-tuple-element.85), channel_id=1, source_target_pairs={{0,10},{2,12},{4,14},{6,0},{8,2},{10,4},{12,6},{14,8},{1,11},{3,13... | collective-permute-start | bytes 688136 | tf_op jit(solution)/shard_map/ppermute | solution.py:339
  37.7 13.3 %collective-permute-start.7 = (bf16[112,1024]{1,0:T(8,128)(2,1)S(1)}, bf16[112,1024]{1,0:T(8,128)(2,1)S(1)}, u32[]{:S(2)}, u32[]{:S(2)}) collective-permute-start(bf16[112,1024]{1,0:T(8,128)(2,1)S(1)} %get-tuple-element.86), channel_id=1, source_target_pairs={{0,12},{2,14},{4,0},{6,2},{8,4},{10,6},{12,8},{14,10},{1,13},{3,15... | collective-permute-start | bytes 688136 | tf_op jit(solution)/shard_map/ppermute | solution.py:339
  40.3 13.4 %collective-permute-start.8 = (bf16[112,1024]{1,0:T(8,128)(2,1)S(1)}, bf16[112,1024]{1,0:T(8,128)(2,1)}, u32[]{:S(2)}, u32[]{:S(2)}) collective-permute-start(bf16[112,1024]{1,0:T(8,128)(2,1)S(1)} %get-tuple-element.87), channel_id=1, source_target_pairs={{0,14},{2,0},{4,2},{6,4},{8,6},{10,8},{12,10},{14,12},{1,15},{3,1}... | collective-permute-start | bytes 688136 | tf_op jit(solution)/shard_map/ppermute | solution.py:339
  50.3 4.1 %collective-permute-start.9 = (bf16[112,1024]{1,0:T(8,128)(2,1)S(1)}, bf16[112,1024]{1,0:T(8,128)(2,1)S(1)}, u32[]{:S(2)}, u32[]{:S(2)}) collective-permute-start(bf16[112,1024]{1,0:T(8,128)(2,1)S(1)} %get-tuple-element.80.rest_0_), channel_id=1, source_target_pairs={{0,1},{1,0},{2,3},{3,2},{4,5},{5,4},{6,7},{7,6},{8,9},{9,8},{10,11... | collective-permute-start | bytes 688136 | tf_op jit(solution)/shard_map/ppermute | solution.py:340
  51.0 20.3 %collective-permute-start.10 = (bf16[112,1024]{1,0:T(8,128)(2,1)S(1)}, bf16[112,1024]{1,0:T(8,128)(2,1)S(1)}, u32[]{:S(2)}, u32[]{:S(2)}) collective-permute-start(bf16[112,1024]{1,0:T(8,128)(2,1)S(1)} %collective-permute-done.2.rest_1_), channel_id=1, source_target_pairs={{0,1},{1,0},{2,3},{3,2},{4,5},{5,4},{6,7},{7,6},{8,9},{9,8},{10,11... | collective-permute-start | bytes 688136 | tf_op jit(solution)/shard_map/ppermute | solution.py:340
  53.7 19.1 %collective-permute-start.11 = (bf16[112,1024]{1,0:T(8,128)(2,1)S(1)}, bf16[112,1024]{1,0:T(8,128)(2,1)S(1)}, u32[]{:S(2)}, u32[]{:S(2)}) collective-permute-start(bf16[112,1024]{1,0:T(8,128)(2,1)S(1)} %collective-permute-done.3.rest_2_), channel_id=1, source_target_pairs={{0,1},{1,0},{2,3},{3,2},{4,5},{5,4},{6,7},{7,6},{8,9},{9,8},{10,11... | collective-permute-start | bytes 688136 | tf_op jit(solution)/shard_map/ppermute | solution.py:340
  55.1 23.6 %collective-permute-start.18 = (bf16[272,1024]{1,0:T(8,128)(2,1)S(1)}, bf16[272,1024]{1,0:T(8,128)(2,1)S(1)}, u32[]{:S(2)}, u32[]{:S(2)}) collective-permute-start(bf16[272,1024]{1,0:T(8,128)(2,1)S(1)} %get-tuple-element.90.rest_0_), channel_id=1, source_target_pairs={{0,2},{2,0},{4,6},{6,4},{8,10},{10,8},{12,14},{14,12},{1,3},{3,1},... | collective-permute-start | bytes 1671176 | tf_op jit(solution)/shard_map/ppermute | solution.py:342
  59.6 22.6 %collective-permute-start.22 = (bf16[272,1024]{1,0:T(8,128)(2,1)S(1)}, bf16[272,1024]{1,0:T(8,128)(2,1)S(1)}, u32[]{:S(2)}, u32[]{:S(2)}) collective-permute-start(bf16[272,1024]{1,0:T(8,128)(2,1)S(1)} %collective-permute-done.21.rest_4_), channel_id=1, source_target_pairs={{0,4},{2,6},{4,8},{6,10},{8,12},{10,14},{1,5},{3,7},{5,9},{7,11},{... | collective-permute-start | bytes 1671176 | tf_op jit(solution)/shard_map/ppermute | solution.py:323
  70.0 17.4 %collective-permute-start.25 = (bf16[272,1024]{1,0:T(8,128)(2,1)S(1)}, bf16[272,1024]{1,0:T(8,128)(2,1)S(1)}, u32[]{:S(2)}, u32[]{:S(2)}) collective-permute-start(bf16[272,1024]{1,0:T(8,128)(2,1)S(1)} %collective-permute-done.24.rest_7_), channel_id=1, source_target_pairs={{4,0},{6,2},{8,4},{10,6},{12,8},{14,10},{5,1},{7,3},{9,5},{11,7},{... | collective-permute-start | bytes 1671176 | tf_op jit(solution)/shard_map/ppermute | solution.py:324
  72.1 2.6 %collective-permute-start.12 = (bf16[112,1024]{1,0:T(8,128)(2,1)S(1)}, bf16[112,1024]{1,0:T(8,128)(2,1)S(1)}, u32[]{:S(2)}, u32[]{:S(2)}) collective-permute-start(bf16[112,1024]{1,0:T(8,128)(2,1)S(1)} %collective-permute-done.4.rest_3_), channel_id=1, source_target_pairs={{0,1},{1,0},{2,3},{3,2},{4,5},{5,4},{6,7},{7,6},{8,9},{9,8},{10,11... | collective-permute-start | bytes 688136 | tf_op jit(solution)/shard_map/ppermute | solution.py:340
  73.4 2.6 %collective-permute-start.13 = (bf16[112,1024]{1,0:T(8,128)(2,1)S(1)}, bf16[112,1024]{1,0:T(8,128)(2,1)S(1)}, u32[]{:S(2)}, u32[]{:S(2)}) collective-permute-start(bf16[112,1024]{1,0:T(8,128)(2,1)S(1)} %collective-permute-done.5.rest_4_), channel_id=1, source_target_pairs={{0,1},{1,0},{2,3},{3,2},{4,5},{5,4},{6,7},{7,6},{8,9},{9,8},{10,11... | collective-permute-start | bytes 688136 | tf_op jit(solution)/shard_map/ppermute | solution.py:340
  75.4 2.6 %collective-permute-start.14 = (bf16[112,1024]{1,0:T(8,128)(2,1)S(1)}, bf16[112,1024]{1,0:T(8,128)(2,1)S(1)}, u32[]{:S(2)}, u32[]{:S(2)}) collective-permute-start(bf16[112,1024]{1,0:T(8,128)(2,1)S(1)} %collective-permute-done.6.rest_5_), channel_id=1, source_target_pairs={{0,1},{1,0},{2,3},{3,2},{4,5},{5,4},{6,7},{7,6},{8,9},{9,8},{10,11... | collective-permute-start | bytes 688136 | tf_op jit(solution)/shard_map/ppermute | solution.py:340
  76.7 12.0 %collective-permute-start.15 = (bf16[112,1024]{1,0:T(8,128)(2,1)S(1)}, bf16[112,1024]{1,0:T(8,128)(2,1)S(1)}, u32[]{:S(2)}, u32[]{:S(2)}) collective-permute-start(bf16[112,1024]{1,0:T(8,128)(2,1)S(1)} %collective-permute-done.7.rest_6_), channel_id=1, source_target_pairs={{0,1},{1,0},{2,3},{3,2},{4,5},{5,4},{6,7},{7,6},{8,9},{9,8},{10,11... | collective-permute-start | bytes 688136 | tf_op jit(solution)/shard_map/ppermute | solution.py:340
  78.7 44.2 %collective-permute-start.19 = (bf16[272,1024]{1,0:T(8,128)(2,1)S(1)}, bf16[272,1024]{1,0:T(8,128)(2,1)}, u32[]{:S(2)}, u32[]{:S(2)}) collective-permute-start(bf16[272,1024]{1,0:T(8,128)(2,1)S(1)} %get-tuple-element.90.rest_0_), channel_id=1, source_target_pairs={{0,1},{1,0},{2,3},{3,2},{4,5},{5,4},{6,7},{7,6},{8,9},{9,8},{10,11... | collective-permute-start | bytes 1671176 | tf_op jit(solution)/shard_map/ppermute | solution.py:343
  78.7 44.2 %collective-permute-start.20 = (bf16[272,1024]{1,0:T(8,128)(2,1)S(1)}, bf16[272,1024]{1,0:T(8,128)(2,1)}, u32[]{:S(2)}, u32[]{:S(2)}) collective-permute-start(bf16[272,1024]{1,0:T(8,128)(2,1)S(1)} %collective-permute-done.18.rest_1_), channel_id=1, source_target_pairs={{0,1},{1,0},{2,3},{3,2},{4,5},{5,4},{6,7},{7,6},{8,9},{9,8},{10,11... | collective-permute-start | bytes 1671176 | tf_op jit(solution)/shard_map/ppermute | solution.py:344
  82.2 40.6 %collective-permute-start.23 = (bf16[272,1024]{1,0:T(8,128)(2,1)S(1)}, bf16[272,1024]{1,0:T(8,128)(2,1)}, u32[]{:S(2)}, u32[]{:S(2)}) collective-permute-start(bf16[272,1024]{1,0:T(8,128)(2,1)S(1)} %collective-permute-done.22.rest_5_), channel_id=1, source_target_pairs={{0,4},{2,6},{4,8},{6,10},{8,12},{10,14},{1,5},{3,7},{5,9},{7,11},{... | collective-permute-start | bytes 1671176 | tf_op jit(solution)/shard_map/ppermute | solution.py:323
  87.5 35.4 %collective-permute-start.26 = (bf16[272,1024]{1,0:T(8,128)(2,1)S(1)}, bf16[272,1024]{1,0:T(8,128)(2,1)}, u32[]{:S(2)}, u32[]{:S(2)}) collective-permute-start(bf16[272,1024]{1,0:T(8,128)(2,1)S(1)} %collective-permute-done.25.rest_8_), channel_id=1, source_target_pairs={{4,0},{6,2},{8,4},{10,6},{12,8},{14,10},{5,1},{7,3},{9,5},{11,7},{... | collective-permute-start | bytes 1671176 | tf_op jit(solution)/shard_map/ppermute | solution.py:324
  89.4 1.8 %collective-permute-start.16 = (bf16[112,1024]{1,0:T(8,128)(2,1)}, bf16[112,1024]{1,0:T(8,128)(2,1)}, u32[]{:S(2)}, u32[]{:S(2)}) collective-permute-start(bf16[112,1024]{1,0:T(8,128)(2,1)} %collective-permute-done.8.rest_7_), channel_id=1, source_target_pairs={{0,1},{1,0},{2,3},{3,2},{4,5},{5,4},{6,7},{7,6},{8,9},{9,8},{10,11... | collective-permute-start | bytes 688136 | tf_op jit(solution)/shard_map/ppermute | solution.py:340
  91.3 0.9 copy-start.1
  114.6 19.2 %copy-start.28 = (s32[1024]{0:T(1024)S(1)}, s32[1024]{0:T(1024)}, u32[]{:S(2)}) copy-start(s32[1024]{0:T(1024)} %param.7) | copy-start | bytes 12292
  114.6 16.7 %all-to-all-start.3 = ((f32[8,1,128]{2,1,0:T(1,128)}), f32[8,1,128]{2,1,0:T(1,128)S(1)}, u32[]{:S(2)}, u32[]{:S(2)}) async-start(f32[8,1,128]{2,1,0:T(1,128)} %bitcast.12), calls=%async_computation.3 | async-start | bytes 8192 | tf_op jit(solution)/shard_map/all_to_all | solution.py:378
  121.3 8.9 %collective-permute-start.17 = (f32[8,128]{1,0:T(8,128)S(1)}, f32[8,128]{1,0:T(8,128)S(1)}, u32[]{:S(2)}, u32[]{:S(2)}) collective-permute-start(f32[8,128]{1,0:T(8,128)S(1)} %get-tuple-element.88), channel_id=1, source_target_pairs={{0,16},{16,0},{1,17},{17,1},{2,18},{18,2},{3,19},{19,3},{4,20},{20... | collective-permute-start | bytes 12296 | tf_op jit(solution)/shard_map/ppermute | solution.py:381
  127.0 2.3 %collective-permute-start.29 = (f32[1,256]{1,0:T(1,128)S(1)}, f32[1,256]{1,0:T(1,128)S(1)}, u32[]{:S(2)}, u32[]{:S(2)}) collective-permute-start(f32[1,256]{1,0:T(1,128)S(1)} %get-tuple-element.94), channel_id=1, source_target_pairs={{0,1},{1,0},{2,3},{3,2},{4,5},{5,4},{6,7},{7,6},{8,9},{9,8},{10,11... | collective-permute-start | bytes 3080 | tf_op jit(solution)/shard_map/ppermute | solution.py:365
  127.0 4.2 %collective-permute-start.27 = (f32[1,256]{1,0:T(1,128)S(1)}, f32[1,256]{1,0:T(1,128)S(1)}, u32[]{:S(2)}, u32[]{:S(2)}) collective-permute-start(f32[1,256]{1,0:T(1,128)S(1)} %get-tuple-element.92), channel_id=1, source_target_pairs={{0,2},{2,0},{4,6},{6,4},{8,10},{10,8},{12,14},{14,12},{1,3},{3,1},... | collective-permute-start | bytes 3080 | tf_op jit(solution)/shard_map/ppermute | solution.py:363
  129.1 2.1 %collective-permute-start.28 = (f32[1,256]{1,0:T(1,128)S(1)}, f32[1,256]{1,0:T(1,128)S(1)}, u32[]{:S(2)}, u32[]{:S(2)}) collective-permute-start(f32[1,256]{1,0:T(1,128)S(1)} %get-tuple-element.93), channel_id=1, source_target_pairs={{0,1},{1,0},{2,3},{3,2},{4,5},{5,4},{6,7},{7,6},{8,9},{9,8},{10,11... | collective-permute-start | bytes 3080 | tf_op jit(solution)/shard_map/ppermute | solution.py:364
  129.3 3.6 %collective-permute-start.30 = (f32[1,256]{1,0:T(1,128)S(1)}, f32[1,256]{1,0:T(1,128)S(1)}, u32[]{:S(2)}, u32[]{:S(2)}) collective-permute-start(f32[1,256]{1,0:T(1,128)S(1)} %collective-permute-done.29), channel_id=1, source_target_pairs={{0,2},{2,0},{4,6},{6,4},{8,10},{10,8},{12,14},{14,12},{1,3},{3,1},... | collective-permute-start | bytes 3080 | tf_op jit(solution)/shard_map/ppermute | solution.py:365
  (28 other events, 22.6 us)

commit v2 on v1

--- a/solution.py
+++ b/solution.py
@@ -11,8 +11,7 @@
 CL_DEV = 8
 LANES = 128
 SUB = 16
-VMEM_LIMIT = 48 * 1024 * 1024
-ANY = pl.BlockSpec(memory_space=pl.ANY)
+VMEM_LIMIT = 24 * 1024 * 1024
 VMEM = pl.BlockSpec(memory_space=pltpu.VMEM)
 SMEM = pl.BlockSpec(memory_space=pltpu.SMEM)
 NT = (((1,), (1,)), ((), ()))
@@ -53,11 +52,13 @@
     lead_short = jnp.max(jnp.where(tio == leader, cap - counts, 0), axis=0, keepdims=True)
     bad = ((others > block - 1) | (lead_short != 0)).astype(jnp.int32)
     is_lead = target == leader
-    rel = target - me_ref[0]
-    rel = jnp.where(rel < 0, rel + peers, rel)
     slots = peers * block
     fits = rank < block - 1
-    dest = jnp.where(is_lead, slots + rank, jnp.where(fits, rel * block + rank, -1))
+    reach = peers // 2
+    shift = jnp.right_shift(target, 1) - me_ref[0] // 2
+    shift = jnp.where(shift < 0, shift + reach, shift)
+    place = jnp.where(jnp.bitwise_and(target, 1) == me_ref[0] % 2, shift, reach + shift)
+    dest = jnp.where(is_lead, slots + rank, jnp.where(fits, place * block + rank, -1))
     pitch = -(-block // LANES) * LANES
     final = jnp.where(is_lead, peers * pitch + rank, target * pitch + rank)
     row8 = lax.broadcasted_iota(jnp.int32, (8, count), 0)
@@ -90,7 +91,8 @@
 
 
 def pack_kernel(peers, block, unit_ref, info_ref, hdr_ref, *rest):
-    outs, pick = rest[:peers], rest[peers]
+    reach = peers // 2
+    straight, across, pick = rest[:reach], rest[reach], rest[reach + 1]
     count, width = unit_ref.shape
     dest = info_ref[0:1, :]
     at = lax.broadcasted_iota(jnp.int32, (peers * block, count), 0)
@@ -102,120 +104,198 @@
         acc = jnp.dot(pick[...], unit_ref[:, cols], preferred_element_type=jnp.float32)
         for k in range(peers):
             rows = acc[k * block : (k + 1) * block]
-            rows = jnp.where(is_hdr, hdr_ref[0:1, cols], rows)
-            outs[k][:, cols] = rows.astype(jnp.bfloat16)
-
-
-def leader_best_kernel(reach, cap, pos_ref, *rest):
-    queries, rest = rest[:4], rest[4:]
-    ups, rest = rest[: reach - 1], rest[reach - 1 :]
-    downs, rest = rest[: reach - 1], rest[reach - 1 :]
-    outs, (q, c, q_hdr, c_hdr, sem) = rest[:4], rest[4:]
-    pos = pos_ref[0]
-
-    def copies(src, index, rows, hdrs, which):
-        return [
-            pltpu.make_async_copy(src.at[pl.ds(0, cap), :], rows.at[pl.ds(index * cap, cap), :], sem.at[which]),
-            pltpu.make_async_copy(src.at[pl.ds(cap, SUB), :], hdrs.at[pl.ds(index * SUB, SUB), :], sem.at[which + 1]),
-        ]
-
-    started = []
-    for j in range(4):
-        started += copies(queries[j], j, q, q_hdr, 2 * j)
-    started += copies(queries[0], 0, c, c_hdr, 8)
-    for copy in started:
-        copy.start()
-    for k in range(1, reach):
-        up = copies(ups[k - 1], k, c, c_hdr, 8 + 2 * k)
-        down = copies(downs[reach - k - 1], k, c, c_hdr, 8 + 2 * k)
-
-        @pl.when(pos >= k)
-        def _():
-            for copy in up:
-                copy.start()
-
-        @pl.when(pos < k)
-        def _():
-            for copy in down:
-                copy.start()
-
-        started += up
-    for copy in started:
-        copy.wait()
-    c_ids = [c_hdr[k * SUB : (k + 1) * SUB, :cap].astype(jnp.float32)[0:1] for k in range(reach)]
-    c_col = as_column(jnp.concatenate(c_ids, axis=1))
-    for j in range(4):
-        q_id = q_hdr[j * SUB : (j + 1) * SUB, :cap].astype(jnp.float32)[0:1]
-        scores = lax.dot_general(c[...], q[j * cap : (j + 1) * cap, :], NT, preferred_element_type=jnp.float32)
-        same = c_col == q_id
-        if j == 0:
-            r = lax.broadcasted_iota(jnp.int32, (reach * cap, cap), 0)
-            l = lax.broadcasted_iota(jnp.int32, (reach * cap, cap), 1)
+            rows = jnp.where(is_hdr, hdr_ref[0:1, cols], rows).astype(jnp.bfloat16)
+            if k < reach:
+                straight[k][:, cols] = rows
+            else:
+                across[(k - reach) * block : (k - reach + 1) * block, cols] = rows
+
+
+def relay_kernel(peers, block, lead_rows, me_ref, own_up, own_down, across, lead, lead_up, lead_down, *outs):
+    reach = peers // 2
+    up, down, ends, queries, near = outs[:5]
+    far = outs[5:]
+    z = me_ref[0] // 2
+    up[:lead_rows, :] = lead_up[...]
+    up[lead_rows : lead_rows + block, :] = own_up[...]
+    up[lead_rows + block :, :] = across[block : 2 * block, :]
+    down[:lead_rows, :] = lead_down[...]
+    down[lead_rows : lead_rows + block, :] = own_down[...]
+    down[lead_rows + block :, :] = across[(reach - 1) * block :, :]
+    for s in range(2, reach - 1):
+        far[s - 2][...] = across[s * block : (s + 1) * block, :]
+    queries[:lead_rows, :] = lead[...]
+    for k, rows in enumerate((lead, lead_up, lead_down)):
+        near[k * lead_rows : (k + 1) * lead_rows, :] = rows[...]
+
+    def put(rows, straight, start):
+        ends[:block, :] = straight[...]
+        ends[block:, :] = across[start : start + block, :]
+
+    pl.when(z == reach - 1)(functools.partial(put, ends, own_up, block))
+    pl.when(z != reach - 1)(functools.partial(put, ends, own_down, (reach - 1) * block))
+
+    def keep(rows):
+        queries[lead_rows:, :] = rows[...]
+
+    pl.when(z < reach // 2)(functools.partial(keep, lead_up))
+    pl.when(z >= reach // 2)(functools.partial(keep, lead_down))
+
+
+def collect_kernel(peers, block, lead_rows, me_ref, mine, across, up, down, ends, *rest):
+    reach = peers // 2
+    far, far_across, own = rest[: reach - 3], rest[reach - 3 : 2 * reach - 6], rest[-1]
+    rest = rest[2 * reach - 6 : -1]
+    count = len(rest) // 2
+    z = me_ref[0] // 2
+    skip = lead_rows
+
+    def keep(slot, src):
+        at = peers * block + slot * lead_rows
+        own[at : at + lead_rows, :] = src[:lead_rows, :]
+
+    for slot in range(count):
+        k = slot + 2 if slot < reach - 3 else reach - 1
+        pl.when(z >= k)(functools.partial(keep, slot, rest[slot]))
+        pl.when(z < k)(functools.partial(keep, slot, rest[count + slot]))
+
+    def put(k, src, start=0):
+        own[k * block : (k + 1) * block, :] = src[start : start + block, :]
+
+    def put_two(k, src, start):
+        put(k, src, start)
+        put(reach + k, src, start + block)
+
+    put(0, mine)
+    put(reach, across)
+    for s in range(2, reach - 1):
+        put(s, far[s - 2])
+        put(reach + s, far_across[s - 2])
+    for slot, src, missing in ((1, up, 0), (reach - 1, down, reach - 1)):
+        pl.when(z == missing)(functools.partial(put_two, slot, ends, 0))
+        pl.when(z != missing)(functools.partial(put_two, slot, src, skip))
+
+
+def lead_ids(rows, start, cap):
+    return rows[start + cap : start + cap + SUB, :cap].astype(jnp.float32)[0:1]
+
+
+def lead_column(rows, start, count, cap):
+    gap = jnp.zeros((SUB, 1), jnp.float32)
+    parts = []
+    for k in range(count):
+        parts += [as_column(lead_ids(rows, start + k * (cap + SUB), cap)), gap]
+    return jnp.concatenate(parts, axis=0)
+
+
+def lead_tops(columns, column_ids, queries, start, cap, diagonal):
+    rows = queries[start : start + cap, :]
+    scores = lax.dot_general(columns, rows, NT, preferred_element_type=jnp.float32)
+    same = column_ids == lead_ids(queries, start, cap)
+    if diagonal:
+        r = lax.broadcasted_iota(jnp.int32, scores.shape, 0)
+        l = lax.broadcasted_iota(jnp.int32, scores.shape, 1)
+        same = same & (r != l)
+    return jnp.max(jnp.where(same, scores, -1.0), axis=0, keepdims=True)
+
+
+def lead_best_kernel(slots, cap, asked, asked_y, near, near_other, own, top):
+    lead_rows = cap + SUB
+    count = (own.shape[0] - slots) // lead_rows
+    near_ids, other_ids = lead_column(near, 0, 3, cap), lead_column(near_other, 0, 3, cap)
+    far_ids = lead_column(own, slots, count, cap)
+    top[...] = jnp.full(top.shape, -1.0, jnp.float32)
+    for i, queries in enumerate((asked, asked_y)):
+        best = lead_tops(near[...], near_ids, queries, 0, cap, i == 0)
+        best = jnp.maximum(best, lead_tops(near_other[...], other_ids, queries, 0, cap, False))
+        best = jnp.maximum(best, lead_tops(own[slots:, :], far_ids, queries, 0, cap, False))
+        top[i : i + 1, :] = best
+        top[2 + i : 3 + i, :] = lead_tops(own[slots:, :], far_ids, queries, lead_rows, cap, False)
+
+
+def ids_of(rows, peers, block):
+    width = rows.shape[1]
+    lane = lax.broadcasted_iota(jnp.int32, (1, width), 1)
+    total = jnp.zeros((1, width), jnp.float32)
+    for k in range(peers):
+        tail = rows[(k + 1) * block - SUB : (k + 1) * block, :].astype(jnp.float32)[SUB - 1 : SUB]
+        total = jnp.where((lane >= k * block) & (lane < (k + 1) * block), tail, total)
+    return total
+
+
+def tops_of(rows, ids, queries, q_ids, diagonal, tile):
+    slots = q_ids.shape[1]
+    column = as_column(ids)[:slots]
+    tops = []
+    for start in range(0, slots, tile):
+        stop = min(start + tile, slots)
+        scores = lax.dot_general(rows[:slots, :], queries[start:stop, :], NT, preferred_element_type=jnp.float32)
+        same = column == q_ids[:, start:stop]
+        if diagonal:
+            r = lax.broadcasted_iota(jnp.int32, scores.shape, 0)
+            l = lax.broadcasted_iota(jnp.int32, scores.shape, 1) + start
             same = same & (r != l)
-        outs[j][...] = jnp.max(jnp.where(same, scores, -1.0), axis=0, keepdims=True)
-
-
-def block_best_kernel(peers, block, me_ref, *rest):
-    mine, rest = rest[:peers], rest[peers:]
-    other, rest = rest[:peers], rest[peers:]
-    out, flag, (own, far, sem) = rest[0], rest[1], rest[2:]
+        tops.append(jnp.max(jnp.where(same, scores, -1.0), axis=0, keepdims=True))
+    return jnp.concatenate(tops, axis=1)
+
+
+def own_best_kernel(peers, block, own, top):
+    slots = peers * block
+    ids = ids_of(own, peers, block)
+    top[0:1, :] = tops_of(own, ids, own, ids[:, :slots], True, 256)
+    top[1:2, :] = ids[:, :slots]
+
+
+def far_best_kernel(peers, block, edges, me_ref, own, far, top, asked, asked_y, lead_top, out, flag):
     width = own.shape[1]
     slots = peers * block
-    started = []
-    for k in range(peers):
-        started.append(pltpu.make_async_copy(mine[k], own.at[pl.ds(k * block, block), :], sem.at[k]))
-        started.append(pltpu.make_async_copy(other[k], far.at[pl.ds(k * block, block), :], sem.at[peers + k]))
-    for copy in started:
-        copy.start()
-    for copy in started:
-        copy.wait()
-    lane = lax.broadcasted_iota(jnp.int32, (1, width), 1)
-
-    def ids_of(rows):
-        total = jnp.zeros((1, width), jnp.float32)
-        for k in range(peers):
-            tail = rows[(k + 1) * block - SUB : (k + 1) * block, :].astype(jnp.float32)[SUB - 1 : SUB]
-            inside = (lane >= k * block) & (lane < (k + 1) * block)
-            total = jnp.where(inside, tail, total)
-        return total
-
-    own_ids, far_ids = ids_of(own), ids_of(far)
+    own_ids, far_ids = top[1:2, :], ids_of(far, peers, block)
+    lane = lax.broadcasted_iota(jnp.int32, (1, slots), 1)
     is_code = functools.reduce(jnp.logical_or, [lane == k * block + block - 1 for k in range(peers)])
     my_code = own_ids[:, block - 1 : block]
-    odd = jnp.where(is_code & ((own_ids != my_code) | (far_ids != my_code)), 1.0, 0.0)
+    odd = jnp.where(is_code & ((own_ids != my_code) | (far_ids[:, :slots] != my_code)), 1.0, 0.0)
     half = jnp.floor(my_code * 0.5)
     odd = jnp.maximum(jnp.max(odd, axis=1, keepdims=True), my_code - 2.0 * half)
     flag[...] = jnp.broadcast_to(odd, flag.shape)
-
-    q_id = own_ids[:, :slots]
-    best = None
-    for rows, ids in ((own, own_ids), (far, far_ids)):
-        scores = lax.dot_general(rows[...], own[...], NT, preferred_element_type=jnp.float32)
-        same = as_column(ids)[:slots] == q_id
-        if rows is own:
-            r = lax.broadcasted_iota(jnp.int32, (slots, slots), 0)
-            l = lax.broadcasted_iota(jnp.int32, (slots, slots), 1)
-            same = same & (r != l)
-        top = jnp.max(jnp.where(same, scores, -1.0), axis=0, keepdims=True)
-        best = top if best is None else jnp.maximum(best, top)
+    best = jnp.maximum(top[0:1, :], tops_of(far, far_ids, own, own_ids, False, 256))
     best = jnp.broadcast_to(pad_lanes(best, width), (8, width))
-    pitch = out.shape[1]
+    reach = peers // 2
+    pitch = -(-block // LANES) * LANES
+    cap = out.shape[2] - pitch
+    z, y = me_ref[0] // 2, me_ref[0] % 2
+    none = jnp.full((1, cap), -1.0, jnp.float32)
     for k in range(peers):
         piece = best if k == 0 else pltpu.roll(best, width - k * block, 1)
-        to = me_ref[0] - k
-        to = jnp.where(to < 0, to + peers, to)
-        out[pl.ds(to, 1), :] = piece[0:1, :pitch]
-
-
-def final_kernel(peers, cap, info_ref, back_ref, *rest):
-    leads, out = rest[:-1], rest[-1]
+        row = z - k % reach
+        row = 2 * jnp.where(row < 0, row + reach, row) + (y if k < reach else 1 - y)
+        out[row, :, :pitch] = piece[0:1, :pitch]
+        out[k, :, pitch:] = none
+    count = (far.shape[0] - slots) // (cap + SUB)
+    ids = lead_column(far, slots, count, cap)
+    lead = []
+    for i, (queries, start) in enumerate(((asked, 0), (asked_y, 0), (asked, cap + SUB), (asked_y, cap + SUB))):
+        late = lead_tops(far[slots:, :], ids, queries, start, cap, False)
+        lead.append(jnp.maximum(lead_top[i : i + 1, :], late))
+    out[2 * z + y, :, pitch:] = lead[0]
+    out[2 * z + 1 - y, :, pitch:] = lead[1]
+    if edges:
+        for at, to in ((1, 0), (reach - 2, reach - 1)):
+
+            @pl.when(z == at)
+            def _():
+                out[2 * to + y, :, pitch:] = lead[2]
+                out[2 * to + 1 - y, :, pitch:] = lead[3]
+
+
+def final_kernel(peers, cap, info_ref, back_ref, out):
     count = info_ref.shape[1]
-    pitch = back_ref.shape[1]
+    pitch = back_ref.shape[2] - cap
     where = info_ref[1:2, :]
-    lead = functools.reduce(jnp.maximum, [ref[...] for ref in leads])
+    rows = [back_ref[h] for h in range(peers)]
+    lead = functools.reduce(jnp.maximum, [row[:, pitch:] for row in rows])
     total = jnp.zeros((1, count), jnp.float32)
     at = lax.broadcasted_iota(jnp.int32, (pitch, count), 0)
-    cols = jnp.transpose(jnp.concatenate([back_ref[...]] * (8 // math.gcd(peers, 8)), axis=0))
+    cols = jnp.transpose(jnp.concatenate([row[:, :pitch] for row in rows], axis=0))
     for h in range(peers):
         hit = at + h * pitch == where
         total += jnp.sum(jnp.where(hit, cols[:, h : h + 1], 0.0), axis=0, keepdims=True)
@@ -317,64 +397,92 @@
     down_pairs = dp_pairs(lambda z, y: (z - 1, y) if z > 0 else None)
     swap = [(0, 1), (1, 0)]
 
-    ups, downs = [], []
-    up, down = lead, lead
-    for _ in range(reach - 1):
-        up = lax.ppermute(up, "dp", up_pairs)
-        down = lax.ppermute(down, "dp", down_pairs)
-        ups.append(up)
-        downs.append(down)
-    blocks = call(
+    ends_pairs = dp_pairs(lambda z, y: (reach - 1 - z, y) if z in (0, reach - 1) else None)
+    shift_pairs = [dp_pairs(lambda z, y, s=s: ((z + s) % reach, y)) for s in range(2, reach - 1)]
+
+    one = shape((block, width), bf16)
+    two = shape((2 * block, width), bf16)
+    lead_rows = cap + SUB
+    message = shape((lead_rows + 2 * block, width), bf16)
+    edges = reach == 4
+
+    up1 = lax.ppermute(lead, "dp", up_pairs)
+    down1 = lax.ppermute(lead, "dp", down_pairs)
+    *straight, across = call(
         functools.partial(pack_kernel, peers, block),
         "pack",
-        [shape((block, width), bf16)] * peers,
+        [one] * reach + [shape((reach * block, width), bf16)],
         [VMEM] * 3,
-        [VMEM] * peers,
+        [VMEM] * (reach + 1),
         [pltpu.VMEM((slots, count), bf16)],
         flops=2 * slots * count * width,
         nbytes=4 * count * width,
     )(unit, info, hdr)
-    got = [blocks[0]]
-    for k in range(1, peers):
-        got.append(lax.ppermute(blocks[k], "dp", [(d, (d + k) % peers) for d in range(peers)]))
-    far = [lax.ppermute(rows, "owner", swap) for rows in got]
-
-    lead_y = lax.ppermute(lead, "dp", other_y)
-    lead_o = lax.ppermute(lead, "owner", swap)
-    lead_yo = lax.ppermute(lead_y, "owner", swap)
-    tops = call(
-        functools.partial(leader_best_kernel, reach, cap),
-        "leader_best",
-        [shape((1, cap), f32)] * 4,
-        [SMEM] + [ANY] * (4 + 2 * (reach - 1)),
-        [VMEM] * 4,
-        [
-            pltpu.VMEM((4 * cap, width), bf16),
-            pltpu.VMEM((reach * cap, width), bf16),
-            pltpu.VMEM((4 * SUB, width), bf16),
-            pltpu.VMEM((reach * SUB, width), bf16),
-            pltpu.SemaphoreType.DMA((8 + 2 * reach,)),
-        ],
-        flops=8 * cap * cap * reach * width,
-        nbytes=2 * (4 + reach) * cap * width,
-    )((me // 2).reshape(1), lead, lead_y, lead_o, lead_yo, *ups, *downs)
-    tops = [
-        tops[0],
-        lax.ppermute(tops[1], "dp", other_y),
-        lax.ppermute(tops[2], "owner", swap),
-        lax.ppermute(lax.ppermute(tops[3], "owner", swap), "dp", other_y),
-    ]
-
+    across = lax.ppermute(across, "dp", other_y)
+    fars = [lax.ppermute(straight[s + 2], "dp", pairs) for s, pairs in enumerate(shift_pairs)]
+    across, fars, up1, down1 = lax.optimization_barrier((across, fars, up1, down1))
+    up2, down2, ends, asked, near, *fars_r = call(
+        functools.partial(relay_kernel, peers, block, lead_rows),
+        "relay",
+        [message, message, two, shape((2 * lead_rows, width), bf16), shape((3 * lead_rows, width), bf16)] + [one] * (reach - 3),
+        [SMEM] + [VMEM] * 6,
+        [VMEM] * (2 + reach),
+        nbytes=2 * slots * width,
+    )(me1, straight[1], straight[reach - 1], across, lead, up1, down1)
+    up2 = lax.ppermute(up2, "dp", up_pairs)
+    down2 = lax.ppermute(down2, "dp", down_pairs)
+    ends = lax.ppermute(ends, "dp", ends_pairs)
+    fars_r = [lax.ppermute(rows, "dp", pairs) for rows, pairs in zip(fars_r, shift_pairs)]
+    asked_y = lax.ppermute(asked, "dp", other_y)
+    up2, down2, ends, fars_r, asked_y, near = lax.optimization_barrier((up2, down2, ends, fars_r, asked_y, near))
+    near_o = lax.ppermute(near, "owner", swap)
+    ups, downs = [up2], [down2]
+    if not edges:
+        up, down = up2[:lead_rows], down2[:lead_rows]
+        for _ in range(reach - 3):
+            up = lax.ppermute(up, "dp", up_pairs)
+            down = lax.ppermute(down, "dp", down_pairs)
+            ups.append(up)
+            downs.append(down)
+        ups, downs = ups[:-1] + ups[-1:], downs[:-1][::-1] + downs[-1:]
+
+    n_late = len(ups)
+    own = call(
+        functools.partial(collect_kernel, peers, block, lead_rows),
+        "collect",
+        shape((slots + n_late * lead_rows, width), bf16),
+        [SMEM] + [VMEM] * (5 + 2 * (reach - 3) + 2 * n_late),
+        VMEM,
+        nbytes=4 * slots * width,
+    )(me1, straight[0], across, up2, down2, ends, *fars, *fars_r, *ups, *downs)
+    far = lax.ppermute(own, "owner", swap)
+    lead_top = call(
+        functools.partial(lead_best_kernel, slots, cap),
+        "lead_best",
+        shape((8, cap), f32),
+        [VMEM] * 5,
+        VMEM,
+        flops=4 * (6 + 2 * n_late) * cap * cap * width,
+        nbytes=2 * (10 + n_late) * cap * width,
+    )(asked, asked_y, near, near_o, own)
+    top = call(
+        functools.partial(own_best_kernel, peers, block),
+        "own_best",
+        shape((8, slots), f32),
+        [VMEM],
+        VMEM,
+        flops=2 * slots * slots * width,
+        nbytes=2 * slots * width,
+    )(own)
     best, flag = call(
-        functools.partial(block_best_kernel, peers, block),
-        "block_best",
-        [shape((peers, pitch), f32), shape((8, LANES), f32)],
-        [SMEM] + [ANY] * (2 * peers),
+        functools.partial(far_best_kernel, peers, block, edges),
+        "far_best",
+        [shape((peers, 1, pitch + cap), f32), shape((8, LANES), f32)],
+        [SMEM] + [VMEM] * 6,
         [VMEM] * 2,
-        [pltpu.VMEM((slots, width), bf16), pltpu.VMEM((slots, width), bf16), pltpu.SemaphoreType.DMA((2 * peers,))],
-        flops=4 * slots * slots * width,
+        flops=2 * slots * slots * width + 8 * n_late * cap * cap * width,
         nbytes=4 * slots * width,
-    )(me1, *got, *far)
+    )(me1, own, far, top, asked, asked_y, lead_top)
     back = lax.all_to_all(best, "dp", split_axis=0, concat_axis=0, tiled=True)
     flags = [flag]
     for k in range(1, groups):
@@ -384,11 +492,11 @@
         functools.partial(final_kernel, peers, cap),
         "final",
         shape((1, count), f32),
-        [VMEM] * 6,
+        [VMEM] * 2,
         VMEM,
         flops=0,
         nbytes=4 * count,
-    )(info, back, *tops).reshape(count)
+    )(info, back).reshape(count)
     return lax.cond(odd > 0, whole_exchange, lambda e, c: nearest, embeddings, cluster_ids)
 
 

time: 135 us -> 111 us (0.82)
  waiting for transfers between devices: 16.9 us -> 62.9 us
  starting transfers between devices: 71.5 us -> 30 us
  local copies, waits for them, and re-layouts: 24 us -> 1.11 us
  Pallas kernels: 21.2 us -> 15.6 us
    ppermute x28 -> x11, waiting for transfers between devices: 16.9 us -> 59.2 us  [the longest x1 36.5 us: local(): lax.ppermute(rows, 'dp', pairs)]
    ppermute x28 -> x11, starting transfers between devices: 63.2 us -> 25.1 us  [the longest x1 7.37 us: local(): ends = lax.ppermute(ends, 'dp', ends_pairs)]
    unnamed x60 -> x4, local copies, waits for them, and re-layouts: 23.5 us -> 0.59 us
    pallas_call x3 -> x6, Pallas kernels: 16.3 us -> 10.7 us  [the longest x1 3.37 us: local(): call(functools.partial(far_best_kernel, peers, block, edges), 'far_best',...]
    all_to_all x1, starting transfers between devices: 6.76 us -> 3.29 us  [local(): back = lax.all_to_all(best, 'dp', split_axis=0, concat_axis=0, tiled=True)]
    ppermute x1, waiting for transfers between devices: 0.01 us -> 2.12 us  [local(): lax.ppermute(flag, 'groups', [(g, (g + k) % groups) for g in range(groups)])]
    all_to_all x1, waiting for transfers between devices: 0.01 us -> 1.64 us  [local(): back = lax.all_to_all(best, 'dp', split_axis=0, concat_axis=0, tiled=True)]
  transfers between devices with their start and end apart: 30 -> 13, of which waited for: 7 -> 5; matrix products, arithmetic and copies ran while one was open for 0% -> 0% of each run, Pallas kernels for 11% -> 4%
where the time goes in v2:
time: 111 us
  waiting for transfers between devices  62.9 us (57%)
  starting transfers between devices  30 us (27%)
  Pallas kernels  15.6 us (14%)
  local copies, waits for them, and re-layouts  1.11 us (1%)
    ppermute x1, waiting for transfers between devices, local(): lax.ppermute(rows, 'dp', pairs)  36.5 us
    ppermute x1, waiting for transfers between devices, local(): lax.ppermute(straight[s + 2], 'dp', pairs)  18.3 us
    ppermute x1, starting transfers between devices, local(): ends = lax.ppermute(ends, 'dp', ends_pairs)  7.37 us
    ppermute x1, starting transfers between devices, local(): up1 = lax.ppermute(lead, 'dp', up_pairs)  4.58 us
    ppermute x1, waiting for transfers between devices, local(): near_o = lax.ppermute(near, 'owner', swap)  4.33 us
    pallas_call x1, Pallas kernels, local(): call(functools.partial(lead_kernel, peers, cap, block), 'lead', [shape((c...  4.08 us
    ppermute x1, starting transfers between devices, local(): up2 = lax.ppermute(up2, 'dp', up_pairs)  3.7 us
    pallas_call x1, Pallas kernels, local(): call(functools.partial(far_best_kernel, peers, block, edges), 'far_best',...  3.37 us
  transfers between devices with their start and end apart: 13, of which 5 were waited for; matrix products, arithmetic and copies ran while one was open for 0% of the time, Pallas kernels for 4%

profile of v2, /device:TPU:0, one launch (start us, length us, event | category | flops | bytes accessed | tf_op | source)
XLA Modules:
  0.0 110.7 jit_solution(9509191569396530277)
XLA Ops:
  0.0 4.1 %lead.1 = (bf16[1024,1024]{1,0:T(8,128)(2,1)S(1)}, s32[8,1024]{1,0:T(8,128)S(1)}, f32[8,1024]{1,0:T(8,128)S(1)}, bf16[272,1024]{1,0:T(8,128)(2,1)S(1)}) custom-call(s32[1]{0:T(128)} %bitcast.8.me_ref, s32[1,1024]{1,0:T(1,128)} %bitcast.45, f32[1024,1024]{1,0:T(8,128)} %emb_ref.1), custom_call_target="tpu_custom_call" | custom-call | flops 536870912 | bytes 6291456 | tf_op jit(solution)/shard_map/lead/pallas_call | solution.py:376
  4.1 2.1 %pack.1 = (bf16[112,1024]{1,0:T(8,128)(2,1)S(1)}, bf16[112,1024]{1,0:T(8,128)(2,1)S(1)}, bf16[112,1024]{1,0:T(8,128)(2,1)S(1)}, bf16[112,1024]{1,0:T(8,128)(2,1)S(1)}, bf16[448,1024]{1,0:T(8,128)(2,1)S(1)}) custom-call(bf16[1024,1024]{1,0:T(8,128)(2,1)S(1)} %get-tuple-element.86.unit_ref, s32[8,1024]{1,0:T(8,128)S(1)} %get-tuple-element.87.info_ref, ...), custom_call_target="tpu_custom_call" | custom-call | flops 1879048192 | bytes 4194304 | tf_op jit(solution)/shard_map/pack/pallas_call | solution.py:411
  6.1 3.0 %collective-permute-start.2 = (bf16[448,1024]{1,0:T(8,128)(2,1)S(1)}, bf16[448,1024]{1,0:T(8,128)(2,1)S(1)}, u32[]{:S(2)}, u32[]{:S(2)}) collective-permute-start(bf16[448,1024]{1,0:T(8,128)(2,1)S(1)} %get-tuple-element.90), channel_id=1, source_target_pairs={{0,2},{2,0},{4,6},{6,4},{8,10},{10,8},{12,14},{14,12},{1,3},{3,1},... | collective-permute-start | bytes 2752520 | tf_op jit(solution)/shard_map/ppermute | solution.py:421
  9.2 1.3 %collective-permute-start.5 = (bf16[272,1024]{1,0:T(8,128)(2,1)S(1)}, bf16[272,1024]{1,0:T(8,128)(2,1)S(1)}, u32[]{:S(2)}, u32[]{:S(2)}) collective-permute-start(bf16[272,1024]{1,0:T(8,128)(2,1)S(1)} %get-tuple-element.92.lead), channel_id=1, source_target_pairs={{4,0},{6,2},{8,4},{10,6},{12,8},{14,10},{5,1},{7,3},{9,5},{11,7},{... | collective-permute-start | bytes 1671176 | tf_op jit(solution)/shard_map/ppermute | solution.py:410
  10.5 4.6 %collective-permute-start.4 = (bf16[272,1024]{1,0:T(8,128)(2,1)S(1)}, bf16[272,1024]{1,0:T(8,128)(2,1)S(1)}, u32[]{:S(2)}, u32[]{:S(2)}) collective-permute-start(bf16[272,1024]{1,0:T(8,128)(2,1)S(1)} %get-tuple-element.92.lead), channel_id=1, source_target_pairs={{0,4},{2,6},{4,8},{6,10},{8,12},{10,14},{1,5},{3,7},{5,9},{7,11},{... | collective-permute-start | bytes 1671176 | tf_op jit(solution)/shard_map/ppermute | solution.py:409
  15.1 2.7 %collective-permute-start.3 = (bf16[112,1024]{1,0:T(8,128)(2,1)S(1)}, bf16[112,1024]{1,0:T(8,128)(2,1)S(1)}, u32[]{:S(2)}, u32[]{:S(2)}) collective-permute-start(bf16[112,1024]{1,0:T(8,128)(2,1)S(1)} %get-tuple-element.91), channel_id=1, source_target_pairs={{0,8},{2,10},{4,12},{6,14},{8,0},{10,2},{12,4},{14,6},{1,9},{3,11}... | collective-permute-start | bytes 688136 | tf_op jit(solution)/shard_map/ppermute | solution.py:422
  17.7 18.3 %collective-permute-done.3.rest_0_ = bf16[112,1024]{1,0:T(8,128)(2,1)S(1)} collective-permute-done((bf16[112,1024]{1,0:T(8,128)(2,1)S(1)}, bf16[112,1024]{1,0:T(8,128)(2,1)S(1)}, u32[]{:S(2)}, u32[]{:S(2)}) %collective-permute-start.3) | collective-permute-done | bytes 229408 | tf_op jit(solution)/shard_map/ppermute | solution.py:422
  36.0 0.0 collective-permute-done.5.lead_down
  36.0 0.4 relay.1
  36.4 0.6 collective-permute-start.10
  37.0 3.7 %collective-permute-start.6 = (bf16[496,1024]{1,0:T(8,128)(2,1)S(1)}, bf16[496,1024]{1,0:T(8,128)(2,1)S(1)}, u32[]{:S(2)}, u32[]{:S(2)}) collective-permute-start(bf16[496,1024]{1,0:T(8,128)(2,1)S(1)} %get-tuple-element.98), channel_id=1, source_target_pairs={{0,4},{2,6},{4,8},{6,10},{8,12},{10,14},{1,5},{3,7},{5,9},{7,11},{... | collective-permute-start | bytes 3047432 | tf_op jit(solution)/shard_map/ppermute | solution.py:432
  40.7 1.3 %collective-permute-start.7 = (bf16[496,1024]{1,0:T(8,128)(2,1)S(1)}, bf16[496,1024]{1,0:T(8,128)(2,1)S(1)}, u32[]{:S(2)}, u32[]{:S(2)}) collective-permute-start(bf16[496,1024]{1,0:T(8,128)(2,1)S(1)} %get-tuple-element.99), channel_id=1, source_target_pairs={{4,0},{6,2},{8,4},{10,6},{12,8},{14,10},{5,1},{7,3},{9,5},{11,7},{... | collective-permute-start | bytes 3047432 | tf_op jit(solution)/shard_map/ppermute | solution.py:433
  42.0 7.4 %collective-permute-start.8 = (bf16[224,1024]{1,0:T(8,128)(2,1)S(1)}, bf16[224,1024]{1,0:T(8,128)(2,1)S(1)}, u32[]{:S(2)}, u32[]{:S(2)}) collective-permute-start(bf16[224,1024]{1,0:T(8,128)(2,1)S(1)} %get-tuple-element.100), channel_id=1, source_target_pairs={{0,12},{2,14},{12,0},{14,2},{1,13},{3,15},{13,1},{15,3},{16,28},{1... | collective-permute-start | bytes 1376264 | tf_op jit(solution)/shard_map/ppermute | solution.py:434
  49.3 0.1 collective-permute-start.9
  49.4 36.5 %collective-permute-done.9.rest_1_ = bf16[112,1024]{1,0:T(8,128)(2,1)S(1)} collective-permute-done((bf16[112,1024]{1,0:T(8,128)(2,1)S(1)}, bf16[112,1024]{1,0:T(8,128)(2,1)S(1)}, u32[]{:S(2)}, u32[]{:S(2)}) %collective-permute-start.9) | collective-permute-done | bytes 229408 | tf_op jit(solution)/shard_map/ppermute | solution.py:435
  86.0 0.2 collect.1.own
  86.2 0.1 collective-permute-start.11
  86.3 0.5 collective-permute-start.12
  86.8 2.1 %own_best.1.top = f32[8,896]{1,0:T(8,128)S(1)} custom-call(bf16[1168,1024]{1,0:T(8,128)(2,1)S(1)} %collect.1.own), custom_call_target="tpu_custom_call" | custom-call | flops 1644167168 | bytes 1835008 | tf_op jit(solution)/shard_map/own_best/pallas_call | solution.py:468
  88.9 4.3 %collective-permute-done.12.near_other = bf16[816,1024]{1,0:T(8,128)(2,1)S(1)} collective-permute-done((bf16[816,1024]{1,0:T(8,128)(2,1)S(1)}, bf16[816,1024]{1,0:T(8,128)(2,1)S(1)}, u32[]{:S(2)}, u32[]{:S(2)}) %collective-permute-start.12) | collective-permute-done | bytes 1671200 | tf_op jit(solution)/shard_map/ppermute | solution.py:438
  93.2 2.6 %lead_best.1.lead_top = f32[8,256]{1,0:T(8,128)S(1)} custom-call(bf16[544,1024]{1,0:T(8,128)(2,1)S(1)} %get-tuple-element.102.asked, bf16[544,1024]{1,0:T(8,128)(2,1)S(1)} %collective-permute-done.10.asked_y, bf16[816,1024]{1,0:T(8,128)(2,1)S(1)} %get-tuple-element.110.near, bf16[816,1024]{1,0:T(8,128)(2,1)S(1)} %collective-permute-done.12.near_other, ...), custom_call_target="tpu_custom_call" | custom-call | flops 2147483648 | bytes 5767168 | tf_op jit(solution)/shard_map/lead_best/pallas_call | solution.py:459
  95.8 0.0 copy-start
  95.8 3.4 %far_best.1 = (f32[8,1,384]{2,1,0:T(1,128)}, f32[8,128]{1,0:T(8,128)S(1)}) custom-call(s32[1]{0:T(128)} %bitcast.8.me_ref, bf16[1168,1024]{1,0:T(8,128)(2,1)S(1)} %collect.1.own, bf16[1168,1024]{1,0:T(8,128)(2,1)S(1)} %collective-permute-done.11.far, f32[8,896]{1,0:T(8,128)S(1)} %own_best.1.top, bf16[544,1024]{1,0:T(8,128)(2,1)S(1)} %get-tuple-element.102.asked, ...), custom_call_target="tpu_custom_call" | custom-call | flops 2181038080 | bytes 3670016 | tf_op jit(solution)/shard_map/far_best/pallas_call | solution.py:477
  99.2 3.3 %all-to-all-start.3 = ((f32[8,1,384]{2,1,0:T(1,128)}), f32[8,1,384]{2,1,0:T(1,128)S(1)}, u32[]{:S(2)}, u32[]{:S(2)}) async-start(f32[8,1,384]{2,1,0:T(1,128)} %get-tuple-element.112), calls=%async_computation.3 | async-start | bytes 24576 | tf_op jit(solution)/shard_map/all_to_all | solution.py:486
  102.5 1.6 %collective-permute-start.13 = (f32[8,128]{1,0:T(8,128)S(1)}, f32[8,128]{1,0:T(8,128)S(1)}, u32[]{:S(2)}, u32[]{:S(2)}) collective-permute-start(f32[8,128]{1,0:T(8,128)S(1)} %get-tuple-element.111), channel_id=1, source_target_pairs={{0,16},{16,0},{1,17},{17,1},{2,18},{18,2},{3,19},{19,3},{4,20},{20... | collective-permute-start | bytes 12296 | tf_op jit(solution)/shard_map/ppermute | solution.py:489
  104.0 2.1 %collective-permute-done.13 = f32[8,128]{1,0:T(8,128)S(1)} collective-permute-done((f32[8,128]{1,0:T(8,128)S(1)}, f32[8,128]{1,0:T(8,128)S(1)}, u32[]{:S(2)}, u32[]{:S(2)}) %collective-permute-start.13) | collective-permute-done | bytes 4128 | tf_op jit(solution)/shard_map/ppermute | solution.py:489
  106.1 0.5 slice.9
  107.3 1.6 %all-to-all-done.3.back_ref = f32[8,1,384]{2,1,0:T(1,128)S(1)} async-done(((f32[8,1,384]{2,1,0:T(1,128)}), f32[8,1,384]{2,1,0:T(1,128)S(1)}, u32[]{:S(2)}, u32[]{:S(2)}) %all-to-all-start.3) | async-done | bytes 12320 | tf_op jit(solution)/shard_map/all_to_all | solution.py:486
  109.0 0.9 final.1
  109.8 0.2 conditional.1
  110.1 0.0 copy-start.1
  110.1 0.6 copy-done.1
  (9 shorter events, 0.0 us)
Async XLA Ops:
  6.1 29.9 %collective-permute-start.2 = (bf16[448,1024]{1,0:T(8,128)(2,1)S(1)}, bf16[448,1024]{1,0:T(8,128)(2,1)S(1)}, u32[]{:S(2)}, u32[]{:S(2)}) collective-permute-start(bf16[448,1024]{1,0:T(8,128)(2,1)S(1)} %get-tuple-element.90), channel_id=1, source_target_pairs={{0,2},{2,0},{4,6},{6,4},{8,10},{10,8},{12,14},{14,12},{1,3},{3,1},... | collective-permute-start | bytes 2752520 | tf_op jit(solution)/shard_map/ppermute | solution.py:421
  9.2 26.8 %collective-permute-start.5 = (bf16[272,1024]{1,0:T(8,128)(2,1)S(1)}, bf16[272,1024]{1,0:T(8,128)(2,1)S(1)}, u32[]{:S(2)}, u32[]{:S(2)}) collective-permute-start(bf16[272,1024]{1,0:T(8,128)(2,1)S(1)} %get-tuple-element.92.lead), channel_id=1, source_target_pairs={{4,0},{6,2},{8,4},{10,6},{12,8},{14,10},{5,1},{7,3},{9,5},{11,7},{... | collective-permute-start | bytes 1671176 | tf_op jit(solution)/shard_map/ppermute | solution.py:410
  10.5 25.5 %collective-permute-start.4 = (bf16[272,1024]{1,0:T(8,128)(2,1)S(1)}, bf16[272,1024]{1,0:T(8,128)(2,1)S(1)}, u32[]{:S(2)}, u32[]{:S(2)}) collective-permute-start(bf16[272,1024]{1,0:T(8,128)(2,1)S(1)} %get-tuple-element.92.lead), channel_id=1, source_target_pairs={{0,4},{2,6},{4,8},{6,10},{8,12},{10,14},{1,5},{3,7},{5,9},{7,11},{... | collective-permute-start | bytes 1671176 | tf_op jit(solution)/shard_map/ppermute | solution.py:409
  15.1 20.9 %collective-permute-start.3 = (bf16[112,1024]{1,0:T(8,128)(2,1)S(1)}, bf16[112,1024]{1,0:T(8,128)(2,1)S(1)}, u32[]{:S(2)}, u32[]{:S(2)}) collective-permute-start(bf16[112,1024]{1,0:T(8,128)(2,1)S(1)} %get-tuple-element.91), channel_id=1, source_target_pairs={{0,8},{2,10},{4,12},{6,14},{8,0},{10,2},{12,4},{14,6},{1,9},{3,11}... | collective-permute-start | bytes 688136 | tf_op jit(solution)/shard_map/ppermute | solution.py:422
  36.4 49.6 %collective-permute-start.10 = (bf16[544,1024]{1,0:T(8,128)(2,1)S(1)}, bf16[544,1024]{1,0:T(8,128)(2,1)S(1)}, u32[]{:S(2)}, u32[]{:S(2)}) collective-permute-start(bf16[544,1024]{1,0:T(8,128)(2,1)S(1)} %get-tuple-element.102.asked), channel_id=1, source_target_pairs={{0,2},{2,0},{4,6},{6,4},{8,10},{10,8},{12,14},{14,12},{1,3},{3,1},... | collective-permute-start | bytes 3342344 | tf_op jit(solution)/shard_map/ppermute | solution.py:436
  37.0 49.0 %collective-permute-start.6 = (bf16[496,1024]{1,0:T(8,128)(2,1)S(1)}, bf16[496,1024]{1,0:T(8,128)(2,1)S(1)}, u32[]{:S(2)}, u32[]{:S(2)}) collective-permute-start(bf16[496,1024]{1,0:T(8,128)(2,1)S(1)} %get-tuple-element.98), channel_id=1, source_target_pairs={{0,4},{2,6},{4,8},{6,10},{8,12},{10,14},{1,5},{3,7},{5,9},{7,11},{... | collective-permute-start | bytes 3047432 | tf_op jit(solution)/shard_map/ppermute | solution.py:432
  40.7 45.3 %collective-permute-start.7 = (bf16[496,1024]{1,0:T(8,128)(2,1)S(1)}, bf16[496,1024]{1,0:T(8,128)(2,1)S(1)}, u32[]{:S(2)}, u32[]{:S(2)}) collective-permute-start(bf16[496,1024]{1,0:T(8,128)(2,1)S(1)} %get-tuple-element.99), channel_id=1, source_target_pairs={{4,0},{6,2},{8,4},{10,6},{12,8},{14,10},{5,1},{7,3},{9,5},{11,7},{... | collective-permute-start | bytes 3047432 | tf_op jit(solution)/shard_map/ppermute | solution.py:433
  42.0 44.0 %collective-permute-start.8 = (bf16[224,1024]{1,0:T(8,128)(2,1)S(1)}, bf16[224,1024]{1,0:T(8,128)(2,1)S(1)}, u32[]{:S(2)}, u32[]{:S(2)}) collective-permute-start(bf16[224,1024]{1,0:T(8,128)(2,1)S(1)} %get-tuple-element.100), channel_id=1, source_target_pairs={{0,12},{2,14},{12,0},{14,2},{1,13},{3,15},{13,1},{15,3},{16,28},{1... | collective-permute-start | bytes 1376264 | tf_op jit(solution)/shard_map/ppermute | solution.py:434
  49.3 36.6 %collective-permute-start.9 = (bf16[112,1024]{1,0:T(8,128)(2,1)S(1)}, bf16[112,1024]{1,0:T(8,128)(2,1)S(1)}, u32[]{:S(2)}, u32[]{:S(2)}) collective-permute-start(bf16[112,1024]{1,0:T(8,128)(2,1)S(1)} %get-tuple-element.101), channel_id=1, source_target_pairs={{0,8},{2,10},{4,12},{6,14},{8,0},{10,2},{12,4},{14,6},{1,9},{3,11}... | collective-permute-start | bytes 688136 | tf_op jit(solution)/shard_map/ppermute | solution.py:435
  86.2 9.6 %collective-permute-start.11 = (bf16[1168,1024]{1,0:T(8,128)(2,1)S(1)}, bf16[1168,1024]{1,0:T(8,128)(2,1)S(1)}, u32[]{:S(2)}, u32[]{:S(2)}) collective-permute-start(bf16[1168,1024]{1,0:T(8,128)(2,1)S(1)} %collect.1.own), channel_id=1, source_target_pairs={{0,1},{1,0},{2,3},{3,2},{4,5},{5,4},{6,7},{7,6},{8,9},{9,8},{10,11... | collective-permute-start | bytes 7176200 | tf_op jit(solution)/shard_map/ppermute | solution.py:458
  86.3 7.0 %collective-permute-start.12 = (bf16[816,1024]{1,0:T(8,128)(2,1)S(1)}, bf16[816,1024]{1,0:T(8,128)(2,1)S(1)}, u32[]{:S(2)}, u32[]{:S(2)}) collective-permute-start(bf16[816,1024]{1,0:T(8,128)(2,1)S(1)} %get-tuple-element.110.near), channel_id=1, source_target_pairs={{0,1},{1,0},{2,3},{3,2},{4,5},{5,4},{6,7},{7,6},{8,9},{9,8},{10,11... | collective-permute-start | bytes 5013512 | tf_op jit(solution)/shard_map/ppermute | solution.py:438
  95.8 14.0 %copy-start = (s32[1024]{0:T(1024)S(1)}, s32[1024]{0:T(1024)}, u32[]{:S(2)}) copy-start(s32[1024]{0:T(1024)} %param.7) | copy-start | bytes 12292
  99.2 9.8 %all-to-all-start.3 = ((f32[8,1,384]{2,1,0:T(1,128)}), f32[8,1,384]{2,1,0:T(1,128)S(1)}, u32[]{:S(2)}, u32[]{:S(2)}) async-start(f32[8,1,384]{2,1,0:T(1,128)} %get-tuple-element.112), calls=%async_computation.3 | async-start | bytes 24576 | tf_op jit(solution)/shard_map/all_to_all | solution.py:486
  102.5 3.7 %collective-permute-start.13 = (f32[8,128]{1,0:T(8,128)S(1)}, f32[8,128]{1,0:T(8,128)S(1)}, u32[]{:S(2)}, u32[]{:S(2)}) collective-permute-start(f32[8,128]{1,0:T(8,128)S(1)} %get-tuple-element.111), channel_id=1, source_target_pairs={{0,16},{16,0},{1,17},{17,1},{2,18},{18,2},{3,19},{19,3},{4,20},{20... | collective-permute-start | bytes 12296 | tf_op jit(solution)/shard_map/ppermute | solution.py:489
  110.1 0.6 copy-start.1

commit v3 on v2

--- a/solution.py
+++ b/solution.py
@@ -10,8 +10,9 @@
 
 CL_DEV = 8
 LANES = 128
+CHUNKS = 4
 SUB = 16
-VMEM_LIMIT = 24 * 1024 * 1024
+VMEM_LIMIT = 14 * 1024 * 1024
 VMEM = pl.BlockSpec(memory_space=pltpu.VMEM)
 SMEM = pl.BlockSpec(memory_space=pltpu.SMEM)
 NT = (((1,), (1,)), ((), ()))
@@ -32,8 +33,15 @@
     return 16 + 2 * leader + bad
 
 
-def lead_kernel(peers, cap, block, me_ref, ids_ref, emb_ref, unit_ref, info_ref, hdr_ref, lead_ref):
+def pack_kernel(peers, cap, block, me_ref, ids_ref, emb_hbm, info_ref, mine, mine_across, lead, near, odd, across, *rest):
+    far, (emb_ref, unit_ref, pick, sem) = rest[:-4], rest[-4:]
     count, width = emb_ref.shape
+    chunk = count // CHUNKS
+    copies = []
+    for i in range(CHUNKS):
+        rows = pl.ds(i * chunk, chunk)
+        copies.append(pltpu.make_async_copy(emb_hbm.at[rows, :], emb_ref.at[rows, :], sem.at[i]))
+        copies[-1].start()
     ids = ids_ref[...]
     target = jnp.right_shift(ids, int(math.log2(CL_DEV)))
     local_id = jnp.bitwise_and(ids, CL_DEV - 1)
@@ -55,7 +63,9 @@
     slots = peers * block
     fits = rank < block - 1
     reach = peers // 2
-    shift = jnp.right_shift(target, 1) - me_ref[0] // 2
+    z = me_ref[0] // 2
+    shift = jnp.right_shift(target, 1) - z
+    shift = jnp.where(z % 2 == 0, shift, -shift)
     shift = jnp.where(shift < 0, shift + reach, shift)
     place = jnp.where(jnp.bitwise_and(target, 1) == me_ref[0] % 2, shift, reach + shift)
     dest = jnp.where(is_lead, slots + rank, jnp.where(fits, place * block + rank, -1))
@@ -77,103 +87,88 @@
     last = functools.reduce(jnp.logical_or, [slot_lane == k * block + block - 1 for k in range(peers)])
     code = code_of(leader, bad).astype(jnp.float32)
     block_ids = jnp.where(last, code, block_ids)
-    hdr_ref[...] = jnp.broadcast_to(pad_lanes(block_ids, width), (8, width))
-
-    emb = emb_ref[...]
-    squares = jnp.sum(emb * emb, axis=1, keepdims=True)
-    unit = (emb * lax.rsqrt(squares + 1e-06)).astype(jnp.bfloat16)
-    unit_ref[...] = unit
-    at = lax.broadcasted_iota(jnp.int32, (cap, count), 0) + slots
-    pick = jnp.where(at == dest, 1.0, 0.0).astype(jnp.bfloat16)
-    lead_ref[:cap, :] = jnp.dot(pick, unit, preferred_element_type=jnp.float32).astype(jnp.bfloat16)
-    lead_hdr = pad_lanes(ids_at[:, slots:], width)
-    lead_ref[cap:, :] = jnp.broadcast_to(lead_hdr, (SUB, width)).astype(jnp.bfloat16)
-
-
-def pack_kernel(peers, block, unit_ref, info_ref, hdr_ref, *rest):
-    reach = peers // 2
-    straight, across, pick = rest[:reach], rest[reach], rest[reach + 1]
-    count, width = unit_ref.shape
-    dest = info_ref[0:1, :]
-    at = lax.broadcasted_iota(jnp.int32, (peers * block, count), 0)
+    hdr = pad_lanes(block_ids, width)
+    lead_hdr = jnp.broadcast_to(pad_lanes(ids_at[:, slots:], width), (SUB, width)).astype(jnp.bfloat16)
+    lead[cap:, :] = lead_hdr
+    odd[cap : cap + SUB, :] = lead_hdr
+    at = lax.broadcasted_iota(jnp.int32, (slots + cap, count), 0)
     pick[...] = jnp.where(at == dest, 1.0, 0.0).astype(jnp.bfloat16)
+
+    for i in range(CHUNKS):
+        copies[i].wait()
+        rows = slice(i * chunk, (i + 1) * chunk)
+        emb = emb_ref[rows, :]
+        squares = jnp.sum(emb * emb, axis=1, keepdims=True)
+        unit_ref[rows, :] = (emb * lax.rsqrt(squares + 1e-06)).astype(jnp.bfloat16)
+
+    places = [(mine, 0), (near, 0), *[(ref, 0) for ref in far], (odd, cap + SUB), (mine_across, 0)]
+    places += [(across, s * block) for s in range(reach - 1)]
     is_hdr = lax.broadcasted_iota(jnp.int32, (block, 1), 0) == block - 1
     tile = 256
     for start in range(0, width, tile):
         cols = slice(start, start + tile)
         acc = jnp.dot(pick[...], unit_ref[:, cols], preferred_element_type=jnp.float32)
-        for k in range(peers):
+        for k, (ref, at) in enumerate(places):
             rows = acc[k * block : (k + 1) * block]
-            rows = jnp.where(is_hdr, hdr_ref[0:1, cols], rows).astype(jnp.bfloat16)
-            if k < reach:
-                straight[k][:, cols] = rows
-            else:
-                across[(k - reach) * block : (k - reach + 1) * block, cols] = rows
-
-
-def relay_kernel(peers, block, lead_rows, me_ref, own_up, own_down, across, lead, lead_up, lead_down, *outs):
+            ref[at : at + block, cols] = jnp.where(is_hdr, hdr[:, cols], rows).astype(jnp.bfloat16)
+        lead[:cap, cols] = acc[slots:].astype(jnp.bfloat16)
+        odd[:cap, cols] = acc[slots:].astype(jnp.bfloat16)
+
+
+def relay_kernel(peers, block, lead_rows, lead, near, odd, mine_across, across, lead_even, lead_odd, *outs):
     reach = peers // 2
-    up, down, ends, queries, near = outs[:5]
-    far = outs[5:]
+    even_out, odd_out, ends, queries = outs[:4]
+    far = outs[4:]
+    last = (reach - 2) * block
+    even_out[:lead_rows, :] = lead_odd[:lead_rows, :]
+    even_out[lead_rows : lead_rows + block, :] = near[...]
+    even_out[lead_rows + block :, :] = across[:block, :]
+    odd_out[:lead_rows, :] = lead_even[...]
+    odd_out[lead_rows:, :] = across[last:, :]
+    ends[:block, :] = odd[lead_rows:, :]
+    ends[block:, :] = across[last:, :]
+    for s in range(2, reach - 1):
+        far[s - 2][...] = across[(s - 1) * block : s * block, :]
+    queries[:lead_rows, :] = lead[...]
+    queries[lead_rows : 2 * lead_rows, :] = lead_even[...]
+    queries[2 * lead_rows :, :] = mine_across[...]
+
+
+def collect_kernel(peers, block, lead_rows, me_ref, mine, odd, asked_y, even2, odd2, ends, lead, lead_even, *rest):
+    reach = peers // 2
+    far, far_across, (own, cols) = rest[: reach - 3], rest[reach - 3 : 2 * reach - 6], rest[-2:]
+    rest = rest[2 * reach - 6 : -2]
     z = me_ref[0] // 2
-    up[:lead_rows, :] = lead_up[...]
-    up[lead_rows : lead_rows + block, :] = own_up[...]
-    up[lead_rows + block :, :] = across[block : 2 * block, :]
-    down[:lead_rows, :] = lead_down[...]
-    down[lead_rows : lead_rows + block, :] = own_down[...]
-    down[lead_rows + block :, :] = across[(reach - 1) * block :, :]
-    for s in range(2, reach - 1):
-        far[s - 2][...] = across[s * block : (s + 1) * block, :]
-    queries[:lead_rows, :] = lead[...]
-    for k, rows in enumerate((lead, lead_up, lead_down)):
-        near[k * lead_rows : (k + 1) * lead_rows, :] = rows[...]
-
-    def put(rows, straight, start):
-        ends[:block, :] = straight[...]
-        ends[block:, :] = across[start : start + block, :]
-
-    pl.when(z == reach - 1)(functools.partial(put, ends, own_up, block))
-    pl.when(z != reach - 1)(functools.partial(put, ends, own_down, (reach - 1) * block))
-
-    def keep(rows):
-        queries[lead_rows:, :] = rows[...]
-
-    pl.when(z < reach // 2)(functools.partial(keep, lead_up))
-    pl.when(z >= reach // 2)(functools.partial(keep, lead_down))
-
-
-def collect_kernel(peers, block, lead_rows, me_ref, mine, across, up, down, ends, *rest):
-    reach = peers // 2
-    far, far_across, own = rest[: reach - 3], rest[reach - 3 : 2 * reach - 6], rest[-1]
-    rest = rest[2 * reach - 6 : -1]
-    count = len(rest) // 2
-    z = me_ref[0] // 2
-    skip = lead_rows
-
-    def keep(slot, src):
-        at = peers * block + slot * lead_rows
-        own[at : at + lead_rows, :] = src[:lead_rows, :]
-
-    for slot in range(count):
-        k = slot + 2 if slot < reach - 3 else reach - 1
-        pl.when(z >= k)(functools.partial(keep, slot, rest[slot]))
-        pl.when(z < k)(functools.partial(keep, slot, rest[count + slot]))
+    at_end = (z == 0) | (z == reach - 1)
 
     def put(k, src, start=0):
         own[k * block : (k + 1) * block, :] = src[start : start + block, :]
 
-    def put_two(k, src, start):
-        put(k, src, start)
-        put(reach + k, src, start + block)
+    def put_last(first, second, start, then):
+        put(reach - 1, first, start)
+        put(2 * reach - 1, second, then)
 
     put(0, mine)
-    put(reach, across)
+    put(reach, asked_y, 2 * lead_rows)
+    put(1, even2, lead_rows)
+    put(reach + 1, even2, lead_rows + block)
     for s in range(2, reach - 1):
         put(s, far[s - 2])
         put(reach + s, far_across[s - 2])
-    for slot, src, missing in ((1, up, 0), (reach - 1, down, reach - 1)):
-        pl.when(z == missing)(functools.partial(put_two, slot, ends, 0))
-        pl.when(z != missing)(functools.partial(put_two, slot, src, skip))
+    pl.when(at_end)(functools.partial(put_last, ends, ends, 0, block))
+    pl.when(jnp.logical_not(at_end))(functools.partial(put_last, odd, odd2, lead_rows, lead_rows))
+
+    def keep(slot, src):
+        cols[slot * lead_rows : (slot + 1) * lead_rows, :] = src[:lead_rows, :]
+
+    for slot, src in enumerate((lead, lead_even, odd)):
+        keep(slot, src)
+    if reach == 4:
+        pl.when(at_end)(functools.partial(keep, 3, even2))
+        pl.when(jnp.logical_not(at_end))(functools.partial(keep, 3, odd2))
+    else:
+        for slot, src in enumerate(rest):
+            keep(3 + slot, src)
 
 
 def lead_ids(rows, start, cap):
@@ -199,18 +194,18 @@
     return jnp.max(jnp.where(same, scores, -1.0), axis=0, keepdims=True)
 
 
-def lead_best_kernel(slots, cap, asked, asked_y, near, near_other, own, top):
+def lead_best_kernel(cap, asked, asked_y, cols, cols_other, top):
     lead_rows = cap + SUB
-    count = (own.shape[0] - slots) // lead_rows
-    near_ids, other_ids = lead_column(near, 0, 3, cap), lead_column(near_other, 0, 3, cap)
-    far_ids = lead_column(own, slots, count, cap)
+    count = cols.shape[0] // lead_rows
+    late = 3 * lead_rows
     top[...] = jnp.full(top.shape, -1.0, jnp.float32)
-    for i, queries in enumerate((asked, asked_y)):
-        best = lead_tops(near[...], near_ids, queries, 0, cap, i == 0)
-        best = jnp.maximum(best, lead_tops(near_other[...], other_ids, queries, 0, cap, False))
-        best = jnp.maximum(best, lead_tops(own[slots:, :], far_ids, queries, 0, cap, False))
-        top[i : i + 1, :] = best
-        top[2 + i : 3 + i, :] = lead_tops(own[slots:, :], far_ids, queries, lead_rows, cap, False)
+    for columns in (cols, cols_other):
+        ids = lead_column(columns, 0, count, cap)
+        for i, queries in enumerate((asked, asked_y)):
+            best = lead_tops(columns[...], ids, queries, 0, cap, i == 0 and columns is cols)
+            top[i : i + 1, :] = jnp.maximum(top[i : i + 1, :], best)
+            best = lead_tops(columns[late:, :], ids[late:], queries, lead_rows, cap, False)
+            top[2 + i : 3 + i, :] = jnp.maximum(top[2 + i : 3 + i, :], best)
 
 
 def ids_of(rows, peers, block):
@@ -246,7 +241,7 @@
     top[1:2, :] = ids[:, :slots]
 
 
-def far_best_kernel(peers, block, edges, me_ref, own, far, top, asked, asked_y, lead_top, out, flag):
+def far_best_kernel(peers, block, edges, me_ref, own, far, top, lead_top, out, flag):
     width = own.shape[1]
     slots = peers * block
     own_ids, far_ids = top[1:2, :], ids_of(far, peers, block)
@@ -266,16 +261,12 @@
     none = jnp.full((1, cap), -1.0, jnp.float32)
     for k in range(peers):
         piece = best if k == 0 else pltpu.roll(best, width - k * block, 1)
-        row = z - k % reach
-        row = 2 * jnp.where(row < 0, row + reach, row) + (y if k < reach else 1 - y)
+        up = (z % 2 == 0) == (k % 2 == 1)
+        row = z + jnp.where(up, k % reach, reach - k % reach)
+        row = 2 * (row % reach) + (y if k < reach else 1 - y)
         out[row, :, :pitch] = piece[0:1, :pitch]
         out[k, :, pitch:] = none
-    count = (far.shape[0] - slots) // (cap + SUB)
-    ids = lead_column(far, slots, count, cap)
-    lead = []
-    for i, (queries, start) in enumerate(((asked, 0), (asked_y, 0), (asked, cap + SUB), (asked_y, cap + SUB))):
-        late = lead_tops(far[slots:, :], ids, queries, start, cap, False)
-        lead.append(jnp.maximum(lead_top[i : i + 1, :], late))
+    lead = [lead_top[i : i + 1, :] for i in range(4)]
     out[2 * z + y, :, pitch:] = lead[0]
     out[2 * z + 1 - y, :, pitch:] = lead[1]
     if edges:
@@ -373,16 +364,6 @@
     me = lax.axis_index("dp")
     me1 = me.reshape(1)
 
-    unit, info, hdr, lead = call(
-        functools.partial(lead_kernel, peers, cap, block),
-        "lead",
-        [shape((count, width), bf16), shape((8, count), jnp.int32), shape((8, width), f32), shape((cap + SUB, width), bf16)],
-        [SMEM, VMEM, VMEM],
-        [VMEM] * 4,
-        flops=2 * cap * count * width,
-        nbytes=6 * count * width,
-    )(me1, cluster_ids.reshape(1, count), embeddings)
-
     def dp_pairs(step):
         pairs = []
         for z in range(reach):
@@ -398,73 +379,88 @@
     swap = [(0, 1), (1, 0)]
 
     ends_pairs = dp_pairs(lambda z, y: (reach - 1 - z, y) if z in (0, reach - 1) else None)
-    shift_pairs = [dp_pairs(lambda z, y, s=s: ((z + s) % reach, y)) for s in range(2, reach - 1)]
+    shift_pairs = [
+        dp_pairs(lambda z, y, s=s: ((z + (s if z % 2 == 0 else reach - s)) % reach, y)) for s in range(2, reach - 1)
+    ]
+    even_pairs = dp_pairs(lambda z, y: (z ^ 1, y))
+    odd_pairs = dp_pairs(lambda z, y: (((z + 1) ^ 1) - 1, y) if 0 < z < reach - 1 else None)
 
     one = shape((block, width), bf16)
-    two = shape((2 * block, width), bf16)
     lead_rows = cap + SUB
-    message = shape((lead_rows + 2 * block, width), bf16)
+    message = shape((lead_rows + block, width), bf16)
     edges = reach == 4
 
-    up1 = lax.ppermute(lead, "dp", up_pairs)
-    down1 = lax.ppermute(lead, "dp", down_pairs)
-    *straight, across = call(
-        functools.partial(pack_kernel, peers, block),
+    info, mine, mine_across, lead, near, odd, across, *fars = call(
+        functools.partial(pack_kernel, peers, cap, block),
         "pack",
-        [one] * reach + [shape((reach * block, width), bf16)],
-        [VMEM] * 3,
-        [VMEM] * (reach + 1),
-        [pltpu.VMEM((slots, count), bf16)],
-        flops=2 * slots * count * width,
-        nbytes=4 * count * width,
-    )(unit, info, hdr)
+        [shape((8, count), jnp.int32), one, one, shape((lead_rows, width), bf16), one, message]
+        + [shape(((reach - 1) * block, width), bf16)]
+        + [one] * (reach - 3),
+        [SMEM, VMEM, pl.BlockSpec(memory_space=pltpu.HBM)],
+        [VMEM] * (4 + reach),
+        [
+            pltpu.VMEM((count, width), f32),
+            pltpu.VMEM((count, width), bf16),
+            pltpu.VMEM((slots + cap, count), bf16),
+            pltpu.SemaphoreType.DMA((CHUNKS,)),
+        ],
+        flops=2 * (slots + cap) * count * width,
+        nbytes=8 * count * width,
+    )(me1, cluster_ids.reshape(1, count), embeddings)
+    odd1 = lax.ppermute(odd, "dp", odd_pairs)
+    even1 = lax.ppermute(lead, "dp", even_pairs)
     across = lax.ppermute(across, "dp", other_y)
-    fars = [lax.ppermute(straight[s + 2], "dp", pairs) for s, pairs in enumerate(shift_pairs)]
-    across, fars, up1, down1 = lax.optimization_barrier((across, fars, up1, down1))
-    up2, down2, ends, asked, near, *fars_r = call(
+    fars = [lax.ppermute(rows, "dp", pairs) for rows, pairs in zip(fars, shift_pairs)]
+    across, fars, odd1, even1 = lax.optimization_barrier((across, fars, odd1, even1))
+    even2, odd2, ends, asked, *fars_r = call(
         functools.partial(relay_kernel, peers, block, lead_rows),
         "relay",
-        [message, message, two, shape((2 * lead_rows, width), bf16), shape((3 * lead_rows, width), bf16)] + [one] * (reach - 3),
-        [SMEM] + [VMEM] * 6,
-        [VMEM] * (2 + reach),
+        [
+            shape((lead_rows + 2 * block, width), bf16),
+            message,
+            shape((2 * block, width), bf16),
+            shape((2 * lead_rows + block, width), bf16),
+        ]
+        + [one] * (reach - 3),
+        [VMEM] * 7,
+        [VMEM] * (1 + reach),
         nbytes=2 * slots * width,
-    )(me1, straight[1], straight[reach - 1], across, lead, up1, down1)
-    up2 = lax.ppermute(up2, "dp", up_pairs)
-    down2 = lax.ppermute(down2, "dp", down_pairs)
+    )(lead, near, odd, mine_across, across, even1, odd1)
+    odd2 = lax.ppermute(odd2, "dp", odd_pairs)
+    even2 = lax.ppermute(even2, "dp", even_pairs)
     ends = lax.ppermute(ends, "dp", ends_pairs)
     fars_r = [lax.ppermute(rows, "dp", pairs) for rows, pairs in zip(fars_r, shift_pairs)]
     asked_y = lax.ppermute(asked, "dp", other_y)
-    up2, down2, ends, fars_r, asked_y, near = lax.optimization_barrier((up2, down2, ends, fars_r, asked_y, near))
-    near_o = lax.ppermute(near, "owner", swap)
-    ups, downs = [up2], [down2]
+    odd2, even2, ends, fars_r, asked_y = lax.optimization_barrier((odd2, even2, ends, fars_r, asked_y))
+    late = []
     if not edges:
-        up, down = up2[:lead_rows], down2[:lead_rows]
+        is_even = (me // 2) % 2 == 0
+        up = jnp.where(is_even, odd2[:lead_rows], even2[:lead_rows])
+        down = jnp.where(is_even, even2[:lead_rows], odd2[:lead_rows])
+        late = [up, down]
         for _ in range(reach - 3):
             up = lax.ppermute(up, "dp", up_pairs)
             down = lax.ppermute(down, "dp", down_pairs)
-            ups.append(up)
-            downs.append(down)
-        ups, downs = ups[:-1] + ups[-1:], downs[:-1][::-1] + downs[-1:]
-
-    n_late = len(ups)
-    own = call(
+            late += [up, down]
+    own, cols = call(
         functools.partial(collect_kernel, peers, block, lead_rows),
         "collect",
-        shape((slots + n_late * lead_rows, width), bf16),
-        [SMEM] + [VMEM] * (5 + 2 * (reach - 3) + 2 * n_late),
-        VMEM,
+        [shape((slots, width), bf16), shape(((3 + max(1, len(late))) * lead_rows, width), bf16)],
+        [SMEM] + [VMEM] * (8 + 2 * (reach - 3) + len(late)),
+        [VMEM] * 2,
         nbytes=4 * slots * width,
-    )(me1, straight[0], across, up2, down2, ends, *fars, *fars_r, *ups, *downs)
+    )(me1, mine, odd1, asked_y, even2, odd2, ends, lead, even1, *fars, *fars_r, *late)
+    cols_o = lax.ppermute(cols, "owner", swap)
     far = lax.ppermute(own, "owner", swap)
     lead_top = call(
-        functools.partial(lead_best_kernel, slots, cap),
+        functools.partial(lead_best_kernel, cap),
         "lead_best",
         shape((8, cap), f32),
-        [VMEM] * 5,
+        [VMEM] * 4,
         VMEM,
-        flops=4 * (6 + 2 * n_late) * cap * cap * width,
-        nbytes=2 * (10 + n_late) * cap * width,
-    )(asked, asked_y, near, near_o, own)
+        flops=40 * cap * cap * width,
+        nbytes=20 * cap * width,
+    )(asked, asked_y, cols, cols_o)
     top = call(
         functools.partial(own_best_kernel, peers, block),
         "own_best",
@@ -478,11 +474,11 @@
         functools.partial(far_best_kernel, peers, block, edges),
         "far_best",
         [shape((peers, 1, pitch + cap), f32), shape((8, LANES), f32)],
-        [SMEM] + [VMEM] * 6,
+        [SMEM] + [VMEM] * 4,
         [VMEM] * 2,
-        flops=2 * slots * slots * width + 8 * n_late * cap * cap * width,
+        flops=2 * slots * slots * width,
         nbytes=4 * slots * width,
-    )(me1, own, far, top, asked, asked_y, lead_top)
+    )(me1, own, far, top, lead_top)
     back = lax.all_to_all(best, "dp", split_axis=0, concat_axis=0, tiled=True)
     flags = [flag]
     for k in range(1, groups):

time: 111 us -> 105 us (0.946)
  starting transfers between devices: 30 us -> 21.6 us
  waiting for transfers between devices: 62.9 us -> 65.7 us
    ppermute x1 -> x2, waiting for transfers between devices: 36.5 us -> 60.1 us  [local(): lax.ppermute(rows, 'dp', pairs)]
    ppermute x6 -> x5, waiting for transfers between devices: 22.6 us -> 1.72 us  [the longest x1 1.71 us: local(): cols_o = lax.ppermute(cols, 'owner', swap)]
    ppermute x6 -> x5, starting transfers between devices: 14 us -> 5.83 us  [the longest x1 4.35 us: local(): even1 = lax.ppermute(lead, 'dp', even_pairs)]
    ppermute x1, starting transfers between devices: 7.37 us -> 4.39 us  [local(): ends = lax.ppermute(ends, 'dp', ends_pairs)]
    pallas_call x3 -> x2, Pallas kernels: 8.69 us -> 9.11 us  [the longest x1 5.94 us: local(): call(functools.partial(pack_kernel, peers, cap, block), 'pack', [shape((8...]
  transfers between devices with their start and end apart: 13 -> 13, of which waited for: 5 -> 5; matrix products, arithmetic and copies ran while one was open for 0% -> 0% of each run, Pallas kernels for 4% -> 5%
where the time goes in v3:
time: 105 us
  waiting for transfers between devices  65.7 us (63%)
  starting transfers between devices  21.6 us (21%)
  Pallas kernels  15.5 us (15%)
  local copies, waits for them, and re-layouts  1.11 us (1%)
    ppermute x2, waiting for transfers between devices, local(): lax.ppermute(rows, 'dp', pairs)  60.1 us
    pallas_call x1, Pallas kernels, local(): call(functools.partial(pack_kernel, peers, cap, block), 'pack', [shape((8...  5.94 us
    ppermute x1, starting transfers between devices, local(): ends = lax.ppermute(ends, 'dp', ends_pairs)  4.39 us
    ppermute x1, starting transfers between devices, local(): even1 = lax.ppermute(lead, 'dp', even_pairs)  4.35 us
    all_to_all x1, starting transfers between devices, local(): back = lax.all_to_all(best, 'dp', split_axis=0, concat_axis=0, tiled=True)  3.76 us
    pallas_call x1, Pallas kernels, local(): call(functools.partial(lead_best_kernel, cap), 'lead_best', shape((8, cap...  3.17 us
    ppermute x1, starting transfers between devices, local(): across = lax.ppermute(across, 'dp', other_y)  3.03 us
    pallas_call x1, Pallas kernels, local(): call(functools.partial(far_best_kernel, peers, block, edges), 'far_best',...  2.87 us
  transfers between devices with their start and end apart: 13, of which 5 were waited for; matrix products, arithmetic and copies ran while one was open for 0% of the time, Pallas kernels for 5%

profile of v3, /device:TPU:0, one launch (start us, length us, event | category | flops | bytes accessed | tf_op | source)
XLA Modules:
  0.0 104.7 jit_solution(10518044530367673293)
XLA Ops:
  0.0 5.9 %pack.1 = (s32[8,1024]{1,0:T(8,128)S(1)}, bf16[112,1024]{1,0:T(8,128)(2,1)S(1)}, bf16[112,1024]{1,0:T(8,128)(2,1)S(1)}, bf16[272,1024]{1,0:T(8,128)(2,1)S(1)}, b...) custom-call(s32[1]{0:T(128)} %bitcast.8.me_ref, ...), custom_call_target="tpu_custom_call" | custom-call | flops 2415919104 | bytes 8388608 | tf_op jit(solution)/shard_map/pack/pallas_call | solution.py:393
  5.9 0.7 collective-permute-start.4
  6.7 3.0 %collective-permute-start.2 = (bf16[336,1024]{1,0:T(8,128)(2,1)S(1)}, bf16[336,1024]{1,0:T(8,128)(2,1)S(1)}, u32[]{:S(2)}, u32[]{:S(2)}) collective-permute-start(bf16[336,1024]{1,0:T(8,128)(2,1)S(1)} %get-tuple-element.86), channel_id=1, source_target_pairs={{0,2},{2,0},{4,6},{6,4},{8,10},{10,8},{12,14},{14,12},{1,3},{3,1},... | collective-permute-start | bytes 2064392 | tf_op jit(solution)/shard_map/ppermute | solution.py:412
  9.7 4.3 %collective-permute-start.5 = (bf16[272,1024]{1,0:T(8,128)(2,1)S(1)}, bf16[272,1024]{1,0:T(8,128)(2,1)S(1)}, u32[]{:S(2)}, u32[]{:S(2)}) collective-permute-start(bf16[272,1024]{1,0:T(8,128)(2,1)S(1)} %get-tuple-element.89.lead), channel_id=1, source_target_pairs={{0,4},{2,6},{4,0},{6,2},{8,12},{10,14},{12,8},{14,10},{1,5},{3,7},... | collective-permute-start | bytes 1671176 | tf_op jit(solution)/shard_map/ppermute | solution.py:411
  14.1 25.4 %collective-permute-done.3.rest_0_ = bf16[112,1024]{1,0:T(8,128)(2,1)S(1)} collective-permute-done((bf16[112,1024]{1,0:T(8,128)(2,1)S(1)}, bf16[112,1024]{1,0:T(8,128)(2,1)S(1)}, u32[]{:S(2)}, u32[]{:S(2)}) %collective-permute-start.3) | collective-permute-done | bytes 229408 | tf_op jit(solution)/shard_map/ppermute | solution.py:413
  39.4 0.0 collective-permute-done.5.lead_even
  39.4 0.0 collective-permute-done.2.across
  39.4 0.0 collective-permute-done.4.lead_odd.odd
  39.4 0.3 relay.1
  39.7 1.6 %collective-permute-start.10 = (bf16[656,1024]{1,0:T(8,128)(2,1)S(1)}, bf16[656,1024]{1,0:T(8,128)(2,1)S(1)}, u32[]{:S(2)}, u32[]{:S(2)}) collective-permute-start(bf16[656,1024]{1,0:T(8,128)(2,1)S(1)} %get-tuple-element.99.asked), channel_id=1, source_target_pairs={{0,2},{2,0},{4,6},{6,4},{8,10},{10,8},{12,14},{14,12},{1,3},{3,1},... | collective-permute-start | bytes 4030472 | tf_op jit(solution)/shard_map/ppermute | solution.py:433
  41.3 0.0 collective-permute-start.7
  41.3 0.7 collective-permute-start.6
  42.0 4.4 %collective-permute-start.8 = (bf16[224,1024]{1,0:T(8,128)(2,1)S(1)}, bf16[224,1024]{1,0:T(8,128)(2,1)S(1)}, u32[]{:S(2)}, u32[]{:S(2)}) collective-permute-start(bf16[224,1024]{1,0:T(8,128)(2,1)S(1)} %get-tuple-element.97), channel_id=1, source_target_pairs={{0,12},{2,14},{12,0},{14,2},{1,13},{3,15},{13,1},{15,3},{16,28},{1... | collective-permute-start | bytes 1376264 | tf_op jit(solution)/shard_map/ppermute | solution.py:431
  46.4 1.1 %collective-permute-start.9 = (bf16[112,1024]{1,0:T(8,128)(2,1)S(1)}, bf16[112,1024]{1,0:T(8,128)(2,1)S(1)}, u32[]{:S(2)}, u32[]{:S(2)}) collective-permute-start(bf16[112,1024]{1,0:T(8,128)(2,1)S(1)} %get-tuple-element.98), channel_id=1, source_target_pairs={{0,8},{2,10},{4,12},{6,14},{8,0},{10,2},{12,4},{14,6},{1,9},{3,11}... | collective-permute-start | bytes 688136 | tf_op jit(solution)/shard_map/ppermute | solution.py:432
  47.4 34.7 %collective-permute-done.9.rest_1_ = bf16[112,1024]{1,0:T(8,128)(2,1)S(1)} collective-permute-done((bf16[112,1024]{1,0:T(8,128)(2,1)S(1)}, bf16[112,1024]{1,0:T(8,128)(2,1)S(1)}, u32[]{:S(2)}, u32[]{:S(2)}) %collective-permute-start.9) | collective-permute-done | bytes 229408 | tf_op jit(solution)/shard_map/ppermute | solution.py:432
  82.1 0.0 collective-permute-done.8.ends
  82.2 0.3 collect.1
  82.4 0.1 collective-permute-start.12
  82.5 0.5 collective-permute-start.11
  83.0 2.1 %own_best.1.top = f32[8,896]{1,0:T(8,128)S(1)} custom-call(bf16[896,1024]{1,0:T(8,128)(2,1)S(1)} %get-tuple-element.106.own), custom_call_target="tpu_custom_call" | custom-call | flops 1644167168 | bytes 1835008 | tf_op jit(solution)/shard_map/own_best/pallas_call | solution.py:464
  85.1 1.7 %collective-permute-done.12.cols_other = bf16[1088,1024]{1,0:T(8,128)(2,1)S(1)} collective-permute-done((bf16[1088,1024]{1,0:T(8,128)(2,1)S(1)}, bf16[1088,1024]{1,0:T(8,128)(2,1)S(1)}, u32[]{:S(2)}, u32[]{:S(2)}) %collective-permute-start.12) | collective-permute-done | bytes 2228256 | tf_op jit(solution)/shard_map/ppermute | solution.py:453
  86.8 3.2 %lead_best.1.lead_top = f32[8,256]{1,0:T(8,128)S(1)} custom-call(bf16[656,1024]{1,0:T(8,128)(2,1)S(1)} %get-tuple-element.99.asked, bf16[656,1024]{1,0:T(8,128)(2,1)S(1)} %collective-permute-done.10.asked_y, bf16[1088,1024]{1,0:T(8,128)(2,1)S(1)} %get-tuple-element.107.cols, bf16[1088,1024]{1,0:T(8,128)(2,1)S(1)} %collective-permute-done.12.cols_other), custom_call_target="tpu_custom_call" | custom-call | flops 2684354560 | bytes 5242880 | tf_op jit(solution)/shard_map/lead_best/pallas_call | solution.py:455
  90.0 0.0 copy-start
  90.0 2.9 %far_best.1 = (f32[8,1,384]{2,1,0:T(1,128)}, f32[8,128]{1,0:T(8,128)S(1)}) custom-call(s32[1]{0:T(128)} %bitcast.8.me_ref, bf16[896,1024]{1,0:T(8,128)(2,1)S(1)} %get-tuple-element.106.own, bf16[896,1024]{1,0:T(8,128)(2,1)S(1)} %collective-permute-done.11.far, f32[8,896]{1,0:T(8,128)S(1)} %own_best.1.top, f32[8,256]{1,0:T(8,128)S(1)} %lead_best.1.lead_top), custom_call_target="tpu_custom_call" | custom-call | flops 1644167168 | bytes 3670016 | tf_op jit(solution)/shard_map/far_best/pallas_call | solution.py:473
  92.9 3.8 %all-to-all-start.3 = ((f32[8,1,384]{2,1,0:T(1,128)}), f32[8,1,384]{2,1,0:T(1,128)S(1)}, u32[]{:S(2)}, u32[]{:S(2)}) async-start(f32[8,1,384]{2,1,0:T(1,128)} %get-tuple-element.110), calls=%async_computation.3 | async-start | bytes 24576 | tf_op jit(solution)/shard_map/all_to_all | solution.py:482
  96.7 1.5 %collective-permute-start.13 = (f32[8,128]{1,0:T(8,128)S(1)}, f32[8,128]{1,0:T(8,128)S(1)}, u32[]{:S(2)}, u32[]{:S(2)}) collective-permute-start(f32[8,128]{1,0:T(8,128)S(1)} %get-tuple-element.108), channel_id=1, source_target_pairs={{0,16},{16,0},{1,17},{17,1},{2,18},{18,2},{3,19},{19,3},{4,20},{20... | collective-permute-start | bytes 12296 | tf_op jit(solution)/shard_map/ppermute | solution.py:485
  98.2 2.1 %collective-permute-done.13 = f32[8,128]{1,0:T(8,128)S(1)} collective-permute-done((f32[8,128]{1,0:T(8,128)S(1)}, f32[8,128]{1,0:T(8,128)S(1)}, u32[]{:S(2)}, u32[]{:S(2)}) %collective-permute-start.13) | collective-permute-done | bytes 4128 | tf_op jit(solution)/shard_map/ppermute | solution.py:485
  100.3 0.5 slice.9
  101.5 1.8 %all-to-all-done.3.back_ref = f32[8,1,384]{2,1,0:T(1,128)S(1)} async-done(((f32[8,1,384]{2,1,0:T(1,128)}), f32[8,1,384]{2,1,0:T(1,128)S(1)}, u32[]{:S(2)}, u32[]{:S(2)}) %all-to-all-start.3) | async-done | bytes 12320 | tf_op jit(solution)/shard_map/all_to_all | solution.py:482
  103.2 0.9 final.1
  104.1 0.0 copy-start.1
  104.1 0.6 copy-done.1
  (8 shorter events, 0.0 us)
Async XLA Ops:
  5.9 33.5 %collective-permute-start.4 = (bf16[384,1024]{1,0:T(8,128)(2,1)S(1)}, bf16[384,1024]{1,0:T(8,128)(2,1)S(1)}, u32[]{:S(2)}, u32[]{:S(2)}) collective-permute-start(bf16[384,1024]{1,0:T(8,128)(2,1)S(1)} %get-tuple-element.88.odd), channel_id=1, source_target_pairs={{4,8},{6,10},{8,4},{10,6},{5,9},{7,11},{9,5},{11,7},{20,24},{22,26... | collective-permute-start | bytes 2359304 | tf_op jit(solution)/shard_map/ppermute | solution.py:410
  6.7 32.8 %collective-permute-start.2 = (bf16[336,1024]{1,0:T(8,128)(2,1)S(1)}, bf16[336,1024]{1,0:T(8,128)(2,1)S(1)}, u32[]{:S(2)}, u32[]{:S(2)}) collective-permute-start(bf16[336,1024]{1,0:T(8,128)(2,1)S(1)} %get-tuple-element.86), channel_id=1, source_target_pairs={{0,2},{2,0},{4,6},{6,4},{8,10},{10,8},{12,14},{14,12},{1,3},{3,1},... | collective-permute-start | bytes 2064392 | tf_op jit(solution)/shard_map/ppermute | solution.py:412
  9.7 29.7 %collective-permute-start.5 = (bf16[272,1024]{1,0:T(8,128)(2,1)S(1)}, bf16[272,1024]{1,0:T(8,128)(2,1)S(1)}, u32[]{:S(2)}, u32[]{:S(2)}) collective-permute-start(bf16[272,1024]{1,0:T(8,128)(2,1)S(1)} %get-tuple-element.89.lead), channel_id=1, source_target_pairs={{0,4},{2,6},{4,0},{6,2},{8,12},{10,14},{12,8},{14,10},{1,5},{3,7},... | collective-permute-start | bytes 1671176 | tf_op jit(solution)/shard_map/ppermute | solution.py:411
  14.1 25.4 %collective-permute-start.3 = (bf16[112,1024]{1,0:T(8,128)(2,1)S(1)}, bf16[112,1024]{1,0:T(8,128)(2,1)S(1)}, u32[]{:S(2)}, u32[]{:S(2)}) collective-permute-start(bf16[112,1024]{1,0:T(8,128)(2,1)S(1)} %get-tuple-element.87), channel_id=1, source_target_pairs={{0,8},{2,10},{4,12},{6,14},{8,0},{10,2},{12,4},{14,6},{1,9},{3,11}... | collective-permute-start | bytes 688136 | tf_op jit(solution)/shard_map/ppermute | solution.py:413
  39.7 42.5 %collective-permute-start.10 = (bf16[656,1024]{1,0:T(8,128)(2,1)S(1)}, bf16[656,1024]{1,0:T(8,128)(2,1)S(1)}, u32[]{:S(2)}, u32[]{:S(2)}) collective-permute-start(bf16[656,1024]{1,0:T(8,128)(2,1)S(1)} %get-tuple-element.99.asked), channel_id=1, source_target_pairs={{0,2},{2,0},{4,6},{6,4},{8,10},{10,8},{12,14},{14,12},{1,3},{3,1},... | collective-permute-start | bytes 4030472 | tf_op jit(solution)/shard_map/ppermute | solution.py:433
  41.3 40.9 %collective-permute-start.7 = (bf16[496,1024]{1,0:T(8,128)(2,1)S(1)}, bf16[496,1024]{1,0:T(8,128)(2,1)S(1)}, u32[]{:S(2)}, u32[]{:S(2)}) collective-permute-start(bf16[496,1024]{1,0:T(8,128)(2,1)S(1)} %get-tuple-element.96), channel_id=1, source_target_pairs={{0,4},{2,6},{4,0},{6,2},{8,12},{10,14},{12,8},{14,10},{1,5},{3,7},... | collective-permute-start | bytes 3047432 | tf_op jit(solution)/shard_map/ppermute | solution.py:430
  41.3 40.9 %collective-permute-start.6 = (bf16[384,1024]{1,0:T(8,128)(2,1)S(1)}, bf16[384,1024]{1,0:T(8,128)(2,1)S(1)}, u32[]{:S(2)}, u32[]{:S(2)}) collective-permute-start(bf16[384,1024]{1,0:T(8,128)(2,1)S(1)} %get-tuple-element.95), channel_id=1, source_target_pairs={{4,8},{6,10},{8,4},{10,6},{5,9},{7,11},{9,5},{11,7},{20,24},{22,26... | collective-permute-start | bytes 2359304 | tf_op jit(solution)/shard_map/ppermute | solution.py:429
  42.0 40.1 %collective-permute-start.8 = (bf16[224,1024]{1,0:T(8,128)(2,1)S(1)}, bf16[224,1024]{1,0:T(8,128)(2,1)S(1)}, u32[]{:S(2)}, u32[]{:S(2)}) collective-permute-start(bf16[224,1024]{1,0:T(8,128)(2,1)S(1)} %get-tuple-element.97), channel_id=1, source_target_pairs={{0,12},{2,14},{12,0},{14,2},{1,13},{3,15},{13,1},{15,3},{16,28},{1... | collective-permute-start | bytes 1376264 | tf_op jit(solution)/shard_map/ppermute | solution.py:431
  46.4 35.8 %collective-permute-start.9 = (bf16[112,1024]{1,0:T(8,128)(2,1)S(1)}, bf16[112,1024]{1,0:T(8,128)(2,1)S(1)}, u32[]{:S(2)}, u32[]{:S(2)}) collective-permute-start(bf16[112,1024]{1,0:T(8,128)(2,1)S(1)} %get-tuple-element.98), channel_id=1, source_target_pairs={{0,8},{2,10},{4,12},{6,14},{8,0},{10,2},{12,4},{14,6},{1,9},{3,11}... | collective-permute-start | bytes 688136 | tf_op jit(solution)/shard_map/ppermute | solution.py:432
  82.4 4.4 %collective-permute-start.12 = (bf16[1088,1024]{1,0:T(8,128)(2,1)S(1)}, bf16[1088,1024]{1,0:T(8,128)(2,1)S(1)}, u32[]{:S(2)}, u32[]{:S(2)}) collective-permute-start(bf16[1088,1024]{1,0:T(8,128)(2,1)S(1)} %get-tuple-element.107.cols), channel_id=1, source_target_pairs={{0,1},{1,0},{2,3},{3,2},{4,5},{5,4},{6,7},{7,6},{8,9},{9,8},{10,11... | collective-permute-start | bytes 6684680 | tf_op jit(solution)/shard_map/ppermute | solution.py:453
  82.5 7.5 %collective-permute-start.11 = (bf16[896,1024]{1,0:T(8,128)(2,1)S(1)}, bf16[896,1024]{1,0:T(8,128)(2,1)S(1)}, u32[]{:S(2)}, u32[]{:S(2)}) collective-permute-start(bf16[896,1024]{1,0:T(8,128)(2,1)S(1)} %get-tuple-element.106.own), channel_id=1, source_target_pairs={{0,1},{1,0},{2,3},{3,2},{4,5},{5,4},{6,7},{7,6},{8,9},{9,8},{10,11... | collective-permute-start | bytes 5505032 | tf_op jit(solution)/shard_map/ppermute | solution.py:454
  90.0 14.1 %copy-start = (s32[1024]{0:T(1024)S(1)}, s32[1024]{0:T(1024)}, u32[]{:S(2)}) copy-start(s32[1024]{0:T(1024)} %param.7) | copy-start | bytes 12292
  92.9 10.3 %all-to-all-start.3 = ((f32[8,1,384]{2,1,0:T(1,128)}), f32[8,1,384]{2,1,0:T(1,128)S(1)}, u32[]{:S(2)}, u32[]{:S(2)}) async-start(f32[8,1,384]{2,1,0:T(1,128)} %get-tuple-element.110), calls=%async_computation.3 | async-start | bytes 24576 | tf_op jit(solution)/shard_map/all_to_all | solution.py:482
  96.7 3.6 %collective-permute-start.13 = (f32[8,128]{1,0:T(8,128)S(1)}, f32[8,128]{1,0:T(8,128)S(1)}, u32[]{:S(2)}, u32[]{:S(2)}) collective-permute-start(f32[8,128]{1,0:T(8,128)S(1)} %get-tuple-element.108), channel_id=1, source_target_pairs={{0,16},{16,0},{1,17},{17,1},{2,18},{18,2},{3,19},{19,3},{4,20},{20... | collective-permute-start | bytes 12296 | tf_op jit(solution)/shard_map/ppermute | solution.py:485
  104.1 0.6 copy-start.1

commit v4 on v3

--- a/solution.py
+++ b/solution.py
@@ -33,7 +33,7 @@
     return 16 + 2 * leader + bad
 
 
-def pack_kernel(peers, cap, block, me_ref, ids_ref, emb_hbm, info_ref, mine, mine_across, lead, near, odd, across, *rest):
+def pack_kernel(peers, cap, block, me_ref, ids_ref, emb_hbm, info_ref, mine, mine_across, even, odd, across, *rest):
     far, (emb_ref, unit_ref, pick, sem) = rest[:-4], rest[-4:]
     count, width = emb_ref.shape
     chunk = count // CHUNKS
@@ -89,7 +89,7 @@
     block_ids = jnp.where(last, code, block_ids)
     hdr = pad_lanes(block_ids, width)
     lead_hdr = jnp.broadcast_to(pad_lanes(ids_at[:, slots:], width), (SUB, width)).astype(jnp.bfloat16)
-    lead[cap:, :] = lead_hdr
+    even[cap : cap + SUB, :] = lead_hdr
     odd[cap : cap + SUB, :] = lead_hdr
     at = lax.broadcasted_iota(jnp.int32, (slots + cap, count), 0)
     pick[...] = jnp.where(at == dest, 1.0, 0.0).astype(jnp.bfloat16)
@@ -101,7 +101,7 @@
         squares = jnp.sum(emb * emb, axis=1, keepdims=True)
         unit_ref[rows, :] = (emb * lax.rsqrt(squares + 1e-06)).astype(jnp.bfloat16)
 
-    places = [(mine, 0), (near, 0), *[(ref, 0) for ref in far], (odd, cap + SUB), (mine_across, 0)]
+    places = [(mine, 0), (even, cap + SUB), *[(ref, 0) for ref in far], (odd, cap + SUB), (mine_across, 0)]
     places += [(across, s * block) for s in range(reach - 1)]
     is_hdr = lax.broadcasted_iota(jnp.int32, (block, 1), 0) == block - 1
     tile = 256
@@ -111,33 +111,35 @@
         for k, (ref, at) in enumerate(places):
             rows = acc[k * block : (k + 1) * block]
             ref[at : at + block, cols] = jnp.where(is_hdr, hdr[:, cols], rows).astype(jnp.bfloat16)
-        lead[:cap, cols] = acc[slots:].astype(jnp.bfloat16)
+        even[:cap, cols] = acc[slots:].astype(jnp.bfloat16)
         odd[:cap, cols] = acc[slots:].astype(jnp.bfloat16)
 
 
-def relay_kernel(peers, block, lead_rows, lead, near, odd, mine_across, across, lead_even, lead_odd, *outs):
+def relay_kernel(peers, block, lead_rows, even, odd, mine_across, across, lead_even, odd_out, ends, queries, *far):
     reach = peers // 2
-    even_out, odd_out, ends, queries = outs[:4]
-    far = outs[4:]
     last = (reach - 2) * block
-    even_out[:lead_rows, :] = lead_odd[:lead_rows, :]
-    even_out[lead_rows : lead_rows + block, :] = near[...]
-    even_out[lead_rows + block :, :] = across[:block, :]
-    odd_out[:lead_rows, :] = lead_even[...]
+    odd_out[:lead_rows, :] = lead_even[:lead_rows, :]
     odd_out[lead_rows:, :] = across[last:, :]
     ends[:block, :] = odd[lead_rows:, :]
     ends[block:, :] = across[last:, :]
     for s in range(2, reach - 1):
         far[s - 2][...] = across[(s - 1) * block : s * block, :]
-    queries[:lead_rows, :] = lead[...]
-    queries[lead_rows : 2 * lead_rows, :] = lead_even[...]
+    queries[:lead_rows, :] = even[:lead_rows, :]
+    queries[lead_rows : 2 * lead_rows, :] = lead_even[:lead_rows, :]
     queries[2 * lead_rows :, :] = mine_across[...]
 
 
-def collect_kernel(peers, block, lead_rows, me_ref, mine, odd, asked_y, even2, odd2, ends, lead, lead_even, *rest):
+def pass_kernel(block, lead_rows, even, lead_even, lead_odd, across, even_out, cols):
+    even_out[:lead_rows, :] = lead_odd[:lead_rows, :]
+    even_out[lead_rows:, :] = across[:block, :]
+    for k, rows in enumerate((even, lead_even, lead_odd)):
+        cols[k * lead_rows : (k + 1) * lead_rows, :] = rows[:lead_rows, :]
+
+
+def collect_kernel(peers, block, lead_rows, me_ref, mine, even, odd, asked_y, even2, odd2, ends, *rest):
     reach = peers // 2
-    far, far_across, (own, cols) = rest[: reach - 3], rest[reach - 3 : 2 * reach - 6], rest[-2:]
-    rest = rest[2 * reach - 6 : -2]
+    far, far_across, own = rest[: reach - 3], rest[reach - 3 : 2 * reach - 6], rest[-1]
+    rest = rest[2 * reach - 6 : -1]
     z = me_ref[0] // 2
     at_end = (z == 0) | (z == reach - 1)
 
@@ -150,8 +152,8 @@
 
     put(0, mine)
     put(reach, asked_y, 2 * lead_rows)
-    put(1, even2, lead_rows)
-    put(reach + 1, even2, lead_rows + block)
+    put(1, even, lead_rows)
+    put(reach + 1, even2, lead_rows)
     for s in range(2, reach - 1):
         put(s, far[s - 2])
         put(reach + s, far_across[s - 2])
@@ -159,16 +161,15 @@
     pl.when(jnp.logical_not(at_end))(functools.partial(put_last, odd, odd2, lead_rows, lead_rows))
 
     def keep(slot, src):
-        cols[slot * lead_rows : (slot + 1) * lead_rows, :] = src[:lead_rows, :]
-
-    for slot, src in enumerate((lead, lead_even, odd)):
-        keep(slot, src)
+        at = peers * block + slot * lead_rows
+        own[at : at + lead_rows, :] = src[:lead_rows, :]
+
     if reach == 4:
-        pl.when(at_end)(functools.partial(keep, 3, even2))
-        pl.when(jnp.logical_not(at_end))(functools.partial(keep, 3, odd2))
+        pl.when(at_end)(functools.partial(keep, 0, even2))
+        pl.when(jnp.logical_not(at_end))(functools.partial(keep, 0, odd2))
     else:
         for slot, src in enumerate(rest):
-            keep(3 + slot, src)
+            keep(slot, src)
 
 
 def lead_ids(rows, start, cap):
@@ -194,18 +195,29 @@
     return jnp.max(jnp.where(same, scores, -1.0), axis=0, keepdims=True)
 
 
-def lead_best_kernel(cap, asked, asked_y, cols, cols_other, top):
-    lead_rows = cap + SUB
-    count = cols.shape[0] // lead_rows
-    late = 3 * lead_rows
-    top[...] = jnp.full(top.shape, -1.0, jnp.float32)
+def lead_early_kernel(cap, asked, cols, cols_other, top):
+    best = None
     for columns in (cols, cols_other):
-        ids = lead_column(columns, 0, count, cap)
-        for i, queries in enumerate((asked, asked_y)):
-            best = lead_tops(columns[...], ids, queries, 0, cap, i == 0 and columns is cols)
-            top[i : i + 1, :] = jnp.maximum(top[i : i + 1, :], best)
-            best = lead_tops(columns[late:, :], ids[late:], queries, lead_rows, cap, False)
-            top[2 + i : 3 + i, :] = jnp.maximum(top[2 + i : 3 + i, :], best)
+        ids = lead_column(columns, 0, 3, cap)
+        new = lead_tops(columns[...], ids, asked, 0, cap, columns is cols)
+        best = new if best is None else jnp.maximum(best, new)
+    top[...] = jnp.broadcast_to(best, top.shape)
+
+
+def lead_late(rows, slots, cap, asked, asked_y):
+    count = (rows.shape[0] - slots) // (cap + SUB)
+    ids = lead_column(rows, slots, count, cap)
+    places = ((asked, 0), (asked_y, 0), (asked, cap + SUB), (asked_y, cap + SUB))
+    return [lead_tops(rows[slots:, :], ids, queries, start, cap, False) for queries, start in places]
+
+
+def lead_best_kernel(slots, cap, early, asked, asked_y, near, near_other, own, top):
+    best = lead_late(own, slots, cap, asked, asked_y)
+    best[0] = jnp.maximum(best[0], early[0:1, :])
+    for columns in (near, near_other):
+        new = lead_tops(columns[...], lead_column(columns, 0, 3, cap), asked_y, 0, cap, False)
+        best[1] = jnp.maximum(best[1], new)
+    top[...] = jnp.concatenate(best + [jnp.full((4, cap), -1.0, jnp.float32)], axis=0)
 
 
 def ids_of(rows, peers, block):
@@ -241,7 +253,7 @@
     top[1:2, :] = ids[:, :slots]
 
 
-def far_best_kernel(peers, block, edges, me_ref, own, far, top, lead_top, out, flag):
+def far_best_kernel(peers, block, edges, me_ref, own, far, top, asked, asked_y, lead_top, out, flag):
     width = own.shape[1]
     slots = peers * block
     own_ids, far_ids = top[1:2, :], ids_of(far, peers, block)
@@ -266,7 +278,7 @@
         row = 2 * (row % reach) + (y if k < reach else 1 - y)
         out[row, :, :pitch] = piece[0:1, :pitch]
         out[k, :, pitch:] = none
-    lead = [lead_top[i : i + 1, :] for i in range(4)]
+    lead = [jnp.maximum(lead_top[i : i + 1, :], new) for i, new in enumerate(lead_late(far, slots, cap, asked, asked_y))]
     out[2 * z + y, :, pitch:] = lead[0]
     out[2 * z + 1 - y, :, pitch:] = lead[1]
     if edges:
@@ -390,14 +402,14 @@
     message = shape((lead_rows + block, width), bf16)
     edges = reach == 4
 
-    info, mine, mine_across, lead, near, odd, across, *fars = call(
+    info, mine, mine_across, even, odd, across, *fars = call(
         functools.partial(pack_kernel, peers, cap, block),
         "pack",
-        [shape((8, count), jnp.int32), one, one, shape((lead_rows, width), bf16), one, message]
+        [shape((8, count), jnp.int32), one, one, message, message]
         + [shape(((reach - 1) * block, width), bf16)]
         + [one] * (reach - 3),
         [SMEM, VMEM, pl.BlockSpec(memory_space=pltpu.HBM)],
-        [VMEM] * (4 + reach),
+        [VMEM] * (3 + reach),
         [
             pltpu.VMEM((count, width), f32),
             pltpu.VMEM((count, width), bf16),
@@ -408,30 +420,44 @@
         nbytes=8 * count * width,
     )(me1, cluster_ids.reshape(1, count), embeddings)
     odd1 = lax.ppermute(odd, "dp", odd_pairs)
-    even1 = lax.ppermute(lead, "dp", even_pairs)
+    even1 = lax.ppermute(even, "dp", even_pairs)
     across = lax.ppermute(across, "dp", other_y)
     fars = [lax.ppermute(rows, "dp", pairs) for rows, pairs in zip(fars, shift_pairs)]
-    across, fars, odd1, even1 = lax.optimization_barrier((across, fars, odd1, even1))
-    even2, odd2, ends, asked, *fars_r = call(
+    across, even1 = lax.optimization_barrier((across, even1))
+    odd2, ends, asked, *fars_r = call(
         functools.partial(relay_kernel, peers, block, lead_rows),
         "relay",
-        [
-            shape((lead_rows + 2 * block, width), bf16),
-            message,
-            shape((2 * block, width), bf16),
-            shape((2 * lead_rows + block, width), bf16),
-        ]
-        + [one] * (reach - 3),
-        [VMEM] * 7,
-        [VMEM] * (1 + reach),
+        [message, shape((2 * block, width), bf16), shape((2 * lead_rows + block, width), bf16)] + [one] * (reach - 3),
+        [VMEM] * 5,
+        [VMEM] * reach,
         nbytes=2 * slots * width,
-    )(lead, near, odd, mine_across, across, even1, odd1)
+    )(even, odd, mine_across, across, even1)
     odd2 = lax.ppermute(odd2, "dp", odd_pairs)
+    asked_y = lax.ppermute(asked, "dp", other_y)
+    odd1, fars, ends, fars_r, across = lax.optimization_barrier((odd1, fars, ends, fars_r, across))
+    even2, near_cols = call(
+        functools.partial(pass_kernel, block, lead_rows),
+        "pass_on",
+        [message, shape((3 * lead_rows, width), bf16)],
+        [VMEM] * 4,
+        [VMEM] * 2,
+        nbytes=8 * lead_rows * width,
+    )(even, even1, odd1, across)
     even2 = lax.ppermute(even2, "dp", even_pairs)
+    near_o = lax.ppermute(near_cols, "owner", swap)
+    ends, fars_r, near_o = lax.optimization_barrier((ends, fars_r, near_o))
     ends = lax.ppermute(ends, "dp", ends_pairs)
     fars_r = [lax.ppermute(rows, "dp", pairs) for rows, pairs in zip(fars_r, shift_pairs)]
-    asked_y = lax.ppermute(asked, "dp", other_y)
-    odd2, even2, ends, fars_r, asked_y = lax.optimization_barrier((odd2, even2, ends, fars_r, asked_y))
+    early = call(
+        functools.partial(lead_early_kernel, cap),
+        "lead_early",
+        shape((8, cap), f32),
+        [VMEM] * 3,
+        VMEM,
+        flops=12 * cap * cap * width,
+        nbytes=14 * cap * width,
+    )(asked, near_cols, near_o)
+    odd2, even2, ends, fars_r, asked_y, early = lax.optimization_barrier((odd2, even2, ends, fars_r, asked_y, early))
     late = []
     if not edges:
         is_even = (me // 2) % 2 == 0
@@ -442,25 +468,24 @@
             up = lax.ppermute(up, "dp", up_pairs)
             down = lax.ppermute(down, "dp", down_pairs)
             late += [up, down]
-    own, cols = call(
+    own = call(
         functools.partial(collect_kernel, peers, block, lead_rows),
         "collect",
-        [shape((slots, width), bf16), shape(((3 + max(1, len(late))) * lead_rows, width), bf16)],
-        [SMEM] + [VMEM] * (8 + 2 * (reach - 3) + len(late)),
-        [VMEM] * 2,
+        shape((slots + max(1, len(late)) * lead_rows, width), bf16),
+        [SMEM] + [VMEM] * (7 + 2 * (reach - 3) + len(late)),
+        VMEM,
         nbytes=4 * slots * width,
-    )(me1, mine, odd1, asked_y, even2, odd2, ends, lead, even1, *fars, *fars_r, *late)
-    cols_o = lax.ppermute(cols, "owner", swap)
+    )(me1, mine, even1, odd1, asked_y, even2, odd2, ends, *fars, *fars_r, *late)
     far = lax.ppermute(own, "owner", swap)
     lead_top = call(
-        functools.partial(lead_best_kernel, cap),
+        functools.partial(lead_best_kernel, slots, cap),
         "lead_best",
         shape((8, cap), f32),
-        [VMEM] * 4,
+        [VMEM] * 6,
         VMEM,
         flops=40 * cap * cap * width,
         nbytes=20 * cap * width,
-    )(asked, asked_y, cols, cols_o)
+    )(early, asked, asked_y, near_cols, near_o, own)
     top = call(
         functools.partial(own_best_kernel, peers, block),
         "own_best",
@@ -474,11 +499,11 @@
         functools.partial(far_best_kernel, peers, block, edges),
         "far_best",
         [shape((peers, 1, pitch + cap), f32), shape((8, LANES), f32)],
-        [SMEM] + [VMEM] * 4,
+        [SMEM] + [VMEM] * 6,
         [VMEM] * 2,
         flops=2 * slots * slots * width,
         nbytes=4 * slots * width,
-    )(me1, own, far, top, lead_top)
+    )(me1, own, far, top, asked, asked_y, lead_top)
     back = lax.all_to_all(best, "dp", split_axis=0, concat_axis=0, tiled=True)
     flags = [flag]
     for k in range(1, groups):

time: 105 us -> 103 us (0.981)
  waiting for transfers between devices: 65.7 us -> 62.1 us
    ppermute x2, waiting for transfers between devices: 60.1 us -> 23.5 us  [local(): lax.ppermute(rows, 'dp', pairs)]
    ppermute x1, waiting for transfers between devices: 0.01 us -> 13 us  [local(): even2 = lax.ppermute(even2, 'dp', even_pairs)]
    ppermute x1, waiting for transfers between devices: 0.01 us -> 11.6 us  [local(): across = lax.ppermute(across, 'dp', other_y)]
    ppermute x1, waiting for transfers between devices: 0.01 us -> 9.51 us  [local(): asked_y = lax.ppermute(asked, 'dp', other_y)]
    ppermute x2, starting transfers between devices: 1.05 us -> 3.86 us  [local(): lax.ppermute(rows, 'dp', pairs)]
    ppermute x1, starting transfers between devices: 3.03 us -> 1.59 us  [local(): across = lax.ppermute(across, 'dp', other_y)]
    ppermute x2, waiting for transfers between devices: 1.71 us -> 0.29 us  [the longest x1 0.28 us: local(): even1 = lax.ppermute(even, 'dp', even_pairs)]
    ppermute x1, starting transfers between devices: 0.01 us -> 1.37 us  [local(): even2 = lax.ppermute(even2, 'dp', even_pairs)]
  transfers between devices with their start and end apart: 13 -> 13, of which waited for: 5 -> 9; matrix products, arithmetic and copies ran while one was open for 0% -> 1% of each run, Pallas kernels for 5% -> 5%
where the time goes in v4:
time: 103 us; the launch traced here: 102 us
  waiting for transfers between devices  62.1 us (60%)
  starting transfers between devices  22.6 us (22%)
  Pallas kernels  15.6 us (15%)
  local copies, waits for them, and re-layouts  1.11 us (1%)
    ppermute x2, waiting for transfers between devices, local(): lax.ppermute(rows, 'dp', pairs)  23.5 us
    ppermute x1, waiting for transfers between devices, local(): even2 = lax.ppermute(even2, 'dp', even_pairs)  13 us
    ppermute x1, waiting for transfers between devices, local(): across = lax.ppermute(across, 'dp', other_y)  11.6 us
    ppermute x1, waiting for transfers between devices, local(): asked_y = lax.ppermute(asked, 'dp', other_y)  9.51 us
    pallas_call x1, Pallas kernels, local(): call(functools.partial(pack_kernel, peers, cap, block), 'pack', [shape((8...  5.88 us
    ppermute x1, starting transfers between devices, local(): ends = lax.ppermute(ends, 'dp', ends_pairs)  4.53 us
    ppermute x2, starting transfers between devices, local(): lax.ppermute(rows, 'dp', pairs)  3.86 us
    all_to_all x1, starting transfers between devices, local(): back = lax.all_to_all(best, 'dp', split_axis=0, concat_axis=0, tiled=True)  3.47 us
  transfers between devices with their start and end apart: 13, of which 9 were waited for; matrix products, arithmetic and copies ran while one was open for 1% of the time, Pallas kernels for 5%

profile of v4, /device:TPU:0, one launch (start us, length us, event | category | flops | bytes accessed | tf_op | source)
XLA Modules:
  0.0 102.2 jit_solution(4193556598901129959)
XLA Ops:
  0.0 5.9 %pack.1 = (s32[8,1024]{1,0:T(8,128)S(1)}, bf16[112,1024]{1,0:T(8,128)(2,1)S(1)}, bf16[112,1024]{1,0:T(8,128)(2,1)S(1)}, bf16[384,1024]{1,0:T(8,128)(2,1)S(1)}, b...) custom-call(s32[1]{0:T(128)} %bitcast.8.me_ref, s32[1,1024]{1,0:T(1,128)} %bitcast.47, ...), custom_call_target="tpu_custom_call" | custom-call | flops 2415919104 | bytes 8388608 | tf_op jit(solution)/shard_map/pack/pallas_call | solution.py:405
  5.9 3.1 %collective-permute-start.3 = (bf16[384,1024]{1,0:T(8,128)(2,1)S(1)}, bf16[384,1024]{1,0:T(8,128)(2,1)S(1)}, u32[]{:S(2)}, u32[]{:S(2)}) collective-permute-start(bf16[384,1024]{1,0:T(8,128)(2,1)S(1)} %get-tuple-element.92.even), channel_id=1, source_target_pairs={{0,4},{2,6},{4,0},{6,2},{8,12},{10,14},{12,8},{14,10},{1,5},{3,7},... | collective-permute-start | bytes 2359304 | tf_op jit(solution)/shard_map/ppermute | solution.py:423
  9.0 0.7 collective-permute-start.4
  9.7 1.6 %collective-permute-start.2 = (bf16[336,1024]{1,0:T(8,128)(2,1)S(1)}, bf16[336,1024]{1,0:T(8,128)(2,1)S(1)}, u32[]{:S(2)}, u32[]{:S(2)}) collective-permute-start(bf16[336,1024]{1,0:T(8,128)(2,1)S(1)} %get-tuple-element.91), channel_id=1, source_target_pairs={{0,2},{2,0},{4,6},{6,4},{8,10},{10,8},{12,14},{14,12},{1,3},{3,1},... | collective-permute-start | bytes 2064392 | tf_op jit(solution)/shard_map/ppermute | solution.py:424
  11.3 3.8 %collective-permute-start.5 = (bf16[112,1024]{1,0:T(8,128)(2,1)S(1)}, bf16[112,1024]{1,0:T(8,128)(2,1)S(1)}, u32[]{:S(2)}, u32[]{:S(2)}) collective-permute-start(bf16[112,1024]{1,0:T(8,128)(2,1)S(1)} %get-tuple-element.95), channel_id=1, source_target_pairs={{0,8},{2,10},{4,12},{6,14},{8,0},{10,2},{12,4},{14,6},{1,9},{3,11}... | collective-permute-start | bytes 688136 | tf_op jit(solution)/shard_map/ppermute | solution.py:425
  15.1 11.6 %collective-permute-done.2.across = bf16[336,1024]{1,0:T(8,128)(2,1)S(1)} collective-permute-done((bf16[336,1024]{1,0:T(8,128)(2,1)S(1)}, bf16[336,1024]{1,0:T(8,128)(2,1)S(1)}, u32[]{:S(2)}, u32[]{:S(2)}) %collective-permute-start.2) | collective-permute-done | bytes 688160 | tf_op jit(solution)/shard_map/ppermute | solution.py:424
  26.6 0.3 collective-permute-done.3.lead_even.even
  26.9 0.2 relay.1
  27.1 13.4 %collective-permute-done.5.rest_0_ = bf16[112,1024]{1,0:T(8,128)(2,1)S(1)} collective-permute-done((bf16[112,1024]{1,0:T(8,128)(2,1)S(1)}, bf16[112,1024]{1,0:T(8,128)(2,1)S(1)}, u32[]{:S(2)}, u32[]{:S(2)}) %collective-permute-start.5) | collective-permute-done | bytes 229408 | tf_op jit(solution)/shard_map/ppermute | solution.py:425
  40.5 0.2 pass_on.1
  40.7 0.1 collective-permute-start.8
  40.8 1.6 %collective-permute-start.11 = (bf16[656,1024]{1,0:T(8,128)(2,1)S(1)}, bf16[656,1024]{1,0:T(8,128)(2,1)S(1)}, u32[]{:S(2)}, u32[]{:S(2)}) collective-permute-start(bf16[656,1024]{1,0:T(8,128)(2,1)S(1)} %get-tuple-element.109.asked), channel_id=1, source_target_pairs={{0,2},{2,0},{4,6},{6,4},{8,10},{10,8},{12,14},{14,12},{1,3},{3,1},... | collective-permute-start | bytes 4030472 | tf_op jit(solution)/shard_map/ppermute | solution.py:436
  42.4 0.7 collective-permute-start.6
  43.1 1.4 %collective-permute-start.7 = (bf16[384,1024]{1,0:T(8,128)(2,1)S(1)}, bf16[384,1024]{1,0:T(8,128)(2,1)S(1)}, u32[]{:S(2)}, u32[]{:S(2)}) collective-permute-start(bf16[384,1024]{1,0:T(8,128)(2,1)S(1)} %get-tuple-element.103), channel_id=1, source_target_pairs={{0,4},{2,6},{4,0},{6,2},{8,12},{10,14},{12,8},{14,10},{1,5},{3,7},... | collective-permute-start | bytes 2359304 | tf_op jit(solution)/shard_map/ppermute | solution.py:446
  44.4 4.5 %collective-permute-start.9 = (bf16[224,1024]{1,0:T(8,128)(2,1)S(1)}, bf16[224,1024]{1,0:T(8,128)(2,1)S(1)}, u32[]{:S(2)}, u32[]{:S(2)}) collective-permute-start(bf16[224,1024]{1,0:T(8,128)(2,1)S(1)} %get-tuple-element.107), channel_id=1, source_target_pairs={{0,12},{2,14},{12,0},{14,2},{1,13},{3,15},{13,1},{15,3},{16,28},{1... | collective-permute-start | bytes 1376264 | tf_op jit(solution)/shard_map/ppermute | solution.py:449
  49.0 0.1 collective-permute-start.10
  49.1 1.1 %lead_early.1.early = f32[8,256]{1,0:T(8,128)S(1)} custom-call(bf16[656,1024]{1,0:T(8,128)(2,1)S(1)} %get-tuple-element.109.asked, bf16[816,1024]{1,0:T(8,128)(2,1)S(1)} %get-tuple-element.106.cols.near, bf16[816,1024]{1,0:T(8,128)(2,1)S(1)} %collective-permute-done.8.cols_other.near_other), custom_call_target="tpu_custom_call" | custom-call | flops 805306368 | bytes 3670016 | tf_op jit(solution)/shard_map/lead_early/pallas_call | solution.py:451
  50.2 13.0 %collective-permute-done.7.even2 = bf16[384,1024]{1,0:T(8,128)(2,1)S(1)} collective-permute-done((bf16[384,1024]{1,0:T(8,128)(2,1)S(1)}, bf16[384,1024]{1,0:T(8,128)(2,1)S(1)}, u32[]{:S(2)}, u32[]{:S(2)}) %collective-permute-start.7) | collective-permute-done | bytes 786464 | tf_op jit(solution)/shard_map/ppermute | solution.py:446
  63.2 9.5 %collective-permute-done.11.asked_y = bf16[656,1024]{1,0:T(8,128)(2,1)S(1)} collective-permute-done((bf16[656,1024]{1,0:T(8,128)(2,1)S(1)}, bf16[656,1024]{1,0:T(8,128)(2,1)S(1)}, u32[]{:S(2)}, u32[]{:S(2)}) %collective-permute-start.11) | collective-permute-done | bytes 1343520 | tf_op jit(solution)/shard_map/ppermute | solution.py:436
  72.7 10.1 %collective-permute-done.10.rest_1_ = bf16[112,1024]{1,0:T(8,128)(2,1)S(1)} collective-permute-done((bf16[112,1024]{1,0:T(8,128)(2,1)S(1)}, bf16[112,1024]{1,0:T(8,128)(2,1)S(1)}, u32[]{:S(2)}, u32[]{:S(2)}) %collective-permute-start.10) | collective-permute-done | bytes 229408 | tf_op jit(solution)/shard_map/ppermute | solution.py:450
  82.8 0.2 collect.1.own
  83.0 2.1 %own_best.1.top = f32[8,896]{1,0:T(8,128)S(1)} custom-call(bf16[1168,1024]{1,0:T(8,128)(2,1)S(1)} %collect.1.own), custom_call_target="tpu_custom_call" | custom-call | flops 1644167168 | bytes 1835008 | tf_op jit(solution)/shard_map/own_best/pallas_call | solution.py:489
  85.2 1.7 %lead_best.1.lead_top = f32[8,256]{1,0:T(8,128)S(1)} custom-call(f32[8,256]{1,0:T(8,128)S(1)} %lead_early.1.early, bf16[656,1024]{1,0:T(8,128)(2,1)S(1)} %get-tuple-element.109.asked, bf16[656,1024]{1,0:T(8,128)(2,1)S(1)} %collective-permute-done.11.asked_y, bf16[816,1024]{1,0:T(8,128)(2,1)S(1)} %get-tuple-element.106.cols.near, ...), custom_call_target="tpu_custom_call" | custom-call | flops 2684354560 | bytes 5242880 | tf_op jit(solution)/shard_map/lead_best/pallas_call | solution.py:480
  86.9 0.7 collective-permute-done.12.far
  87.6 3.4 %far_best.1 = (f32[8,1,384]{2,1,0:T(1,128)}, f32[8,128]{1,0:T(8,128)S(1)}) custom-call(s32[1]{0:T(128)} %bitcast.8.me_ref, bf16[1168,1024]{1,0:T(8,128)(2,1)S(1)} %collect.1.own, bf16[1168,1024]{1,0:T(8,128)(2,1)S(1)} %collective-permute-done.12.far, f32[8,896]{1,0:T(8,128)S(1)} %own_best.1.top, bf16[656,1024]{1,0:T(8,128)(2,1)S(1)} %get-tuple-element.109.asked, ...), custom_call_target="tpu_custom_call" | custom-call | flops 1644167168 | bytes 3670016 | tf_op jit(solution)/shard_map/far_best/pallas_call | solution.py:498
  91.0 3.5 %all-to-all-start.3 = ((f32[8,1,384]{2,1,0:T(1,128)}), f32[8,1,384]{2,1,0:T(1,128)S(1)}, u32[]{:S(2)}, u32[]{:S(2)}) async-start(f32[8,1,384]{2,1,0:T(1,128)} %get-tuple-element.120), calls=%async_computation.3 | async-start | bytes 24576 | tf_op jit(solution)/shard_map/all_to_all | solution.py:507
  94.4 1.6 %collective-permute-start.13 = (f32[8,128]{1,0:T(8,128)S(1)}, f32[8,128]{1,0:T(8,128)S(1)}, u32[]{:S(2)}, u32[]{:S(2)}) collective-permute-start(f32[8,128]{1,0:T(8,128)S(1)} %get-tuple-element.118), channel_id=1, source_target_pairs={{0,16},{16,0},{1,17},{17,1},{2,18},{18,2},{3,19},{19,3},{4,20},{20... | collective-permute-start | bytes 12296 | tf_op jit(solution)/shard_map/ppermute | solution.py:510
  96.0 2.1 %collective-permute-done.13 = f32[8,128]{1,0:T(8,128)S(1)} collective-permute-done((f32[8,128]{1,0:T(8,128)S(1)}, f32[8,128]{1,0:T(8,128)S(1)}, u32[]{:S(2)}, u32[]{:S(2)}) %collective-permute-start.13) | collective-permute-done | bytes 4128 | tf_op jit(solution)/shard_map/ppermute | solution.py:510
  98.1 0.5 slice.9
  99.3 1.5 %all-to-all-done.3.back_ref = f32[8,1,384]{2,1,0:T(1,128)S(1)} async-done(((f32[8,1,384]{2,1,0:T(1,128)}), f32[8,1,384]{2,1,0:T(1,128)S(1)}, u32[]{:S(2)}, u32[]{:S(2)}) %all-to-all-start.3) | async-done | bytes 12320 | tf_op jit(solution)/shard_map/all_to_all | solution.py:507
  100.8 0.9 final.1
  101.7 0.6 copy-done.1
  (10 shorter events, 0.1 us)
Async XLA Ops:
  5.9 21.0 %collective-permute-start.3 = (bf16[384,1024]{1,0:T(8,128)(2,1)S(1)}, bf16[384,1024]{1,0:T(8,128)(2,1)S(1)}, u32[]{:S(2)}, u32[]{:S(2)}) collective-permute-start(bf16[384,1024]{1,0:T(8,128)(2,1)S(1)} %get-tuple-element.92.even), channel_id=1, source_target_pairs={{0,4},{2,6},{4,0},{6,2},{8,12},{10,14},{12,8},{14,10},{1,5},{3,7},... | collective-permute-start | bytes 2359304 | tf_op jit(solution)/shard_map/ppermute | solution.py:423
  9.0 31.6 %collective-permute-start.4 = (bf16[384,1024]{1,0:T(8,128)(2,1)S(1)}, bf16[384,1024]{1,0:T(8,128)(2,1)S(1)}, u32[]{:S(2)}, u32[]{:S(2)}) collective-permute-start(bf16[384,1024]{1,0:T(8,128)(2,1)S(1)} %get-tuple-element.94.odd), channel_id=1, source_target_pairs={{4,8},{6,10},{8,4},{10,6},{5,9},{7,11},{9,5},{11,7},{20,24},{22,26... | collective-permute-start | bytes 2359304 | tf_op jit(solution)/shard_map/ppermute | solution.py:422
  9.7 17.0 %collective-permute-start.2 = (bf16[336,1024]{1,0:T(8,128)(2,1)S(1)}, bf16[336,1024]{1,0:T(8,128)(2,1)S(1)}, u32[]{:S(2)}, u32[]{:S(2)}) collective-permute-start(bf16[336,1024]{1,0:T(8,128)(2,1)S(1)} %get-tuple-element.91), channel_id=1, source_target_pairs={{0,2},{2,0},{4,6},{6,4},{8,10},{10,8},{12,14},{14,12},{1,3},{3,1},... | collective-permute-start | bytes 2064392 | tf_op jit(solution)/shard_map/ppermute | solution.py:424
  11.3 29.3 %collective-permute-start.5 = (bf16[112,1024]{1,0:T(8,128)(2,1)S(1)}, bf16[112,1024]{1,0:T(8,128)(2,1)S(1)}, u32[]{:S(2)}, u32[]{:S(2)}) collective-permute-start(bf16[112,1024]{1,0:T(8,128)(2,1)S(1)} %get-tuple-element.95), channel_id=1, source_target_pairs={{0,8},{2,10},{4,12},{6,14},{8,0},{10,2},{12,4},{14,6},{1,9},{3,11}... | collective-permute-start | bytes 688136 | tf_op jit(solution)/shard_map/ppermute | solution.py:425
  40.7 3.7 %collective-permute-start.8 = (bf16[816,1024]{1,0:T(8,128)(2,1)S(1)}, bf16[816,1024]{1,0:T(8,128)(2,1)S(1)}, u32[]{:S(2)}, u32[]{:S(2)}) collective-permute-start(bf16[816,1024]{1,0:T(8,128)(2,1)S(1)} %get-tuple-element.106.cols.near), channel_id=1, source_target_pairs={{0,1},{1,0},{2,3},{3,2},{4,5},{5,4},{6,7},{7,6},{8,9},{9,8},{10,11... | collective-permute-start | bytes 5013512 | tf_op jit(solution)/shard_map/ppermute | solution.py:447
  40.8 31.9 %collective-permute-start.11 = (bf16[656,1024]{1,0:T(8,128)(2,1)S(1)}, bf16[656,1024]{1,0:T(8,128)(2,1)S(1)}, u32[]{:S(2)}, u32[]{:S(2)}) collective-permute-start(bf16[656,1024]{1,0:T(8,128)(2,1)S(1)} %get-tuple-element.109.asked), channel_id=1, source_target_pairs={{0,2},{2,0},{4,6},{6,4},{8,10},{10,8},{12,14},{14,12},{1,3},{3,1},... | collective-permute-start | bytes 4030472 | tf_op jit(solution)/shard_map/ppermute | solution.py:436
  42.4 7.8 %collective-permute-start.6 = (bf16[384,1024]{1,0:T(8,128)(2,1)S(1)}, bf16[384,1024]{1,0:T(8,128)(2,1)S(1)}, u32[]{:S(2)}, u32[]{:S(2)}) collective-permute-start(bf16[384,1024]{1,0:T(8,128)(2,1)S(1)} %get-tuple-element.101), channel_id=1, source_target_pairs={{4,8},{6,10},{8,4},{10,6},{5,9},{7,11},{9,5},{11,7},{20,24},{22,26... | collective-permute-start | bytes 2359304 | tf_op jit(solution)/shard_map/ppermute | solution.py:435
  43.1 20.1 %collective-permute-start.7 = (bf16[384,1024]{1,0:T(8,128)(2,1)S(1)}, bf16[384,1024]{1,0:T(8,128)(2,1)S(1)}, u32[]{:S(2)}, u32[]{:S(2)}) collective-permute-start(bf16[384,1024]{1,0:T(8,128)(2,1)S(1)} %get-tuple-element.103), channel_id=1, source_target_pairs={{0,4},{2,6},{4,0},{6,2},{8,12},{10,14},{12,8},{14,10},{1,5},{3,7},... | collective-permute-start | bytes 2359304 | tf_op jit(solution)/shard_map/ppermute | solution.py:446
  44.4 38.3 %collective-permute-start.9 = (bf16[224,1024]{1,0:T(8,128)(2,1)S(1)}, bf16[224,1024]{1,0:T(8,128)(2,1)S(1)}, u32[]{:S(2)}, u32[]{:S(2)}) collective-permute-start(bf16[224,1024]{1,0:T(8,128)(2,1)S(1)} %get-tuple-element.107), channel_id=1, source_target_pairs={{0,12},{2,14},{12,0},{14,2},{1,13},{3,15},{13,1},{15,3},{16,28},{1... | collective-permute-start | bytes 1376264 | tf_op jit(solution)/shard_map/ppermute | solution.py:449
  49.0 33.8 %collective-permute-start.10 = (bf16[112,1024]{1,0:T(8,128)(2,1)S(1)}, bf16[112,1024]{1,0:T(8,128)(2,1)S(1)}, u32[]{:S(2)}, u32[]{:S(2)}) collective-permute-start(bf16[112,1024]{1,0:T(8,128)(2,1)S(1)} %get-tuple-element.108), channel_id=1, source_target_pairs={{0,8},{2,10},{4,12},{6,14},{8,0},{10,2},{12,4},{14,6},{1,9},{3,11}... | collective-permute-start | bytes 688136 | tf_op jit(solution)/shard_map/ppermute | solution.py:450
  82.9 4.6 %collective-permute-start.12 = (bf16[1168,1024]{1,0:T(8,128)(2,1)S(1)}, bf16[1168,1024]{1,0:T(8,128)(2,1)S(1)}, u32[]{:S(2)}, u32[]{:S(2)}) collective-permute-start(bf16[1168,1024]{1,0:T(8,128)(2,1)S(1)} %collect.1.own), channel_id=1, source_target_pairs={{0,1},{1,0},{2,3},{3,2},{4,5},{5,4},{6,7},{7,6},{8,9},{9,8},{10,11... | collective-permute-start | bytes 7176200 | tf_op jit(solution)/shard_map/ppermute | solution.py:479
  86.9 14.7 %copy-start = (s32[1024]{0:T(1024)S(1)}, s32[1024]{0:T(1024)}, u32[]{:S(2)}) copy-start(s32[1024]{0:T(1024)} %param.7) | copy-start | bytes 12292
  91.0 9.8 %all-to-all-start.3 = ((f32[8,1,384]{2,1,0:T(1,128)}), f32[8,1,384]{2,1,0:T(1,128)S(1)}, u32[]{:S(2)}, u32[]{:S(2)}) async-start(f32[8,1,384]{2,1,0:T(1,128)} %get-tuple-element.120), calls=%async_computation.3 | async-start | bytes 24576 | tf_op jit(solution)/shard_map/all_to_all | solution.py:507
  94.4 3.7 %collective-permute-start.13 = (f32[8,128]{1,0:T(8,128)S(1)}, f32[8,128]{1,0:T(8,128)S(1)}, u32[]{:S(2)}, u32[]{:S(2)}) collective-permute-start(f32[8,128]{1,0:T(8,128)S(1)} %get-tuple-element.118), channel_id=1, source_target_pairs={{0,16},{16,0},{1,17},{17,1},{2,18},{18,2},{3,19},{19,3},{4,20},{20... | collective-permute-start | bytes 12296 | tf_op jit(solution)/shard_map/ppermute | solution.py:510
  101.6 0.6 copy-start.1

commit v5 on v4

--- a/solution.py
+++ b/solution.py
@@ -115,11 +115,13 @@
         odd[:cap, cols] = acc[slots:].astype(jnp.bfloat16)
 
 
-def relay_kernel(peers, block, lead_rows, even, odd, mine_across, across, lead_even, odd_out, ends, queries, *far):
+def relay_kernel(peers, block, lead_rows, even, odd, mine_across, across, lead_even, odd_out, ends, queries, cols, *far):
     reach = peers // 2
     last = (reach - 2) * block
     odd_out[:lead_rows, :] = lead_even[:lead_rows, :]
     odd_out[lead_rows:, :] = across[last:, :]
+    cols[:lead_rows, :] = even[:lead_rows, :]
+    cols[lead_rows:, :] = lead_even[:lead_rows, :]
     ends[:block, :] = odd[lead_rows:, :]
     ends[block:, :] = across[last:, :]
     for s in range(2, reach - 1):
@@ -129,11 +131,9 @@
     queries[2 * lead_rows :, :] = mine_across[...]
 
 
-def pass_kernel(block, lead_rows, even, lead_even, lead_odd, across, even_out, cols):
+def pass_kernel(block, lead_rows, lead_odd, across, even_out):
     even_out[:lead_rows, :] = lead_odd[:lead_rows, :]
     even_out[lead_rows:, :] = across[:block, :]
-    for k, rows in enumerate((even, lead_even, lead_odd)):
-        cols[k * lead_rows : (k + 1) * lead_rows, :] = rows[:lead_rows, :]
 
 
 def collect_kernel(peers, block, lead_rows, me_ref, mine, even, odd, asked_y, even2, odd2, ends, *rest):
@@ -164,6 +164,7 @@
         at = peers * block + slot * lead_rows
         own[at : at + lead_rows, :] = src[:lead_rows, :]
 
+    keep((own.shape[0] - peers * block) // lead_rows - 1, odd)
     if reach == 4:
         pl.when(at_end)(functools.partial(keep, 0, even2))
         pl.when(jnp.logical_not(at_end))(functools.partial(keep, 0, odd2))
@@ -195,13 +196,14 @@
     return jnp.max(jnp.where(same, scores, -1.0), axis=0, keepdims=True)
 
 
-def lead_early_kernel(cap, asked, cols, cols_other, top):
-    best = None
+def lead_early_kernel(cap, asked, asked_y, cols, cols_other, top):
+    best = [jnp.full((1, cap), -1.0, jnp.float32)] * 8
     for columns in (cols, cols_other):
-        ids = lead_column(columns, 0, 3, cap)
-        new = lead_tops(columns[...], ids, asked, 0, cap, columns is cols)
-        best = new if best is None else jnp.maximum(best, new)
-    top[...] = jnp.broadcast_to(best, top.shape)
+        ids = lead_column(columns, 0, 2, cap)
+        for i, queries in enumerate((asked, asked_y)):
+            new = lead_tops(columns[...], ids, queries, 0, cap, i == 0 and columns is cols)
+            best[i] = jnp.maximum(best[i], new)
+    top[...] = jnp.concatenate(best, axis=0)
 
 
 def lead_late(rows, slots, cap, asked, asked_y):
@@ -211,12 +213,9 @@
     return [lead_tops(rows[slots:, :], ids, queries, start, cap, False) for queries, start in places]
 
 
-def lead_best_kernel(slots, cap, early, asked, asked_y, near, near_other, own, top):
-    best = lead_late(own, slots, cap, asked, asked_y)
-    best[0] = jnp.maximum(best[0], early[0:1, :])
-    for columns in (near, near_other):
-        new = lead_tops(columns[...], lead_column(columns, 0, 3, cap), asked_y, 0, cap, False)
-        best[1] = jnp.maximum(best[1], new)
+def lead_best_kernel(slots, cap, early, asked, asked_y, own, top):
+    late = lead_late(own, slots, cap, asked, asked_y)
+    best = [jnp.maximum(early[i : i + 1, :], new) for i, new in enumerate(late)]
     top[...] = jnp.concatenate(best + [jnp.full((4, cap), -1.0, jnp.float32)], axis=0)
 
 
@@ -423,40 +422,45 @@
     even1 = lax.ppermute(even, "dp", even_pairs)
     across = lax.ppermute(across, "dp", other_y)
     fars = [lax.ppermute(rows, "dp", pairs) for rows, pairs in zip(fars, shift_pairs)]
-    across, even1 = lax.optimization_barrier((across, even1))
-    odd2, ends, asked, *fars_r = call(
+    across, even1, fars = lax.optimization_barrier((across, even1, fars))
+    odd2, ends, asked, near_cols, *fars_r = call(
         functools.partial(relay_kernel, peers, block, lead_rows),
         "relay",
-        [message, shape((2 * block, width), bf16), shape((2 * lead_rows + block, width), bf16)] + [one] * (reach - 3),
+        [
+            message,
+            shape((2 * block, width), bf16),
+            shape((2 * lead_rows + block, width), bf16),
+            shape((2 * lead_rows, width), bf16),
+        ]
+        + [one] * (reach - 3),
         [VMEM] * 5,
-        [VMEM] * reach,
+        [VMEM] * (1 + reach),
         nbytes=2 * slots * width,
     )(even, odd, mine_across, across, even1)
     odd2 = lax.ppermute(odd2, "dp", odd_pairs)
     asked_y = lax.ppermute(asked, "dp", other_y)
-    odd1, fars, ends, fars_r, across = lax.optimization_barrier((odd1, fars, ends, fars_r, across))
-    even2, near_cols = call(
+    near_o = lax.ppermute(near_cols, "owner", swap)
+    even2 = call(
         functools.partial(pass_kernel, block, lead_rows),
         "pass_on",
-        [message, shape((3 * lead_rows, width), bf16)],
-        [VMEM] * 4,
+        message,
         [VMEM] * 2,
+        VMEM,
         nbytes=8 * lead_rows * width,
-    )(even, even1, odd1, across)
+    )(odd1, across)
     even2 = lax.ppermute(even2, "dp", even_pairs)
-    near_o = lax.ppermute(near_cols, "owner", swap)
-    ends, fars_r, near_o = lax.optimization_barrier((ends, fars_r, near_o))
     ends = lax.ppermute(ends, "dp", ends_pairs)
     fars_r = [lax.ppermute(rows, "dp", pairs) for rows, pairs in zip(fars_r, shift_pairs)]
+    odd2, asked_y, near_cols, near_o = lax.optimization_barrier((odd2, asked_y, near_cols, near_o))
     early = call(
         functools.partial(lead_early_kernel, cap),
         "lead_early",
         shape((8, cap), f32),
-        [VMEM] * 3,
+        [VMEM] * 4,
         VMEM,
-        flops=12 * cap * cap * width,
+        flops=24 * cap * cap * width,
         nbytes=14 * cap * width,
-    )(asked, near_cols, near_o)
+    )(asked, asked_y, near_cols, near_o)
     odd2, even2, ends, fars_r, asked_y, early = lax.optimization_barrier((odd2, even2, ends, fars_r, asked_y, early))
     late = []
     if not edges:
@@ -471,7 +475,7 @@
     own = call(
         functools.partial(collect_kernel, peers, block, lead_rows),
         "collect",
-        shape((slots + max(1, len(late)) * lead_rows, width), bf16),
+        shape((slots + (1 + max(1, len(late))) * lead_rows, width), bf16),
         [SMEM] + [VMEM] * (7 + 2 * (reach - 3) + len(late)),
         VMEM,
         nbytes=4 * slots * width,
@@ -481,11 +485,11 @@
         functools.partial(lead_best_kernel, slots, cap),
         "lead_best",
         shape((8, cap), f32),
-        [VMEM] * 6,
+        [VMEM] * 4,
         VMEM,
         flops=40 * cap * cap * width,
         nbytes=20 * cap * width,
-    )(early, asked, asked_y, near_cols, near_o, own)
+    )(early, asked, asked_y, own)
     top = call(
         functools.partial(own_best_kernel, peers, block),
         "own_best",

time: 103 us -> 99 us (0.961)
  waiting for transfers between devices: 62.1 us -> 39.3 us
  starting transfers between devices: 22.6 us -> 41.3 us
    ppermute x2, starting transfers between devices: 3.86 us -> 17.1 us  [local(): lax.ppermute(rows, 'dp', pairs)]
    ppermute x1, waiting for transfers between devices: 13 us -> 0.01 us  [local(): even2 = lax.ppermute(even2, 'dp', even_pairs)]
    ppermute x1, waiting for transfers between devices: 11.6 us -> 0.01 us  [local(): across = lax.ppermute(across, 'dp', other_y)]
    ppermute x2, waiting for transfers between devices: 23.5 us -> 30.7 us  [local(): lax.ppermute(rows, 'dp', pairs)]
    ppermute x1, waiting for transfers between devices: 9.51 us -> 2.35 us  [local(): asked_y = lax.ppermute(asked, 'dp', other_y)]
    ppermute x1, starting transfers between devices: 1.37 us -> 6.45 us  [local(): even2 = lax.ppermute(even2, 'dp', even_pairs)]
    ppermute x1, waiting for transfers between devices: 0.69 us -> 1.81 us  [local(): far = lax.ppermute(own, 'owner', swap)]
  transfers between devices with their start and end apart: 13 -> 13, of which waited for: 9 -> 7; matrix products, arithmetic and copies ran while one was open for 1% -> 1% of each run, Pallas kernels for 5% -> 5%
where the time goes in v5:
time: 99 us; the launch traced here: 98.7 us
  starting transfers between devices  41.3 us (42%)
  waiting for transfers between devices  39.3 us (40%)
  Pallas kernels  16.1 us (16%)
  local copies, waits for them, and re-layouts  1.11 us (1%)
    ppermute x2, waiting for transfers between devices, local(): lax.ppermute(rows, 'dp', pairs)  30.7 us
    ppermute x2, starting transfers between devices, local(): lax.ppermute(rows, 'dp', pairs)  17.1 us
    ppermute x1, starting transfers between devices, local(): even2 = lax.ppermute(even2, 'dp', even_pairs)  6.45 us
    pallas_call x1, Pallas kernels, local(): call(functools.partial(pack_kernel, peers, cap, block), 'pack', [shape((8...  5.88 us
    ppermute x1, starting transfers between devices, local(): ends = lax.ppermute(ends, 'dp', ends_pairs)  4.85 us
    pallas_call x1, Pallas kernels, local(): call(functools.partial(far_best_kernel, peers, block, edges), 'far_best',...  3.94 us
    all_to_all x1, starting transfers between devices, local(): back = lax.all_to_all(best, 'dp', split_axis=0, concat_axis=0, tiled=True)  3.5 us
    ppermute x1, starting transfers between devices, local(): even1 = lax.ppermute(even, 'dp', even_pairs)  3.08 us
  transfers between devices with their start and end apart: 13, of which 7 were waited for; matrix products, arithmetic and copies ran while one was open for 1% of the time, Pallas kernels for 5%

profile of v5, /device:TPU:0, one launch (start us, length us, event | category | flops | bytes accessed | tf_op | source)
XLA Modules:
  0.0 98.7 jit_solution(9486662189887891937)
XLA Ops:
  0.0 5.9 %pack.1 = (s32[8,1024]{1,0:T(8,128)S(1)}, bf16[112,1024]{1,0:T(8,128)(2,1)S(1)}, bf16[112,1024]{1,0:T(8,128)(2,1)S(1)}, bf16[384,1024]{1,0:T(8,128)(2,1)S(1)}, b...) custom-call(s32[1]{0:T(128)} %bitcast.8.me_ref, s32[1,1024]{1,0:T(1,128)} %bitcast.47, ...), custom_call_target="tpu_custom_call" | custom-call | flops 2415919104 | bytes 8388608 | tf_op jit(solution)/shard_map/pack/pallas_call | solution.py:404
  5.9 3.1 %collective-permute-start.3 = (bf16[384,1024]{1,0:T(8,128)(2,1)S(1)}, bf16[384,1024]{1,0:T(8,128)(2,1)S(1)}, u32[]{:S(2)}, u32[]{:S(2)}) collective-permute-start(bf16[384,1024]{1,0:T(8,128)(2,1)S(1)} %get-tuple-element.88.even), channel_id=1, source_target_pairs={{0,4},{2,6},{4,0},{6,2},{8,12},{10,14},{12,8},{14,10},{1,5},{3,7},... | collective-permute-start | bytes 2359304 | tf_op jit(solution)/shard_map/ppermute | solution.py:422
  9.0 1.5 %collective-permute-start.2 = (bf16[336,1024]{1,0:T(8,128)(2,1)S(1)}, bf16[336,1024]{1,0:T(8,128)(2,1)S(1)}, u32[]{:S(2)}, u32[]{:S(2)}) collective-permute-start(bf16[336,1024]{1,0:T(8,128)(2,1)S(1)} %get-tuple-element.87), channel_id=1, source_target_pairs={{0,2},{2,0},{4,6},{6,4},{8,10},{10,8},{12,14},{14,12},{1,3},{3,1},... | collective-permute-start | bytes 2064392 | tf_op jit(solution)/shard_map/ppermute | solution.py:423
  10.5 2.6 %collective-permute-start.4 = (bf16[112,1024]{1,0:T(8,128)(2,1)S(1)}, bf16[112,1024]{1,0:T(8,128)(2,1)S(1)}, u32[]{:S(2)}, u32[]{:S(2)}) collective-permute-start(bf16[112,1024]{1,0:T(8,128)(2,1)S(1)} %get-tuple-element.89), channel_id=1, source_target_pairs={{0,8},{2,10},{4,12},{6,14},{8,0},{10,2},{12,4},{14,6},{1,9},{3,11}... | collective-permute-start | bytes 688136 | tf_op jit(solution)/shard_map/ppermute | solution.py:424
  13.1 0.7 collective-permute-start.5
  13.8 16.9 %collective-permute-done.4.rest_0_ = bf16[112,1024]{1,0:T(8,128)(2,1)S(1)} collective-permute-done((bf16[112,1024]{1,0:T(8,128)(2,1)S(1)}, bf16[112,1024]{1,0:T(8,128)(2,1)S(1)}, u32[]{:S(2)}, u32[]{:S(2)}) %collective-permute-start.4) | collective-permute-done | bytes 229408 | tf_op jit(solution)/shard_map/ppermute | solution.py:424
  30.7 0.7 collective-permute-done.3.lead_even.even
  31.4 0.3 relay.1
  31.7 1.8 %collective-permute-start.7 = (bf16[656,1024]{1,0:T(8,128)(2,1)S(1)}, bf16[656,1024]{1,0:T(8,128)(2,1)S(1)}, u32[]{:S(2)}, u32[]{:S(2)}) collective-permute-start(bf16[656,1024]{1,0:T(8,128)(2,1)S(1)} %get-tuple-element.95.asked), channel_id=1, source_target_pairs={{0,2},{2,0},{4,6},{6,4},{8,10},{10,8},{12,14},{14,12},{1,3},{3,1},... | collective-permute-start | bytes 4030472 | tf_op jit(solution)/shard_map/ppermute | solution.py:441
  33.4 0.7 collective-permute-start.6
  34.2 0.1 pass_on.1
  34.2 6.5 %collective-permute-start.9 = (bf16[384,1024]{1,0:T(8,128)(2,1)S(1)}, bf16[384,1024]{1,0:T(8,128)(2,1)S(1)}, u32[]{:S(2)}, u32[]{:S(2)}) collective-permute-start(bf16[384,1024]{1,0:T(8,128)(2,1)S(1)} %pass_on.1), channel_id=1, source_target_pairs={{0,4},{2,6},{4,0},{6,2},{8,12},{10,14},{12,8},{14,10},{1,5},{3,7},... | collective-permute-start | bytes 2359304 | tf_op jit(solution)/shard_map/ppermute | solution.py:451
  40.7 4.8 %collective-permute-start.10 = (bf16[224,1024]{1,0:T(8,128)(2,1)S(1)}, bf16[224,1024]{1,0:T(8,128)(2,1)S(1)}, u32[]{:S(2)}, u32[]{:S(2)}) collective-permute-start(bf16[224,1024]{1,0:T(8,128)(2,1)S(1)} %get-tuple-element.98), channel_id=1, source_target_pairs={{0,12},{2,14},{12,0},{14,2},{1,13},{3,15},{13,1},{15,3},{16,28},{1... | collective-permute-start | bytes 1376264 | tf_op jit(solution)/shard_map/ppermute | solution.py:452
  45.5 14.5 %collective-permute-start.11 = (bf16[112,1024]{1,0:T(8,128)(2,1)S(1)}, bf16[112,1024]{1,0:T(8,128)(2,1)S(1)}, u32[]{:S(2)}, u32[]{:S(2)}) collective-permute-start(bf16[112,1024]{1,0:T(8,128)(2,1)S(1)} %get-tuple-element.99), channel_id=1, source_target_pairs={{0,8},{2,10},{4,12},{6,14},{8,0},{10,2},{12,4},{14,6},{1,9},{3,11}... | collective-permute-start | bytes 688136 | tf_op jit(solution)/shard_map/ppermute | solution.py:453
  60.1 2.4 %collective-permute-done.7.asked_y = bf16[656,1024]{1,0:T(8,128)(2,1)S(1)} collective-permute-done((bf16[656,1024]{1,0:T(8,128)(2,1)S(1)}, bf16[656,1024]{1,0:T(8,128)(2,1)S(1)}, u32[]{:S(2)}, u32[]{:S(2)}) %collective-permute-start.7) | collective-permute-done | bytes 1343520 | tf_op jit(solution)/shard_map/ppermute | solution.py:441
  62.4 1.4 %lead_early.1.early = f32[8,256]{1,0:T(8,128)S(1)} custom-call(bf16[656,1024]{1,0:T(8,128)(2,1)S(1)} %get-tuple-element.95.asked, bf16[656,1024]{1,0:T(8,128)(2,1)S(1)} %collective-permute-done.7.asked_y, bf16[544,1024]{1,0:T(8,128)(2,1)S(1)} %get-tuple-element.101.cols, bf16[544,1024]{1,0:T(8,128)(2,1)S(1)} %collective-permute-done.8.cols_other), custom_call_target="tpu_custom_call" | custom-call | flops 1610612736 | bytes 3670016 | tf_op jit(solution)/shard_map/lead_early/pallas_call | solution.py:455
  63.8 13.8 %collective-permute-done.11.rest_1_ = bf16[112,1024]{1,0:T(8,128)(2,1)S(1)} collective-permute-done((bf16[112,1024]{1,0:T(8,128)(2,1)S(1)}, bf16[112,1024]{1,0:T(8,128)(2,1)S(1)}, u32[]{:S(2)}, u32[]{:S(2)}) %collective-permute-start.11) | collective-permute-done | bytes 229408 | tf_op jit(solution)/shard_map/ppermute | solution.py:453
  77.6 0.2 collect.1.own
  77.8 0.1 collective-permute-start.12
  77.9 2.1 %own_best.1.top = f32[8,896]{1,0:T(8,128)S(1)} custom-call(bf16[1440,1024]{1,0:T(8,128)(2,1)S(1)} %collect.1.own), custom_call_target="tpu_custom_call" | custom-call | flops 1644167168 | bytes 1835008 | tf_op jit(solution)/shard_map/own_best/pallas_call | solution.py:493
  80.0 1.4 %lead_best.1.lead_top = f32[8,256]{1,0:T(8,128)S(1)} custom-call(f32[8,256]{1,0:T(8,128)S(1)} %lead_early.1.early, bf16[656,1024]{1,0:T(8,128)(2,1)S(1)} %get-tuple-element.95.asked, bf16[656,1024]{1,0:T(8,128)(2,1)S(1)} %collective-permute-done.7.asked_y, bf16[1440,1024]{1,0:T(8,128)(2,1)S(1)} %collect.1.own), custom_call_target="tpu_custom_call" | custom-call | flops 2684354560 | bytes 5242880 | tf_op jit(solution)/shard_map/lead_best/pallas_call | solution.py:484
  81.4 0.0 copy-start
  81.4 1.8 %collective-permute-done.12.far = bf16[1440,1024]{1,0:T(8,128)(2,1)S(1)} collective-permute-done((bf16[1440,1024]{1,0:T(8,128)(2,1)S(1)}, bf16[1440,1024]{1,0:T(8,128)(2,1)S(1)}, u32[]{:S(2)}, u32[]{:S(2)}) %collective-permute-start.12) | collective-permute-done | bytes 2949152 | tf_op jit(solution)/shard_map/ppermute | solution.py:483
  83.3 3.9 %far_best.1 = (f32[8,1,384]{2,1,0:T(1,128)}, f32[8,128]{1,0:T(8,128)S(1)}) custom-call(s32[1]{0:T(128)} %bitcast.8.me_ref, bf16[1440,1024]{1,0:T(8,128)(2,1)S(1)} %collect.1.own, bf16[1440,1024]{1,0:T(8,128)(2,1)S(1)} %collective-permute-done.12.far, f32[8,896]{1,0:T(8,128)S(1)} %own_best.1.top, bf16[656,1024]{1,0:T(8,128)(2,1)S(1)} %get-tuple-element.95.asked, ...), custom_call_target="tpu_custom_call" | custom-call | flops 1644167168 | bytes 3670016 | tf_op jit(solution)/shard_map/far_best/pallas_call | solution.py:502
  87.2 3.5 %all-to-all-start.3 = ((f32[8,1,384]{2,1,0:T(1,128)}), f32[8,1,384]{2,1,0:T(1,128)S(1)}, u32[]{:S(2)}, u32[]{:S(2)}) async-start(f32[8,1,384]{2,1,0:T(1,128)} %get-tuple-element.112), calls=%async_computation.3 | async-start | bytes 24576 | tf_op jit(solution)/shard_map/all_to_all | solution.py:511
  90.7 1.5 %collective-permute-start.13 = (f32[8,128]{1,0:T(8,128)S(1)}, f32[8,128]{1,0:T(8,128)S(1)}, u32[]{:S(2)}, u32[]{:S(2)}) collective-permute-start(f32[8,128]{1,0:T(8,128)S(1)} %get-tuple-element.110), channel_id=1, source_target_pairs={{0,16},{16,0},{1,17},{17,1},{2,18},{18,2},{3,19},{19,3},{4,20},{20... | collective-permute-start | bytes 12296 | tf_op jit(solution)/shard_map/ppermute | solution.py:514
  92.2 2.1 %collective-permute-done.13 = f32[8,128]{1,0:T(8,128)S(1)} collective-permute-done((f32[8,128]{1,0:T(8,128)S(1)}, f32[8,128]{1,0:T(8,128)S(1)}, u32[]{:S(2)}, u32[]{:S(2)}) %collective-permute-start.13) | collective-permute-done | bytes 4128 | tf_op jit(solution)/shard_map/ppermute | solution.py:514
  94.4 0.5 slice.9
  95.5 1.6 %all-to-all-done.3.back_ref = f32[8,1,384]{2,1,0:T(1,128)S(1)} async-done(((f32[8,1,384]{2,1,0:T(1,128)}), f32[8,1,384]{2,1,0:T(1,128)S(1)}, u32[]{:S(2)}, u32[]{:S(2)}) %all-to-all-start.3) | async-done | bytes 12320 | tf_op jit(solution)/shard_map/all_to_all | solution.py:511
  97.2 0.9 final.1
  98.1 0.0 copy-start.1
  98.1 0.6 copy-done.1
  (10 shorter events, 0.0 us)
Async XLA Ops:
  5.9 25.5 %collective-permute-start.3 = (bf16[384,1024]{1,0:T(8,128)(2,1)S(1)}, bf16[384,1024]{1,0:T(8,128)(2,1)S(1)}, u32[]{:S(2)}, u32[]{:S(2)}) collective-permute-start(bf16[384,1024]{1,0:T(8,128)(2,1)S(1)} %get-tuple-element.88.even), channel_id=1, source_target_pairs={{0,4},{2,6},{4,0},{6,2},{8,12},{10,14},{12,8},{14,10},{1,5},{3,7},... | collective-permute-start | bytes 2359304 | tf_op jit(solution)/shard_map/ppermute | solution.py:422
  9.0 21.8 %collective-permute-start.2 = (bf16[336,1024]{1,0:T(8,128)(2,1)S(1)}, bf16[336,1024]{1,0:T(8,128)(2,1)S(1)}, u32[]{:S(2)}, u32[]{:S(2)}) collective-permute-start(bf16[336,1024]{1,0:T(8,128)(2,1)S(1)} %get-tuple-element.87), channel_id=1, source_target_pairs={{0,2},{2,0},{4,6},{6,4},{8,10},{10,8},{12,14},{14,12},{1,3},{3,1},... | collective-permute-start | bytes 2064392 | tf_op jit(solution)/shard_map/ppermute | solution.py:423
  10.5 20.2 %collective-permute-start.4 = (bf16[112,1024]{1,0:T(8,128)(2,1)S(1)}, bf16[112,1024]{1,0:T(8,128)(2,1)S(1)}, u32[]{:S(2)}, u32[]{:S(2)}) collective-permute-start(bf16[112,1024]{1,0:T(8,128)(2,1)S(1)} %get-tuple-element.89), channel_id=1, source_target_pairs={{0,8},{2,10},{4,12},{6,14},{8,0},{10,2},{12,4},{14,6},{1,9},{3,11}... | collective-permute-start | bytes 688136 | tf_op jit(solution)/shard_map/ppermute | solution.py:424
  13.1 21.1 %collective-permute-start.5 = (bf16[384,1024]{1,0:T(8,128)(2,1)S(1)}, bf16[384,1024]{1,0:T(8,128)(2,1)S(1)}, u32[]{:S(2)}, u32[]{:S(2)}) collective-permute-start(bf16[384,1024]{1,0:T(8,128)(2,1)S(1)} %get-tuple-element.91.odd), channel_id=1, source_target_pairs={{4,8},{6,10},{8,4},{10,6},{5,9},{7,11},{9,5},{11,7},{20,24},{22,26... | collective-permute-start | bytes 2359304 | tf_op jit(solution)/shard_map/ppermute | solution.py:421
  31.7 30.7 %collective-permute-start.7 = (bf16[656,1024]{1,0:T(8,128)(2,1)S(1)}, bf16[656,1024]{1,0:T(8,128)(2,1)S(1)}, u32[]{:S(2)}, u32[]{:S(2)}) collective-permute-start(bf16[656,1024]{1,0:T(8,128)(2,1)S(1)} %get-tuple-element.95.asked), channel_id=1, source_target_pairs={{0,2},{2,0},{4,6},{6,4},{8,10},{10,8},{12,14},{14,12},{1,3},{3,1},... | collective-permute-start | bytes 4030472 | tf_op jit(solution)/shard_map/ppermute | solution.py:441
  33.4 26.6 %collective-permute-start.8 = (bf16[544,1024]{1,0:T(8,128)(2,1)S(1)}, bf16[544,1024]{1,0:T(8,128)(2,1)S(1)}, u32[]{:S(2)}, u32[]{:S(2)}) collective-permute-start(bf16[544,1024]{1,0:T(8,128)(2,1)S(1)} %get-tuple-element.101.cols), channel_id=1, source_target_pairs={{0,1},{1,0},{2,3},{3,2},{4,5},{5,4},{6,7},{7,6},{8,9},{9,8},{10,11... | collective-permute-start | bytes 3342344 | tf_op jit(solution)/shard_map/ppermute | solution.py:442
  33.4 12.1 %collective-permute-start.6 = (bf16[384,1024]{1,0:T(8,128)(2,1)S(1)}, bf16[384,1024]{1,0:T(8,128)(2,1)S(1)}, u32[]{:S(2)}, u32[]{:S(2)}) collective-permute-start(bf16[384,1024]{1,0:T(8,128)(2,1)S(1)} %get-tuple-element.94), channel_id=1, source_target_pairs={{4,8},{6,10},{8,4},{10,6},{5,9},{7,11},{9,5},{11,7},{20,24},{22,26... | collective-permute-start | bytes 2359304 | tf_op jit(solution)/shard_map/ppermute | solution.py:440
  34.2 43.4 %collective-permute-start.9 = (bf16[384,1024]{1,0:T(8,128)(2,1)S(1)}, bf16[384,1024]{1,0:T(8,128)(2,1)S(1)}, u32[]{:S(2)}, u32[]{:S(2)}) collective-permute-start(bf16[384,1024]{1,0:T(8,128)(2,1)S(1)} %pass_on.1), channel_id=1, source_target_pairs={{0,4},{2,6},{4,0},{6,2},{8,12},{10,14},{12,8},{14,10},{1,5},{3,7},... | collective-permute-start | bytes 2359304 | tf_op jit(solution)/shard_map/ppermute | solution.py:451
  40.7 36.9 %collective-permute-start.10 = (bf16[224,1024]{1,0:T(8,128)(2,1)S(1)}, bf16[224,1024]{1,0:T(8,128)(2,1)S(1)}, u32[]{:S(2)}, u32[]{:S(2)}) collective-permute-start(bf16[224,1024]{1,0:T(8,128)(2,1)S(1)} %get-tuple-element.98), channel_id=1, source_target_pairs={{0,12},{2,14},{12,0},{14,2},{1,13},{3,15},{13,1},{15,3},{16,28},{1... | collective-permute-start | bytes 1376264 | tf_op jit(solution)/shard_map/ppermute | solution.py:452
  45.5 32.1 %collective-permute-start.11 = (bf16[112,1024]{1,0:T(8,128)(2,1)S(1)}, bf16[112,1024]{1,0:T(8,128)(2,1)S(1)}, u32[]{:S(2)}, u32[]{:S(2)}) collective-permute-start(bf16[112,1024]{1,0:T(8,128)(2,1)S(1)} %get-tuple-element.99), channel_id=1, source_target_pairs={{0,8},{2,10},{4,12},{6,14},{8,0},{10,2},{12,4},{14,6},{1,9},{3,11}... | collective-permute-start | bytes 688136 | tf_op jit(solution)/shard_map/ppermute | solution.py:453
  77.8 5.4 %collective-permute-start.12 = (bf16[1440,1024]{1,0:T(8,128)(2,1)S(1)}, bf16[1440,1024]{1,0:T(8,128)(2,1)S(1)}, u32[]{:S(2)}, u32[]{:S(2)}) collective-permute-start(bf16[1440,1024]{1,0:T(8,128)(2,1)S(1)} %collect.1.own), channel_id=1, source_target_pairs={{0,1},{1,0},{2,3},{3,2},{4,5},{5,4},{6,7},{7,6},{8,9},{9,8},{10,11... | collective-permute-start | bytes 8847368 | tf_op jit(solution)/shard_map/ppermute | solution.py:483
  81.4 16.6 %copy-start = (s32[1024]{0:T(1024)S(1)}, s32[1024]{0:T(1024)}, u32[]{:S(2)}) copy-start(s32[1024]{0:T(1024)} %param.7) | copy-start | bytes 12292
  87.2 10.0 %all-to-all-start.3 = ((f32[8,1,384]{2,1,0:T(1,128)}), f32[8,1,384]{2,1,0:T(1,128)S(1)}, u32[]{:S(2)}, u32[]{:S(2)}) async-start(f32[8,1,384]{2,1,0:T(1,128)} %get-tuple-element.112), calls=%async_computation.3 | async-start | bytes 24576 | tf_op jit(solution)/shard_map/all_to_all | solution.py:511
  90.7 3.7 %collective-permute-start.13 = (f32[8,128]{1,0:T(8,128)S(1)}, f32[8,128]{1,0:T(8,128)S(1)}, u32[]{:S(2)}, u32[]{:S(2)}) collective-permute-start(f32[8,128]{1,0:T(8,128)S(1)} %get-tuple-element.110), channel_id=1, source_target_pairs={{0,16},{16,0},{1,17},{17,1},{2,18},{18,2},{3,19},{19,3},{4,20},{20... | collective-permute-start | bytes 12296 | tf_op jit(solution)/shard_map/ppermute | solution.py:514
  98.1 0.6 copy-start.1

commit v6 on v5

--- a/solution.py
+++ b/solution.py
@@ -11,6 +11,7 @@
 CL_DEV = 8
 LANES = 128
 CHUNKS = 4
+FIRST = 2
 SUB = 16
 VMEM_LIMIT = 14 * 1024 * 1024
 VMEM = pl.BlockSpec(memory_space=pltpu.VMEM)
@@ -138,13 +139,16 @@
 
 def collect_kernel(peers, block, lead_rows, me_ref, mine, even, odd, asked_y, even2, odd2, ends, *rest):
     reach = peers // 2
-    far, far_across, own = rest[: reach - 3], rest[reach - 3 : 2 * reach - 6], rest[-1]
-    rest = rest[2 * reach - 6 : -1]
+    far, far_across, own = rest[: reach - 3], rest[reach - 3 : 2 * reach - 6], rest[-3]
+    first, second = rest[-2:]
+    rest = rest[2 * reach - 6 : -3]
     z = me_ref[0] // 2
     at_end = (z == 0) | (z == reach - 1)
 
     def put(k, src, start=0):
         own[k * block : (k + 1) * block, :] = src[start : start + block, :]
+        there, at = (first, k) if k < FIRST else (second, k - FIRST)
+        there[at * block : (at + 1) * block, :] = src[start : start + block, :]
 
     def put_last(first, second, start, then):
         put(reach - 1, first, start)
@@ -161,10 +165,10 @@
     pl.when(jnp.logical_not(at_end))(functools.partial(put_last, odd, odd2, lead_rows, lead_rows))
 
     def keep(slot, src):
-        at = peers * block + slot * lead_rows
-        own[at : at + lead_rows, :] = src[:lead_rows, :]
-
-    keep((own.shape[0] - peers * block) // lead_rows - 1, odd)
+        at = FIRST * block + slot * lead_rows
+        first[at : at + lead_rows, :] = src[:lead_rows, :]
+
+    keep((first.shape[0] - FIRST * block) // lead_rows - 1, odd)
     if reach == 4:
         pl.when(at_end)(functools.partial(keep, 0, even2))
         pl.when(jnp.logical_not(at_end))(functools.partial(keep, 0, odd2))
@@ -206,36 +210,40 @@
     top[...] = jnp.concatenate(best, axis=0)
 
 
-def lead_late(rows, slots, cap, asked, asked_y):
-    count = (rows.shape[0] - slots) // (cap + SUB)
-    ids = lead_column(rows, slots, count, cap)
-    places = ((asked, 0), (asked_y, 0), (asked, cap + SUB), (asked_y, cap + SUB))
-    return [lead_tops(rows[slots:, :], ids, queries, start, cap, False) for queries, start in places]
-
-
-def lead_best_kernel(slots, cap, early, asked, asked_y, own, top):
-    late = lead_late(own, slots, cap, asked, asked_y)
+def lead_late(rows, start, cap, asked, asked_y):
+    lead_rows = cap + SUB
+    count = (rows.shape[0] - start) // lead_rows
+    ids = lead_column(rows, start, count, cap)
+    best = [lead_tops(rows[start:, :], ids, queries, 0, cap, False) for queries in (asked, asked_y)]
+    stop = (count - 1) * lead_rows
+    for queries in (asked, asked_y):
+        best.append(lead_tops(rows[start : start + stop, :], ids[:stop], queries, lead_rows, cap, False))
+    return best
+
+
+def lead_best_kernel(cap, block, early, asked, asked_y, first, top):
+    late = lead_late(first, FIRST * block, cap, asked, asked_y)
     best = [jnp.maximum(early[i : i + 1, :], new) for i, new in enumerate(late)]
     top[...] = jnp.concatenate(best + [jnp.full((4, cap), -1.0, jnp.float32)], axis=0)
 
 
-def ids_of(rows, peers, block):
+def ids_of(rows, blocks, block):
     width = rows.shape[1]
     lane = lax.broadcasted_iota(jnp.int32, (1, width), 1)
     total = jnp.zeros((1, width), jnp.float32)
-    for k in range(peers):
-        tail = rows[(k + 1) * block - SUB : (k + 1) * block, :].astype(jnp.float32)[SUB - 1 : SUB]
+    for i, k in enumerate(blocks):
+        tail = rows[(i + 1) * block - SUB : (i + 1) * block, :].astype(jnp.float32)[SUB - 1 : SUB]
         total = jnp.where((lane >= k * block) & (lane < (k + 1) * block), tail, total)
     return total
 
 
-def tops_of(rows, ids, queries, q_ids, diagonal, tile):
+def tops_of(rows, ids, begin, queries, q_ids, diagonal, tile):
     slots = q_ids.shape[1]
-    column = as_column(ids)[:slots]
+    column = as_column(ids)[begin : begin + rows.shape[0]]
     tops = []
     for start in range(0, slots, tile):
         stop = min(start + tile, slots)
-        scores = lax.dot_general(rows[:slots, :], queries[start:stop, :], NT, preferred_element_type=jnp.float32)
+        scores = lax.dot_general(rows, queries[start:stop, :], NT, preferred_element_type=jnp.float32)
         same = column == q_ids[:, start:stop]
         if diagonal:
             r = lax.broadcasted_iota(jnp.int32, scores.shape, 0)
@@ -247,23 +255,38 @@
 
 def own_best_kernel(peers, block, own, top):
     slots = peers * block
-    ids = ids_of(own, peers, block)
-    top[0:1, :] = tops_of(own, ids, own, ids[:, :slots], True, 256)
+    ids = ids_of(own, range(peers), block)
+    top[0:1, :] = tops_of(own[...], ids, 0, own, ids[:, :slots], True, 256)
     top[1:2, :] = ids[:, :slots]
 
 
-def far_best_kernel(peers, block, edges, me_ref, own, far, top, asked, asked_y, lead_top, out, flag):
+def first_best_kernel(peers, block, cap, own, first, top, asked, asked_y, lead_top, out, lead_out):
+    slots = peers * block
+    ids = ids_of(first, range(FIRST), block)
+    best = tops_of(first[: FIRST * block, :], ids, 0, own, top[1:2, :], False, 256)
+    out[0:1, :] = jnp.maximum(top[0:1, :], best)
+    out[1:2, :] = top[1:2, :]
+    out[2:3, :] = ids[:, :slots]
+    late = lead_late(first, FIRST * block, cap, asked, asked_y)
+    best = [jnp.maximum(lead_top[i : i + 1, :], new) for i, new in enumerate(late)]
+    lead_out[...] = jnp.concatenate(best + [jnp.full((4, cap), -1.0, jnp.float32)], axis=0)
+
+
+def far_best_kernel(peers, block, edges, me_ref, own, second, top, lead_top, out, flag):
     width = own.shape[1]
     slots = peers * block
-    own_ids, far_ids = top[1:2, :], ids_of(far, peers, block)
+    own_ids = top[1:2, :]
+    second_ids = ids_of(second, range(FIRST, peers), block)
     lane = lax.broadcasted_iota(jnp.int32, (1, slots), 1)
+    far_ids = jnp.where(lane < FIRST * block, top[2:3, :], second_ids[:, :slots])
     is_code = functools.reduce(jnp.logical_or, [lane == k * block + block - 1 for k in range(peers)])
     my_code = own_ids[:, block - 1 : block]
-    odd = jnp.where(is_code & ((own_ids != my_code) | (far_ids[:, :slots] != my_code)), 1.0, 0.0)
+    odd = jnp.where(is_code & ((own_ids != my_code) | (far_ids != my_code)), 1.0, 0.0)
     half = jnp.floor(my_code * 0.5)
     odd = jnp.maximum(jnp.max(odd, axis=1, keepdims=True), my_code - 2.0 * half)
     flag[...] = jnp.broadcast_to(odd, flag.shape)
-    best = jnp.maximum(top[0:1, :], tops_of(far, far_ids, own, own_ids, False, 256))
+    best = tops_of(second[...], second_ids, FIRST * block, own, own_ids, False, 256)
+    best = jnp.maximum(top[0:1, :], best)
     best = jnp.broadcast_to(pad_lanes(best, width), (8, width))
     reach = peers // 2
     pitch = -(-block // LANES) * LANES
@@ -277,7 +300,7 @@
         row = 2 * (row % reach) + (y if k < reach else 1 - y)
         out[row, :, :pitch] = piece[0:1, :pitch]
         out[k, :, pitch:] = none
-    lead = [jnp.maximum(lead_top[i : i + 1, :], new) for i, new in enumerate(lead_late(far, slots, cap, asked, asked_y))]
+    lead = [lead_top[i : i + 1, :] for i in range(4)]
     out[2 * z + y, :, pitch:] = lead[0]
     out[2 * z + 1 - y, :, pitch:] = lead[1]
     if edges:
@@ -472,24 +495,29 @@
             up = lax.ppermute(up, "dp", up_pairs)
             down = lax.ppermute(down, "dp", down_pairs)
             late += [up, down]
-    own = call(
+    own, first, second = call(
         functools.partial(collect_kernel, peers, block, lead_rows),
         "collect",
-        shape((slots + (1 + max(1, len(late))) * lead_rows, width), bf16),
+        [
+            shape((slots, width), bf16),
+            shape((FIRST * block + (1 + max(1, len(late))) * lead_rows, width), bf16),
+            shape((slots - FIRST * block, width), bf16),
+        ],
         [SMEM] + [VMEM] * (7 + 2 * (reach - 3) + len(late)),
-        VMEM,
+        [VMEM] * 3,
         nbytes=4 * slots * width,
     )(me1, mine, even1, odd1, asked_y, even2, odd2, ends, *fars, *fars_r, *late)
-    far = lax.ppermute(own, "owner", swap)
+    first_o = lax.ppermute(first, "owner", swap)
+    second_o = lax.ppermute(second, "owner", swap)
     lead_top = call(
-        functools.partial(lead_best_kernel, slots, cap),
+        functools.partial(lead_best_kernel, cap, block),
         "lead_best",
         shape((8, cap), f32),
         [VMEM] * 4,
         VMEM,
         flops=40 * cap * cap * width,
         nbytes=20 * cap * width,
-    )(early, asked, asked_y, own)
+    )(early, asked, asked_y, first)
     top = call(
         functools.partial(own_best_kernel, peers, block),
         "own_best",
@@ -499,15 +527,24 @@
         flops=2 * slots * slots * width,
         nbytes=2 * slots * width,
     )(own)
+    top, lead_top = call(
+        functools.partial(first_best_kernel, peers, block, cap),
+        "first_best",
+        [shape((8, slots), f32), shape((8, cap), f32)],
+        [VMEM] * 6,
+        [VMEM] * 2,
+        flops=2 * FIRST * block * slots * width + 14 * cap * cap * width,
+        nbytes=4 * slots * width,
+    )(own, first_o, top, asked, asked_y, lead_top)
     best, flag = call(
         functools.partial(far_best_kernel, peers, block, edges),
         "far_best",
         [shape((peers, 1, pitch + cap), f32), shape((8, LANES), f32)],
-        [SMEM] + [VMEM] * 6,
+        [SMEM] + [VMEM] * 4,
         [VMEM] * 2,
         flops=2 * slots * slots * width,
         nbytes=4 * slots * width,
-    )(me1, own, far, top, asked, asked_y, lead_top)
+    )(me1, own, second_o, top, lead_top)
     back = lax.all_to_all(best, "dp", split_axis=0, concat_axis=0, tiled=True)
     flags = [flag]
     for k in range(1, groups):

time: 99 us -> 97.5 us (0.985)
  waiting for transfers between devices: 39.3 us -> 37.3 us
    ppermute x1 -> x2, waiting for transfers between devices: 1.81 us -> 0.01 us  [the longest x1 0.01 us: local(): first_o = lax.ppermute(first, 'owner', swap)]
    pallas_call x1, Pallas kernels: 3.94 us -> 2.41 us  [local(): call(functools.partial(far_best_kernel, peers, block, edges), 'far_best',...]
    pallas_call x1 -> x2, Pallas kernels: 1.39 us -> 2.82 us  [the longest x1 1.69 us: local(): call(functools.partial(first_best_kernel, peers, block, cap), 'first_best...]
  transfers between devices with their start and end apart: 13 -> 14, of which waited for: 7 -> 6; matrix products, arithmetic and copies ran while one was open for 1% -> 1% of each run, Pallas kernels for 5% -> 7%
where the time goes in v6:
time: 97.5 us; the launch traced here: 97.2 us
  starting transfers between devices  41.8 us (43%)
  waiting for transfers between devices  37.3 us (38%)
  Pallas kernels  16.1 us (17%)
  local copies, waits for them, and re-layouts  1.11 us (1%)
    ppermute x2, waiting for transfers between devices, local(): lax.ppermute(rows, 'dp', pairs)  30.7 us
    ppermute x2, starting transfers between devices, local(): lax.ppermute(rows, 'dp', pairs)  17.1 us
    ppermute x1, starting transfers between devices, local(): even2 = lax.ppermute(even2, 'dp', even_pairs)  6.45 us
    pallas_call x1, Pallas kernels, local(): call(functools.partial(pack_kernel, peers, cap, block), 'pack', [shape((8...  5.88 us
    ppermute x1, starting transfers between devices, local(): ends = lax.ppermute(ends, 'dp', ends_pairs)  4.85 us
    all_to_all x1, starting transfers between devices, local(): back = lax.all_to_all(best, 'dp', split_axis=0, concat_axis=0, tiled=True)  3.52 us
    ppermute x1, starting transfers between devices, local(): even1 = lax.ppermute(even, 'dp', even_pairs)  3.08 us
    pallas_call x1, Pallas kernels, local(): call(functools.partial(far_best_kernel, peers, block, edges), 'far_best',...  2.41 us
  transfers between devices with their start and end apart: 14, of which 6 were waited for; matrix products, arithmetic and copies ran while one was open for 1% of the time, Pallas kernels for 7%

profile of v6, /device:TPU:0, one launch (start us, length us, event | category | flops | bytes accessed | tf_op | source)
XLA Modules:
  0.0 97.2 jit_solution(11641852649470765573)
XLA Ops:
  0.0 5.9 %pack.1 = (s32[8,1024]{1,0:T(8,128)S(1)}, bf16[112,1024]{1,0:T(8,128)(2,1)S(1)}, bf16[112,1024]{1,0:T(8,128)(2,1)S(1)}, bf16[384,1024]{1,0:T(8,128)(2,1)S(1)}, b...) custom-call(s32[1]{0:T(128)} %bitcast.8.me_ref, s32[1,1024]{1,0:T(1,128)} %bitcast.47, ...), custom_call_target="tpu_custom_call" | custom-call | flops 2415919104 | bytes 8388608 | tf_op jit(solution)/shard_map/pack/pallas_call | solution.py:427
  5.9 3.1 %collective-permute-start.3 = (bf16[384,1024]{1,0:T(8,128)(2,1)S(1)}, bf16[384,1024]{1,0:T(8,128)(2,1)S(1)}, u32[]{:S(2)}, u32[]{:S(2)}) collective-permute-start(bf16[384,1024]{1,0:T(8,128)(2,1)S(1)} %get-tuple-element.93.even), channel_id=1, source_target_pairs={{0,4},{2,6},{4,0},{6,2},{8,12},{10,14},{12,8},{14,10},{1,5},{3,7},... | collective-permute-start | bytes 2359304 | tf_op jit(solution)/shard_map/ppermute | solution.py:445
  9.0 1.5 %collective-permute-start.2 = (bf16[336,1024]{1,0:T(8,128)(2,1)S(1)}, bf16[336,1024]{1,0:T(8,128)(2,1)S(1)}, u32[]{:S(2)}, u32[]{:S(2)}) collective-permute-start(bf16[336,1024]{1,0:T(8,128)(2,1)S(1)} %get-tuple-element.92), channel_id=1, source_target_pairs={{0,2},{2,0},{4,6},{6,4},{8,10},{10,8},{12,14},{14,12},{1,3},{3,1},... | collective-permute-start | bytes 2064392 | tf_op jit(solution)/shard_map/ppermute | solution.py:446
  10.5 2.6 %collective-permute-start.4 = (bf16[112,1024]{1,0:T(8,128)(2,1)S(1)}, bf16[112,1024]{1,0:T(8,128)(2,1)S(1)}, u32[]{:S(2)}, u32[]{:S(2)}) collective-permute-start(bf16[112,1024]{1,0:T(8,128)(2,1)S(1)} %get-tuple-element.94), channel_id=1, source_target_pairs={{0,8},{2,10},{4,12},{6,14},{8,0},{10,2},{12,4},{14,6},{1,9},{3,11}... | collective-permute-start | bytes 688136 | tf_op jit(solution)/shard_map/ppermute | solution.py:447
  13.1 0.7 collective-permute-start.5
  13.8 16.9 %collective-permute-done.4.rest_0_ = bf16[112,1024]{1,0:T(8,128)(2,1)S(1)} collective-permute-done((bf16[112,1024]{1,0:T(8,128)(2,1)S(1)}, bf16[112,1024]{1,0:T(8,128)(2,1)S(1)}, u32[]{:S(2)}, u32[]{:S(2)}) %collective-permute-start.4) | collective-permute-done | bytes 229408 | tf_op jit(solution)/shard_map/ppermute | solution.py:447
  30.7 0.7 collective-permute-done.3.lead_even.even
  31.4 0.3 relay.1
  31.7 1.8 %collective-permute-start.7 = (bf16[656,1024]{1,0:T(8,128)(2,1)S(1)}, bf16[656,1024]{1,0:T(8,128)(2,1)S(1)}, u32[]{:S(2)}, u32[]{:S(2)}) collective-permute-start(bf16[656,1024]{1,0:T(8,128)(2,1)S(1)} %get-tuple-element.100.asked), channel_id=1, source_target_pairs={{0,2},{2,0},{4,6},{6,4},{8,10},{10,8},{12,14},{14,12},{1,3},{3,1},... | collective-permute-start | bytes 4030472 | tf_op jit(solution)/shard_map/ppermute | solution.py:464
  33.4 0.7 collective-permute-start.6
  34.2 0.1 pass_on.1
  34.2 6.5 %collective-permute-start.9 = (bf16[384,1024]{1,0:T(8,128)(2,1)S(1)}, bf16[384,1024]{1,0:T(8,128)(2,1)S(1)}, u32[]{:S(2)}, u32[]{:S(2)}) collective-permute-start(bf16[384,1024]{1,0:T(8,128)(2,1)S(1)} %pass_on.1), channel_id=1, source_target_pairs={{0,4},{2,6},{4,0},{6,2},{8,12},{10,14},{12,8},{14,10},{1,5},{3,7},... | collective-permute-start | bytes 2359304 | tf_op jit(solution)/shard_map/ppermute | solution.py:474
  40.7 4.8 %collective-permute-start.10 = (bf16[224,1024]{1,0:T(8,128)(2,1)S(1)}, bf16[224,1024]{1,0:T(8,128)(2,1)S(1)}, u32[]{:S(2)}, u32[]{:S(2)}) collective-permute-start(bf16[224,1024]{1,0:T(8,128)(2,1)S(1)} %get-tuple-element.103), channel_id=1, source_target_pairs={{0,12},{2,14},{12,0},{14,2},{1,13},{3,15},{13,1},{15,3},{16,28},{1... | collective-permute-start | bytes 1376264 | tf_op jit(solution)/shard_map/ppermute | solution.py:475
  45.5 14.5 %collective-permute-start.11 = (bf16[112,1024]{1,0:T(8,128)(2,1)S(1)}, bf16[112,1024]{1,0:T(8,128)(2,1)S(1)}, u32[]{:S(2)}, u32[]{:S(2)}) collective-permute-start(bf16[112,1024]{1,0:T(8,128)(2,1)S(1)} %get-tuple-element.104), channel_id=1, source_target_pairs={{0,8},{2,10},{4,12},{6,14},{8,0},{10,2},{12,4},{14,6},{1,9},{3,11}... | collective-permute-start | bytes 688136 | tf_op jit(solution)/shard_map/ppermute | solution.py:476
  60.1 2.4 %collective-permute-done.7.asked_y = bf16[656,1024]{1,0:T(8,128)(2,1)S(1)} collective-permute-done((bf16[656,1024]{1,0:T(8,128)(2,1)S(1)}, bf16[656,1024]{1,0:T(8,128)(2,1)S(1)}, u32[]{:S(2)}, u32[]{:S(2)}) %collective-permute-start.7) | collective-permute-done | bytes 1343520 | tf_op jit(solution)/shard_map/ppermute | solution.py:464
  62.4 1.4 %lead_early.1.early = f32[8,256]{1,0:T(8,128)S(1)} custom-call(bf16[656,1024]{1,0:T(8,128)(2,1)S(1)} %get-tuple-element.100.asked, bf16[656,1024]{1,0:T(8,128)(2,1)S(1)} %collective-permute-done.7.asked_y, bf16[544,1024]{1,0:T(8,128)(2,1)S(1)} %get-tuple-element.106.cols, bf16[544,1024]{1,0:T(8,128)(2,1)S(1)} %collective-permute-done.8.cols_other), custom_call_target="tpu_custom_call" | custom-call | flops 1610612736 | bytes 3670016 | tf_op jit(solution)/shard_map/lead_early/pallas_call | solution.py:478
  63.8 13.8 %collective-permute-done.11.rest_1_ = bf16[112,1024]{1,0:T(8,128)(2,1)S(1)} collective-permute-done((bf16[112,1024]{1,0:T(8,128)(2,1)S(1)}, bf16[112,1024]{1,0:T(8,128)(2,1)S(1)}, u32[]{:S(2)}, u32[]{:S(2)}) %collective-permute-start.11) | collective-permute-done | bytes 229408 | tf_op jit(solution)/shard_map/ppermute | solution.py:476
  77.6 0.3 collect.1
  77.9 0.1 collective-permute-start.13
  78.0 0.5 collective-permute-start.12
  78.5 2.1 %own_best.1.top = f32[8,896]{1,0:T(8,128)S(1)} custom-call(bf16[896,1024]{1,0:T(8,128)(2,1)S(1)} %get-tuple-element.114.own), custom_call_target="tpu_custom_call" | custom-call | flops 1644167168 | bytes 1835008 | tf_op jit(solution)/shard_map/own_best/pallas_call | solution.py:521
  80.6 1.1 %lead_best.1.lead_top = f32[8,256]{1,0:T(8,128)S(1)} custom-call(f32[8,256]{1,0:T(8,128)S(1)} %lead_early.1.early, bf16[656,1024]{1,0:T(8,128)(2,1)S(1)} %get-tuple-element.100.asked, bf16[656,1024]{1,0:T(8,128)(2,1)S(1)} %collective-permute-done.7.asked_y, bf16[768,1024]{1,0:T(8,128)(2,1)S(1)} %get-tuple-element.116.first), custom_call_target="tpu_custom_call" | custom-call | flops 2684354560 | bytes 5242880 | tf_op jit(solution)/shard_map/lead_best/pallas_call | solution.py:512
  81.8 1.7 %first_best.1 = (f32[8,896]{1,0:T(8,128)S(1)}, f32[8,256]{1,0:T(8,128)S(1)}) custom-call(bf16[896,1024]{1,0:T(8,128)(2,1)S(1)} %get-tuple-element.114.own, bf16[768,1024]{1,0:T(8,128)(2,1)S(1)} %collective-permute-done.13.first, f32[8,896]{1,0:T(8,128)S(1)} %own_best.1.top, bf16[656,1024]{1,0:T(8,128)(2,1)S(1)} %get-tuple-element.100.asked, ...), custom_call_target="tpu_custom_call" | custom-call | flops 1350565888 | bytes 3670016 | tf_op jit(solution)/shard_map/first_best/pallas_call | solution.py:530
  83.5 0.0 copy-start
  83.5 2.4 %far_best.1 = (f32[8,1,384]{2,1,0:T(1,128)}, f32[8,128]{1,0:T(8,128)S(1)}) custom-call(s32[1]{0:T(128)} %bitcast.8.me_ref, bf16[896,1024]{1,0:T(8,128)(2,1)S(1)} %get-tuple-element.114.own, bf16[672,1024]{1,0:T(8,128)(2,1)S(1)} %collective-permute-done.12.second, f32[8,896]{1,0:T(8,128)S(1)} %get-tuple-element.118.top, f32[8,256]{1,0:T(8,128)S(1)} %get-tuple-element.119.lead_top), custom_call_target="tpu_custom_call" | custom-call | flops 1644167168 | bytes 3670016 | tf_op jit(solution)/shard_map/far_best/pallas_call | solution.py:539
  85.9 3.5 %all-to-all-start.3 = ((f32[8,1,384]{2,1,0:T(1,128)}), f32[8,1,384]{2,1,0:T(1,128)S(1)}, u32[]{:S(2)}, u32[]{:S(2)}) async-start(f32[8,1,384]{2,1,0:T(1,128)} %get-tuple-element.122), calls=%async_computation.3 | async-start | bytes 24576 | tf_op jit(solution)/shard_map/all_to_all | solution.py:548
  89.4 1.6 %collective-permute-start.14 = (f32[8,128]{1,0:T(8,128)S(1)}, f32[8,128]{1,0:T(8,128)S(1)}, u32[]{:S(2)}, u32[]{:S(2)}) collective-permute-start(f32[8,128]{1,0:T(8,128)S(1)} %get-tuple-element.120), channel_id=1, source_target_pairs={{0,16},{16,0},{1,17},{17,1},{2,18},{18,2},{3,19},{19,3},{4,20},{20... | collective-permute-start | bytes 12296 | tf_op jit(solution)/shard_map/ppermute | solution.py:551
  91.0 2.1 %collective-permute-done.14 = f32[8,128]{1,0:T(8,128)S(1)} collective-permute-done((f32[8,128]{1,0:T(8,128)S(1)}, f32[8,128]{1,0:T(8,128)S(1)}, u32[]{:S(2)}, u32[]{:S(2)}) %collective-permute-start.14) | collective-permute-done | bytes 4128 | tf_op jit(solution)/shard_map/ppermute | solution.py:551
  93.1 0.5 slice.9
  94.3 1.5 %all-to-all-done.3.back_ref = f32[8,1,384]{2,1,0:T(1,128)S(1)} async-done(((f32[8,1,384]{2,1,0:T(1,128)}), f32[8,1,384]{2,1,0:T(1,128)S(1)}, u32[]{:S(2)}, u32[]{:S(2)}) %all-to-all-start.3) | async-done | bytes 12320 | tf_op jit(solution)/shard_map/all_to_all | solution.py:548
  95.7 0.9 final.1
  96.6 0.6 copy-done.1
  (13 shorter events, 0.0 us)
Async XLA Ops:
  5.9 25.5 %collective-permute-start.3 = (bf16[384,1024]{1,0:T(8,128)(2,1)S(1)}, bf16[384,1024]{1,0:T(8,128)(2,1)S(1)}, u32[]{:S(2)}, u32[]{:S(2)}) collective-permute-start(bf16[384,1024]{1,0:T(8,128)(2,1)S(1)} %get-tuple-element.93.even), channel_id=1, source_target_pairs={{0,4},{2,6},{4,0},{6,2},{8,12},{10,14},{12,8},{14,10},{1,5},{3,7},... | collective-permute-start | bytes 2359304 | tf_op jit(solution)/shard_map/ppermute | solution.py:445
  9.0 21.8 %collective-permute-start.2 = (bf16[336,1024]{1,0:T(8,128)(2,1)S(1)}, bf16[336,1024]{1,0:T(8,128)(2,1)S(1)}, u32[]{:S(2)}, u32[]{:S(2)}) collective-permute-start(bf16[336,1024]{1,0:T(8,128)(2,1)S(1)} %get-tuple-element.92), channel_id=1, source_target_pairs={{0,2},{2,0},{4,6},{6,4},{8,10},{10,8},{12,14},{14,12},{1,3},{3,1},... | collective-permute-start | bytes 2064392 | tf_op jit(solution)/shard_map/ppermute | solution.py:446
  10.5 20.2 %collective-permute-start.4 = (bf16[112,1024]{1,0:T(8,128)(2,1)S(1)}, bf16[112,1024]{1,0:T(8,128)(2,1)S(1)}, u32[]{:S(2)}, u32[]{:S(2)}) collective-permute-start(bf16[112,1024]{1,0:T(8,128)(2,1)S(1)} %get-tuple-element.94), channel_id=1, source_target_pairs={{0,8},{2,10},{4,12},{6,14},{8,0},{10,2},{12,4},{14,6},{1,9},{3,11}... | collective-permute-start | bytes 688136 | tf_op jit(solution)/shard_map/ppermute | solution.py:447
  13.1 21.1 %collective-permute-start.5 = (bf16[384,1024]{1,0:T(8,128)(2,1)S(1)}, bf16[384,1024]{1,0:T(8,128)(2,1)S(1)}, u32[]{:S(2)}, u32[]{:S(2)}) collective-permute-start(bf16[384,1024]{1,0:T(8,128)(2,1)S(1)} %get-tuple-element.96.odd), channel_id=1, source_target_pairs={{4,8},{6,10},{8,4},{10,6},{5,9},{7,11},{9,5},{11,7},{20,24},{22,26... | collective-permute-start | bytes 2359304 | tf_op jit(solution)/shard_map/ppermute | solution.py:444
  31.7 30.7 %collective-permute-start.7 = (bf16[656,1024]{1,0:T(8,128)(2,1)S(1)}, bf16[656,1024]{1,0:T(8,128)(2,1)S(1)}, u32[]{:S(2)}, u32[]{:S(2)}) collective-permute-start(bf16[656,1024]{1,0:T(8,128)(2,1)S(1)} %get-tuple-element.100.asked), channel_id=1, source_target_pairs={{0,2},{2,0},{4,6},{6,4},{8,10},{10,8},{12,14},{14,12},{1,3},{3,1},... | collective-permute-start | bytes 4030472 | tf_op jit(solution)/shard_map/ppermute | solution.py:464
  33.4 26.6 %collective-permute-start.8 = (bf16[544,1024]{1,0:T(8,128)(2,1)S(1)}, bf16[544,1024]{1,0:T(8,128)(2,1)S(1)}, u32[]{:S(2)}, u32[]{:S(2)}) collective-permute-start(bf16[544,1024]{1,0:T(8,128)(2,1)S(1)} %get-tuple-element.106.cols), channel_id=1, source_target_pairs={{0,1},{1,0},{2,3},{3,2},{4,5},{5,4},{6,7},{7,6},{8,9},{9,8},{10,11... | collective-permute-start | bytes 3342344 | tf_op jit(solution)/shard_map/ppermute | solution.py:465
  33.4 12.1 %collective-permute-start.6 = (bf16[384,1024]{1,0:T(8,128)(2,1)S(1)}, bf16[384,1024]{1,0:T(8,128)(2,1)S(1)}, u32[]{:S(2)}, u32[]{:S(2)}) collective-permute-start(bf16[384,1024]{1,0:T(8,128)(2,1)S(1)} %get-tuple-element.99), channel_id=1, source_target_pairs={{4,8},{6,10},{8,4},{10,6},{5,9},{7,11},{9,5},{11,7},{20,24},{22,26... | collective-permute-start | bytes 2359304 | tf_op jit(solution)/shard_map/ppermute | solution.py:463
  34.2 43.4 %collective-permute-start.9 = (bf16[384,1024]{1,0:T(8,128)(2,1)S(1)}, bf16[384,1024]{1,0:T(8,128)(2,1)S(1)}, u32[]{:S(2)}, u32[]{:S(2)}) collective-permute-start(bf16[384,1024]{1,0:T(8,128)(2,1)S(1)} %pass_on.1), channel_id=1, source_target_pairs={{0,4},{2,6},{4,0},{6,2},{8,12},{10,14},{12,8},{14,10},{1,5},{3,7},... | collective-permute-start | bytes 2359304 | tf_op jit(solution)/shard_map/ppermute | solution.py:474
  40.7 36.9 %collective-permute-start.10 = (bf16[224,1024]{1,0:T(8,128)(2,1)S(1)}, bf16[224,1024]{1,0:T(8,128)(2,1)S(1)}, u32[]{:S(2)}, u32[]{:S(2)}) collective-permute-start(bf16[224,1024]{1,0:T(8,128)(2,1)S(1)} %get-tuple-element.103), channel_id=1, source_target_pairs={{0,12},{2,14},{12,0},{14,2},{1,13},{3,15},{13,1},{15,3},{16,28},{1... | collective-permute-start | bytes 1376264 | tf_op jit(solution)/shard_map/ppermute | solution.py:475
  45.5 32.1 %collective-permute-start.11 = (bf16[112,1024]{1,0:T(8,128)(2,1)S(1)}, bf16[112,1024]{1,0:T(8,128)(2,1)S(1)}, u32[]{:S(2)}, u32[]{:S(2)}) collective-permute-start(bf16[112,1024]{1,0:T(8,128)(2,1)S(1)} %get-tuple-element.104), channel_id=1, source_target_pairs={{0,8},{2,10},{4,12},{6,14},{8,0},{10,2},{12,4},{14,6},{1,9},{3,11}... | collective-permute-start | bytes 688136 | tf_op jit(solution)/shard_map/ppermute | solution.py:476
  77.9 3.8 %collective-permute-start.13 = (bf16[768,1024]{1,0:T(8,128)(2,1)S(1)}, bf16[768,1024]{1,0:T(8,128)(2,1)S(1)}, u32[]{:S(2)}, u32[]{:S(2)}) collective-permute-start(bf16[768,1024]{1,0:T(8,128)(2,1)S(1)} %get-tuple-element.116.first), channel_id=1, source_target_pairs={{0,1},{1,0},{2,3},{3,2},{4,5},{5,4},{6,7},{7,6},{8,9},{9,8},{10,11... | collective-permute-start | bytes 4718600 | tf_op jit(solution)/shard_map/ppermute | solution.py:510
  78.0 5.5 %collective-permute-start.12 = (bf16[672,1024]{1,0:T(8,128)(2,1)S(1)}, bf16[672,1024]{1,0:T(8,128)(2,1)S(1)}, u32[]{:S(2)}, u32[]{:S(2)}) collective-permute-start(bf16[672,1024]{1,0:T(8,128)(2,1)S(1)} %get-tuple-element.115), channel_id=1, source_target_pairs={{0,1},{1,0},{2,3},{3,2},{4,5},{5,4},{6,7},{7,6},{8,9},{9,8},{10,11... | collective-permute-start | bytes 4128776 | tf_op jit(solution)/shard_map/ppermute | solution.py:511
  83.5 13.1 %copy-start = (s32[1024]{0:T(1024)S(1)}, s32[1024]{0:T(1024)}, u32[]{:S(2)}) copy-start(s32[1024]{0:T(1024)} %param.7) | copy-start | bytes 12292
  85.9 9.8 %all-to-all-start.3 = ((f32[8,1,384]{2,1,0:T(1,128)}), f32[8,1,384]{2,1,0:T(1,128)S(1)}, u32[]{:S(2)}, u32[]{:S(2)}) async-start(f32[8,1,384]{2,1,0:T(1,128)} %get-tuple-element.122), calls=%async_computation.3 | async-start | bytes 24576 | tf_op jit(solution)/shard_map/all_to_all | solution.py:548
  89.4 3.7 %collective-permute-start.14 = (f32[8,128]{1,0:T(8,128)S(1)}, f32[8,128]{1,0:T(8,128)S(1)}, u32[]{:S(2)}, u32[]{:S(2)}) collective-permute-start(f32[8,128]{1,0:T(8,128)S(1)} %get-tuple-element.120), channel_id=1, source_target_pairs={{0,16},{16,0},{1,17},{17,1},{2,18},{18,2},{3,19},{19,3},{4,20},{20... | collective-permute-start | bytes 12296 | tf_op jit(solution)/shard_map/ppermute | solution.py:551
  96.6 0.6 copy-start.1

commit v7 on v6

--- a/solution.py
+++ b/solution.py
@@ -105,7 +105,7 @@
     places = [(mine, 0), (even, cap + SUB), *[(ref, 0) for ref in far], (odd, cap + SUB), (mine_across, 0)]
     places += [(across, s * block) for s in range(reach - 1)]
     is_hdr = lax.broadcasted_iota(jnp.int32, (block, 1), 0) == block - 1
-    tile = 256
+    tile = 512
     for start in range(0, width, tile):
         cols = slice(start, start + tile)
         acc = jnp.dot(pick[...], unit_ref[:, cols], preferred_element_type=jnp.float32)
@@ -256,14 +256,14 @@
 def own_best_kernel(peers, block, own, top):
     slots = peers * block
     ids = ids_of(own, range(peers), block)
-    top[0:1, :] = tops_of(own[...], ids, 0, own, ids[:, :slots], True, 256)
+    top[0:1, :] = tops_of(own[...], ids, 0, own, ids[:, :slots], True, 1024)
     top[1:2, :] = ids[:, :slots]
 
 
 def first_best_kernel(peers, block, cap, own, first, top, asked, asked_y, lead_top, out, lead_out):
     slots = peers * block
     ids = ids_of(first, range(FIRST), block)
-    best = tops_of(first[: FIRST * block, :], ids, 0, own, top[1:2, :], False, 256)
+    best = tops_of(first[: FIRST * block, :], ids, 0, own, top[1:2, :], False, 1024)
     out[0:1, :] = jnp.maximum(top[0:1, :], best)
     out[1:2, :] = top[1:2, :]
     out[2:3, :] = ids[:, :slots]
@@ -285,7 +285,7 @@
     half = jnp.floor(my_code * 0.5)
     odd = jnp.maximum(jnp.max(odd, axis=1, keepdims=True), my_code - 2.0 * half)
     flag[...] = jnp.broadcast_to(odd, flag.shape)
-    best = tops_of(second[...], second_ids, FIRST * block, own, own_ids, False, 256)
+    best = tops_of(second[...], second_ids, FIRST * block, own, own_ids, False, 1024)
     best = jnp.maximum(top[0:1, :], best)
     best = jnp.broadcast_to(pad_lanes(best, width), (8, width))
     reach = peers // 2
@@ -550,7 +550,7 @@
     for k in range(1, groups):
         flags.append(lax.ppermute(flag, "groups", [(g, (g + k) % groups) for g in range(groups)]))
     odd = functools.reduce(jnp.maximum, flags)[0, 0]
-    nearest = call(
+    select = call(
         functools.partial(final_kernel, peers, cap),
         "final",
         shape((1, count), f32),
@@ -558,8 +558,8 @@
         VMEM,
         flops=0,
         nbytes=4 * count,
-    )(info, back).reshape(count)
-    return lax.cond(odd > 0, whole_exchange, lambda e, c: nearest, embeddings, cluster_ids)
+    )
+    return lax.cond(odd > 0, whole_exchange, lambda e, c: select(info, back).reshape(count), embeddings, cluster_ids)
 
 
 def solution(mesh):

time: 97.5 us -> 97.5 us (level)
  no operation moved by 1% of the time
where the time goes in v7:
time: 97.5 us; the launch traced here: 97.2 us
  starting transfers between devices  41.8 us (43%)
  waiting for transfers between devices  37.3 us (38%)
  Pallas kernels  16.1 us (17%)
  local copies, waits for them, and re-layouts  1.11 us (1%)
    ppermute x2, waiting for transfers between devices, local(): lax.ppermute(rows, 'dp', pairs)  30.7 us
    ppermute x2, starting transfers between devices, local(): lax.ppermute(rows, 'dp', pairs)  17.1 us
    ppermute x1, starting transfers between devices, local(): even2 = lax.ppermute(even2, 'dp', even_pairs)  6.45 us
    pallas_call x1, Pallas kernels, local(): call(functools.partial(pack_kernel, peers, cap, block), 'pack', [shape((8...  5.88 us
    ppermute x1, starting transfers between devices, local(): ends = lax.ppermute(ends, 'dp', ends_pairs)  4.85 us
    all_to_all x1, starting transfers between devices, local(): back = lax.all_to_all(best, 'dp', split_axis=0, concat_axis=0, tiled=True)  3.51 us
    ppermute x1, starting transfers between devices, local(): even1 = lax.ppermute(even, 'dp', even_pairs)  3.08 us
    pallas_call x1, Pallas kernels, local(): call(functools.partial(far_best_kernel, peers, block, edges), 'far_best',...  2.4 us
  transfers between devices with their start and end apart: 14, of which 6 were waited for; matrix products, arithmetic and copies ran while one was open for 1% of the time, Pallas kernels for 7%

profile of v7, /device:TPU:0, one launch (start us, length us, event | category | flops | bytes accessed | tf_op | source)
XLA Modules:
  0.0 97.2 jit_solution(7584670875547832927)
XLA Ops:
  0.0 5.9 %pack.1 = (s32[8,1024]{1,0:T(8,128)S(1)}, bf16[112,1024]{1,0:T(8,128)(2,1)S(1)}, bf16[112,1024]{1,0:T(8,128)(2,1)S(1)}, bf16[384,1024]{1,0:T(8,128)(2,1)S(1)}, b...) custom-call(s32[1]{0:T(128)} %bitcast.8.me_ref, s32[1,1024]{1,0:T(1,128)} %bitcast.47, ...), custom_call_target="tpu_custom_call" | custom-call | flops 2415919104 | bytes 8388608 | tf_op jit(solution)/shard_map/pack/pallas_call | solution.py:427
  5.9 3.1 %collective-permute-start.3 = (bf16[384,1024]{1,0:T(8,128)(2,1)S(1)}, bf16[384,1024]{1,0:T(8,128)(2,1)S(1)}, u32[]{:S(2)}, u32[]{:S(2)}) collective-permute-start(bf16[384,1024]{1,0:T(8,128)(2,1)S(1)} %get-tuple-element.96.even), channel_id=1, source_target_pairs={{0,4},{2,6},{4,0},{6,2},{8,12},{10,14},{12,8},{14,10},{1,5},{3,7},... | collective-permute-start | bytes 2359304 | tf_op jit(solution)/shard_map/ppermute | solution.py:445
  9.0 1.5 %collective-permute-start.2 = (bf16[336,1024]{1,0:T(8,128)(2,1)S(1)}, bf16[336,1024]{1,0:T(8,128)(2,1)S(1)}, u32[]{:S(2)}, u32[]{:S(2)}) collective-permute-start(bf16[336,1024]{1,0:T(8,128)(2,1)S(1)} %get-tuple-element.95), channel_id=1, source_target_pairs={{0,2},{2,0},{4,6},{6,4},{8,10},{10,8},{12,14},{14,12},{1,3},{3,1},... | collective-permute-start | bytes 2064392 | tf_op jit(solution)/shard_map/ppermute | solution.py:446
  10.5 2.6 %collective-permute-start.4 = (bf16[112,1024]{1,0:T(8,128)(2,1)S(1)}, bf16[112,1024]{1,0:T(8,128)(2,1)S(1)}, u32[]{:S(2)}, u32[]{:S(2)}) collective-permute-start(bf16[112,1024]{1,0:T(8,128)(2,1)S(1)} %get-tuple-element.97), channel_id=1, source_target_pairs={{0,8},{2,10},{4,12},{6,14},{8,0},{10,2},{12,4},{14,6},{1,9},{3,11}... | collective-permute-start | bytes 688136 | tf_op jit(solution)/shard_map/ppermute | solution.py:447
  13.1 0.7 collective-permute-start.5
  13.8 16.9 %collective-permute-done.4.rest_0_ = bf16[112,1024]{1,0:T(8,128)(2,1)S(1)} collective-permute-done((bf16[112,1024]{1,0:T(8,128)(2,1)S(1)}, bf16[112,1024]{1,0:T(8,128)(2,1)S(1)}, u32[]{:S(2)}, u32[]{:S(2)}) %collective-permute-start.4) | collective-permute-done | bytes 229408 | tf_op jit(solution)/shard_map/ppermute | solution.py:447
  30.7 0.7 collective-permute-done.3.lead_even.even
  31.4 0.3 relay.1
  31.7 1.8 %collective-permute-start.7 = (bf16[656,1024]{1,0:T(8,128)(2,1)S(1)}, bf16[656,1024]{1,0:T(8,128)(2,1)S(1)}, u32[]{:S(2)}, u32[]{:S(2)}) collective-permute-start(bf16[656,1024]{1,0:T(8,128)(2,1)S(1)} %get-tuple-element.103.asked), channel_id=1, source_target_pairs={{0,2},{2,0},{4,6},{6,4},{8,10},{10,8},{12,14},{14,12},{1,3},{3,1},... | collective-permute-start | bytes 4030472 | tf_op jit(solution)/shard_map/ppermute | solution.py:464
  33.4 0.7 collective-permute-start.6
  34.2 0.1 pass_on.1
  34.2 6.5 %collective-permute-start.9 = (bf16[384,1024]{1,0:T(8,128)(2,1)S(1)}, bf16[384,1024]{1,0:T(8,128)(2,1)S(1)}, u32[]{:S(2)}, u32[]{:S(2)}) collective-permute-start(bf16[384,1024]{1,0:T(8,128)(2,1)S(1)} %pass_on.1), channel_id=1, source_target_pairs={{0,4},{2,6},{4,0},{6,2},{8,12},{10,14},{12,8},{14,10},{1,5},{3,7},... | collective-permute-start | bytes 2359304 | tf_op jit(solution)/shard_map/ppermute | solution.py:474
  40.7 4.8 %collective-permute-start.10 = (bf16[224,1024]{1,0:T(8,128)(2,1)S(1)}, bf16[224,1024]{1,0:T(8,128)(2,1)S(1)}, u32[]{:S(2)}, u32[]{:S(2)}) collective-permute-start(bf16[224,1024]{1,0:T(8,128)(2,1)S(1)} %get-tuple-element.106), channel_id=1, source_target_pairs={{0,12},{2,14},{12,0},{14,2},{1,13},{3,15},{13,1},{15,3},{16,28},{1... | collective-permute-start | bytes 1376264 | tf_op jit(solution)/shard_map/ppermute | solution.py:475
  45.5 14.5 %collective-permute-start.11 = (bf16[112,1024]{1,0:T(8,128)(2,1)S(1)}, bf16[112,1024]{1,0:T(8,128)(2,1)S(1)}, u32[]{:S(2)}, u32[]{:S(2)}) collective-permute-start(bf16[112,1024]{1,0:T(8,128)(2,1)S(1)} %get-tuple-element.107), channel_id=1, source_target_pairs={{0,8},{2,10},{4,12},{6,14},{8,0},{10,2},{12,4},{14,6},{1,9},{3,11}... | collective-permute-start | bytes 688136 | tf_op jit(solution)/shard_map/ppermute | solution.py:476
  60.1 2.4 %collective-permute-done.7.asked_y = bf16[656,1024]{1,0:T(8,128)(2,1)S(1)} collective-permute-done((bf16[656,1024]{1,0:T(8,128)(2,1)S(1)}, bf16[656,1024]{1,0:T(8,128)(2,1)S(1)}, u32[]{:S(2)}, u32[]{:S(2)}) %collective-permute-start.7) | collective-permute-done | bytes 1343520 | tf_op jit(solution)/shard_map/ppermute | solution.py:464
  62.4 1.4 %lead_early.1.early = f32[8,256]{1,0:T(8,128)S(1)} custom-call(bf16[656,1024]{1,0:T(8,128)(2,1)S(1)} %get-tuple-element.103.asked, bf16[656,1024]{1,0:T(8,128)(2,1)S(1)} %collective-permute-done.7.asked_y, bf16[544,1024]{1,0:T(8,128)(2,1)S(1)} %get-tuple-element.109.cols, bf16[544,1024]{1,0:T(8,128)(2,1)S(1)} %collective-permute-done.8.cols_other), custom_call_target="tpu_custom_call" | custom-call | flops 1610612736 | bytes 3670016 | tf_op jit(solution)/shard_map/lead_early/pallas_call | solution.py:478
  63.8 13.8 %collective-permute-done.11.rest_1_ = bf16[112,1024]{1,0:T(8,128)(2,1)S(1)} collective-permute-done((bf16[112,1024]{1,0:T(8,128)(2,1)S(1)}, bf16[112,1024]{1,0:T(8,128)(2,1)S(1)}, u32[]{:S(2)}, u32[]{:S(2)}) %collective-permute-start.11) | collective-permute-done | bytes 229408 | tf_op jit(solution)/shard_map/ppermute | solution.py:476
  77.6 0.3 collect.1
  77.9 0.1 collective-permute-start.13
  78.0 0.5 collective-permute-start.12
  78.5 2.1 %own_best.1.top = f32[8,896]{1,0:T(8,128)S(1)} custom-call(bf16[896,1024]{1,0:T(8,128)(2,1)S(1)} %get-tuple-element.117.own), custom_call_target="tpu_custom_call" | custom-call | flops 1644167168 | bytes 1835008 | tf_op jit(solution)/shard_map/own_best/pallas_call | solution.py:521
  80.6 1.1 %lead_best.1.lead_top = f32[8,256]{1,0:T(8,128)S(1)} custom-call(f32[8,256]{1,0:T(8,128)S(1)} %lead_early.1.early, bf16[656,1024]{1,0:T(8,128)(2,1)S(1)} %get-tuple-element.103.asked, bf16[656,1024]{1,0:T(8,128)(2,1)S(1)} %collective-permute-done.7.asked_y, bf16[768,1024]{1,0:T(8,128)(2,1)S(1)} %get-tuple-element.119.first), custom_call_target="tpu_custom_call" | custom-call | flops 2684354560 | bytes 5242880 | tf_op jit(solution)/shard_map/lead_best/pallas_call | solution.py:512
  81.8 1.7 %first_best.1 = (f32[8,896]{1,0:T(8,128)S(1)}, f32[8,256]{1,0:T(8,128)S(1)}) custom-call(bf16[896,1024]{1,0:T(8,128)(2,1)S(1)} %get-tuple-element.117.own, bf16[768,1024]{1,0:T(8,128)(2,1)S(1)} %collective-permute-done.13.first, f32[8,896]{1,0:T(8,128)S(1)} %own_best.1.top, bf16[656,1024]{1,0:T(8,128)(2,1)S(1)} %get-tuple-element.103.asked, ...), custom_call_target="tpu_custom_call" | custom-call | flops 1350565888 | bytes 3670016 | tf_op jit(solution)/shard_map/first_best/pallas_call | solution.py:530
  83.5 2.4 %far_best.1 = (f32[8,1,384]{2,1,0:T(1,128)}, f32[8,128]{1,0:T(8,128)S(1)}) custom-call(s32[1]{0:T(128)} %bitcast.8.me_ref, bf16[896,1024]{1,0:T(8,128)(2,1)S(1)} %get-tuple-element.117.own, bf16[672,1024]{1,0:T(8,128)(2,1)S(1)} %collective-permute-done.12.second, f32[8,896]{1,0:T(8,128)S(1)} %get-tuple-element.121.top, f32[8,256]{1,0:T(8,128)S(1)} %get-tuple-element.122.lead_top), custom_call_target="tpu_custom_call" | custom-call | flops 1644167168 | bytes 3670016 | tf_op jit(solution)/shard_map/far_best/pallas_call | solution.py:539
  85.9 3.5 %all-to-all-start.3 = ((f32[8,1,384]{2,1,0:T(1,128)}), f32[8,1,384]{2,1,0:T(1,128)S(1)}, u32[]{:S(2)}, u32[]{:S(2)}) async-start(f32[8,1,384]{2,1,0:T(1,128)} %get-tuple-element.125), calls=%async_computation.3 | async-start | bytes 24576 | tf_op jit(solution)/shard_map/all_to_all | solution.py:548
  89.4 1.6 %collective-permute-start.14 = (f32[8,128]{1,0:T(8,128)S(1)}, f32[8,128]{1,0:T(8,128)S(1)}, u32[]{:S(2)}, u32[]{:S(2)}) collective-permute-start(f32[8,128]{1,0:T(8,128)S(1)} %get-tuple-element.123), channel_id=1, source_target_pairs={{0,16},{16,0},{1,17},{17,1},{2,18},{18,2},{3,19},{19,3},{4,20},{20... | collective-permute-start | bytes 12296 | tf_op jit(solution)/shard_map/ppermute | solution.py:551
  91.0 2.1 %collective-permute-done.14 = f32[8,128]{1,0:T(8,128)S(1)} collective-permute-done((f32[8,128]{1,0:T(8,128)S(1)}, f32[8,128]{1,0:T(8,128)S(1)}, u32[]{:S(2)}, u32[]{:S(2)}) %collective-permute-start.14) | collective-permute-done | bytes 4128 | tf_op jit(solution)/shard_map/ppermute | solution.py:551
  93.1 0.5 slice.9
  94.3 1.5 %all-to-all-done.3 = f32[8,1,384]{2,1,0:T(1,128)S(1)} async-done(((f32[8,1,384]{2,1,0:T(1,128)}), f32[8,1,384]{2,1,0:T(1,128)S(1)}, u32[]{:S(2)}, u32[]{:S(2)}) %all-to-all-start.3) | async-done | bytes 12320 | tf_op jit(solution)/shard_map/all_to_all | solution.py:548
  95.7 0.9 conditional.1
  95.7 0.9 final.1
  96.6 0.6 copy-done.1
  (13 shorter events, 0.0 us)
Async XLA Ops:
  5.9 25.5 %collective-permute-start.3 = (bf16[384,1024]{1,0:T(8,128)(2,1)S(1)}, bf16[384,1024]{1,0:T(8,128)(2,1)S(1)}, u32[]{:S(2)}, u32[]{:S(2)}) collective-permute-start(bf16[384,1024]{1,0:T(8,128)(2,1)S(1)} %get-tuple-element.96.even), channel_id=1, source_target_pairs={{0,4},{2,6},{4,0},{6,2},{8,12},{10,14},{12,8},{14,10},{1,5},{3,7},... | collective-permute-start | bytes 2359304 | tf_op jit(solution)/shard_map/ppermute | solution.py:445
  9.0 21.8 %collective-permute-start.2 = (bf16[336,1024]{1,0:T(8,128)(2,1)S(1)}, bf16[336,1024]{1,0:T(8,128)(2,1)S(1)}, u32[]{:S(2)}, u32[]{:S(2)}) collective-permute-start(bf16[336,1024]{1,0:T(8,128)(2,1)S(1)} %get-tuple-element.95), channel_id=1, source_target_pairs={{0,2},{2,0},{4,6},{6,4},{8,10},{10,8},{12,14},{14,12},{1,3},{3,1},... | collective-permute-start | bytes 2064392 | tf_op jit(solution)/shard_map/ppermute | solution.py:446
  10.5 20.2 %collective-permute-start.4 = (bf16[112,1024]{1,0:T(8,128)(2,1)S(1)}, bf16[112,1024]{1,0:T(8,128)(2,1)S(1)}, u32[]{:S(2)}, u32[]{:S(2)}) collective-permute-start(bf16[112,1024]{1,0:T(8,128)(2,1)S(1)} %get-tuple-element.97), channel_id=1, source_target_pairs={{0,8},{2,10},{4,12},{6,14},{8,0},{10,2},{12,4},{14,6},{1,9},{3,11}... | collective-permute-start | bytes 688136 | tf_op jit(solution)/shard_map/ppermute | solution.py:447
  13.1 21.1 %collective-permute-start.5 = (bf16[384,1024]{1,0:T(8,128)(2,1)S(1)}, bf16[384,1024]{1,0:T(8,128)(2,1)S(1)}, u32[]{:S(2)}, u32[]{:S(2)}) collective-permute-start(bf16[384,1024]{1,0:T(8,128)(2,1)S(1)} %get-tuple-element.99.odd), channel_id=1, source_target_pairs={{4,8},{6,10},{8,4},{10,6},{5,9},{7,11},{9,5},{11,7},{20,24},{22,26... | collective-permute-start | bytes 2359304 | tf_op jit(solution)/shard_map/ppermute | solution.py:444
  31.7 30.7 %collective-permute-start.7 = (bf16[656,1024]{1,0:T(8,128)(2,1)S(1)}, bf16[656,1024]{1,0:T(8,128)(2,1)S(1)}, u32[]{:S(2)}, u32[]{:S(2)}) collective-permute-start(bf16[656,1024]{1,0:T(8,128)(2,1)S(1)} %get-tuple-element.103.asked), channel_id=1, source_target_pairs={{0,2},{2,0},{4,6},{6,4},{8,10},{10,8},{12,14},{14,12},{1,3},{3,1},... | collective-permute-start | bytes 4030472 | tf_op jit(solution)/shard_map/ppermute | solution.py:464
  33.4 26.6 %collective-permute-start.8 = (bf16[544,1024]{1,0:T(8,128)(2,1)S(1)}, bf16[544,1024]{1,0:T(8,128)(2,1)S(1)}, u32[]{:S(2)}, u32[]{:S(2)}) collective-permute-start(bf16[544,1024]{1,0:T(8,128)(2,1)S(1)} %get-tuple-element.109.cols), channel_id=1, source_target_pairs={{0,1},{1,0},{2,3},{3,2},{4,5},{5,4},{6,7},{7,6},{8,9},{9,8},{10,11... | collective-permute-start | bytes 3342344 | tf_op jit(solution)/shard_map/ppermute | solution.py:465
  33.4 12.1 %collective-permute-start.6 = (bf16[384,1024]{1,0:T(8,128)(2,1)S(1)}, bf16[384,1024]{1,0:T(8,128)(2,1)S(1)}, u32[]{:S(2)}, u32[]{:S(2)}) collective-permute-start(bf16[384,1024]{1,0:T(8,128)(2,1)S(1)} %get-tuple-element.102), channel_id=1, source_target_pairs={{4,8},{6,10},{8,4},{10,6},{5,9},{7,11},{9,5},{11,7},{20,24},{22,26... | collective-permute-start | bytes 2359304 | tf_op jit(solution)/shard_map/ppermute | solution.py:463
  34.2 43.4 %collective-permute-start.9 = (bf16[384,1024]{1,0:T(8,128)(2,1)S(1)}, bf16[384,1024]{1,0:T(8,128)(2,1)S(1)}, u32[]{:S(2)}, u32[]{:S(2)}) collective-permute-start(bf16[384,1024]{1,0:T(8,128)(2,1)S(1)} %pass_on.1), channel_id=1, source_target_pairs={{0,4},{2,6},{4,0},{6,2},{8,12},{10,14},{12,8},{14,10},{1,5},{3,7},... | collective-permute-start | bytes 2359304 | tf_op jit(solution)/shard_map/ppermute | solution.py:474
  40.7 36.9 %collective-permute-start.10 = (bf16[224,1024]{1,0:T(8,128)(2,1)S(1)}, bf16[224,1024]{1,0:T(8,128)(2,1)S(1)}, u32[]{:S(2)}, u32[]{:S(2)}) collective-permute-start(bf16[224,1024]{1,0:T(8,128)(2,1)S(1)} %get-tuple-element.106), channel_id=1, source_target_pairs={{0,12},{2,14},{12,0},{14,2},{1,13},{3,15},{13,1},{15,3},{16,28},{1... | collective-permute-start | bytes 1376264 | tf_op jit(solution)/shard_map/ppermute | solution.py:475
  45.5 32.1 %collective-permute-start.11 = (bf16[112,1024]{1,0:T(8,128)(2,1)S(1)}, bf16[112,1024]{1,0:T(8,128)(2,1)S(1)}, u32[]{:S(2)}, u32[]{:S(2)}) collective-permute-start(bf16[112,1024]{1,0:T(8,128)(2,1)S(1)} %get-tuple-element.107), channel_id=1, source_target_pairs={{0,8},{2,10},{4,12},{6,14},{8,0},{10,2},{12,4},{14,6},{1,9},{3,11}... | collective-permute-start | bytes 688136 | tf_op jit(solution)/shard_map/ppermute | solution.py:476
  77.9 3.9 %collective-permute-start.13 = (bf16[768,1024]{1,0:T(8,128)(2,1)S(1)}, bf16[768,1024]{1,0:T(8,128)(2,1)S(1)}, u32[]{:S(2)}, u32[]{:S(2)}) collective-permute-start(bf16[768,1024]{1,0:T(8,128)(2,1)S(1)} %get-tuple-element.119.first), channel_id=1, source_target_pairs={{0,1},{1,0},{2,3},{3,2},{4,5},{5,4},{6,7},{7,6},{8,9},{9,8},{10,11... | collective-permute-start | bytes 4718600 | tf_op jit(solution)/shard_map/ppermute | solution.py:510
  78.0 5.5 %collective-permute-start.12 = (bf16[672,1024]{1,0:T(8,128)(2,1)S(1)}, bf16[672,1024]{1,0:T(8,128)(2,1)S(1)}, u32[]{:S(2)}, u32[]{:S(2)}) collective-permute-start(bf16[672,1024]{1,0:T(8,128)(2,1)S(1)} %get-tuple-element.118), channel_id=1, source_target_pairs={{0,1},{1,0},{2,3},{3,2},{4,5},{5,4},{6,7},{7,6},{8,9},{9,8},{10,11... | collective-permute-start | bytes 4128776 | tf_op jit(solution)/shard_map/ppermute | solution.py:511
  83.5 12.3 %copy-start = (s32[1024]{0:T(1024)S(1)}, s32[1024]{0:T(1024)}, u32[]{:S(2)}) copy-start(s32[1024]{0:T(1024)} %param.7) | copy-start | bytes 12292
  85.9 9.8 %all-to-all-start.3 = ((f32[8,1,384]{2,1,0:T(1,128)}), f32[8,1,384]{2,1,0:T(1,128)S(1)}, u32[]{:S(2)}, u32[]{:S(2)}) async-start(f32[8,1,384]{2,1,0:T(1,128)} %get-tuple-element.125), calls=%async_computation.3 | async-start | bytes 24576 | tf_op jit(solution)/shard_map/all_to_all | solution.py:548
  89.4 3.7 %collective-permute-start.14 = (f32[8,128]{1,0:T(8,128)S(1)}, f32[8,128]{1,0:T(8,128)S(1)}, u32[]{:S(2)}, u32[]{:S(2)}) collective-permute-start(f32[8,128]{1,0:T(8,128)S(1)} %get-tuple-element.123), channel_id=1, source_target_pairs={{0,16},{16,0},{1,17},{17,1},{2,18},{18,2},{3,19},{19,3},{4,20},{20... | collective-permute-start | bytes 12296 | tf_op jit(solution)/shard_map/ppermute | solution.py:551
  96.6 0.6 copy-start.1
